TPU v7x, 128 devices: a whole 4x4x4 slice. The times are simulated.
128 devices in a mesh: blk: 8 (over z, y_hi), dp: 16 (over x, y_lo, core).
Axes of the slice: x: 4, y: 4 (y_hi: 2, y_lo: 2; y = y_hi * 2 + y_lo), z: 4, core: 2. Of those that a mesh axis runs over, the one named last changes fastest.
Arguments:
- query_states: bfloat16 [16, 1024, 2560], P('dp', 'blk'), may hold values from -6 to 6
- key_states: bfloat16 [16, 1024, 2560], P('dp', 'blk'), may hold values from -6 to 6
- value_states: bfloat16 [16, 1024, 2560], P('dp', 'blk'), may hold values from -6 to 6
- mask_index: int32 [16, 512], P('dp', 'blk'), may hold values from 0 to 1023, as said below
- cotangent: bfloat16 [16, 512, 4096], P('dp', 'blk'), may hold values from -6 to 6
- out_weight: bfloat16 [2560, 4096], replicated, may hold values from -0.125 to 0.125
Outputs:
- query_grad: bfloat16 [16, 1024, 2560], P('dp', 'blk')
- key_grad: bfloat16 [16, 1024, 2560], P('dp', 'blk')
- value_grad: bfloat16 [16, 1024, 2560], P('dp', 'blk')
- weight_grad: float32 [2560, 4096], P(('blk', 'dp'))
Inputs may be any that keep to these rules, and one draw needn't show every extreme that they name: Within each record, entries b * 64 to (b + 1) * 64 - 1 are 64 distinct time steps of the aligned block b * 128 to (b + 1) * 128 - 1, in increasing order; cotangent row i belongs to time step mask_index[r, i].
All inputs are finite; a program needn't handle non-finite values.
Results may differ from a plain program's by a relative error of at most 0.035.
Values may be sent and summed in bfloat16 or wider, within the bound.
No kernel may reach another device: no remote copies, remote signals or barrier semaphores. Data moves between devices by JAX's collectives and lax.ppermute only.
A program may use at most 192 MiB of HBM per device.

v0:
```python
import math

import jax
import jax.numpy as jnp
from jax import lax
from jax.sharding import PartitionSpec as P

HEADS = 20
HEAD_DIM = 128


def split_heads(states, head_count):
    return states.reshape(states.shape[0], head_count, states.shape[1] // head_count)


def shards(query_states, key_states, value_states, mask_index, cotangent, out_weight):
    head_count = HEADS
    score_scale = 1.0 / math.sqrt(HEAD_DIM)
    query_local = query_states[0]
    key_local = key_states[0]
    value_local = value_states[0]
    row_count = query_local.shape[0]
    width = query_local.shape[1]
    row_start = lax.axis_index("blk") * row_count
    key_all, value_all = (
        lax.all_gather(key_local, "blk", axis=0, tiled=True),
        lax.all_gather(value_local, "blk", axis=0, tiled=True),
    )
    query_heads = split_heads(query_local, head_count)
    key_heads = split_heads(key_all, head_count)
    value_heads = split_heads(value_all, head_count)
    scores = (
        jnp.einsum("qhd,khd->hqk", query_heads, key_heads, preferred_element_type=jnp.float32)
        * score_scale
    )
    row_max = jnp.max(scores, axis=-1, keepdims=True)
    log_total = row_max + jnp.log(jnp.sum(jnp.exp(scores - row_max), axis=-1, keepdims=True))
    attn_probs = jnp.exp(scores - log_total).astype(jnp.bfloat16)
    attended = jnp.einsum(
        "hqk,khd->qhd", attn_probs, value_heads, preferred_element_type=jnp.float32
    )
    attended = attended.astype(jnp.bfloat16).reshape(row_count, width)
    local_steps = mask_index[0] - row_start
    selector = (local_steps[:, None] == jnp.arange(row_count, dtype=jnp.int32)[None, :]).astype(
        jnp.bfloat16
    )
    cot_rows = cotangent[0]
    masked_grad = lax.dot_general(
        cot_rows, out_weight, (((1,), (1,)), ((), ())), preferred_element_type=jnp.float32
    )
    masked_grad = masked_grad.astype(jnp.bfloat16)
    attended_grad = jnp.dot(selector.T, masked_grad, preferred_element_type=jnp.float32).astype(
        jnp.bfloat16
    )
    attended_masked = jnp.dot(selector, attended, preferred_element_type=jnp.float32).astype(
        jnp.bfloat16
    )
    grad_heads = split_heads(attended_grad, head_count)
    row_delta = jnp.sum(
        grad_heads.astype(jnp.float32) * split_heads(attended, head_count).astype(jnp.float32),
        axis=-1,
    )
    prob_grad = jnp.einsum(
        "qhd,khd->hqk", grad_heads, value_heads, preferred_element_type=jnp.float32
    )
    score_grad = (attn_probs.astype(jnp.float32) * (prob_grad - row_delta.T[:, :, None])).astype(
        jnp.bfloat16
    )
    query_grad = (
        jnp.einsum("hqk,khd->qhd", score_grad, key_heads, preferred_element_type=jnp.float32)
        * score_scale
    )
    query_grad = query_grad.astype(jnp.bfloat16).reshape(row_count, width)
    key_term = (
        jnp.einsum("hqk,qhd->khd", score_grad, query_heads, preferred_element_type=jnp.float32)
        * score_scale
    )
    value_term = jnp.einsum(
        "hqk,qhd->khd", attn_probs, grad_heads, preferred_element_type=jnp.float32
    )
    all_rows = key_term.shape[0]
    key_grad, value_grad = (
        lax.psum_scatter(key_term.reshape(all_rows, width), "blk", scatter_dimension=0, tiled=True),
        lax.psum_scatter(
            value_term.reshape(all_rows, width), "blk", scatter_dimension=0, tiled=True
        ),
    )
    slab_width = width // lax.axis_size("blk")
    slab_start = lax.axis_index("blk") * slab_width
    attended_piece = lax.all_gather(attended_masked, "blk", axis=0, tiled=True)
    cot_piece = lax.all_gather(cot_rows, "blk", axis=0, tiled=True)
    columns = lax.dynamic_slice_in_dim(attended_piece, slab_start, slab_width, 1)
    slab_total = lax.dot_general(
        columns, cot_piece, (((0,), (0,)), ((), ())), preferred_element_type=jnp.float32
    )
    weight_grad = lax.psum_scatter(slab_total, "dp", scatter_dimension=0, tiled=True)
    return (
        query_grad[None],
        key_grad.astype(jnp.bfloat16)[None],
        value_grad.astype(jnp.bfloat16)[None],
        weight_grad,
    )


def solution(mesh):
    return jax.shard_map(
        shards,
        mesh=mesh,
        in_specs=(
            P("dp", "blk", None),
            P("dp", "blk", None),
            P("dp", "blk", None),
            P("dp", "blk"),
            P("dp", "blk", None),
            P(),
        ),
        out_specs=(
            P("dp", "blk", None),
            P("dp", "blk", None),
            P("dp", "blk", None),
            P(("blk", "dp"), None),
        ),
        check_vma=False,
    )
```

profile of v0, /device:TPU:6, one launch (start us, length us, event | category | flops | bytes accessed | tf_op | source)
XLA Modules:
  0.0 651.3 jit_solution(4396760876739690917)
XLA Ops:
  7.2 2.2 copy.32
  9.5 2.2 copy.36
  12.5 1.4 copy.31
  13.9 11.0 %convolution_convert_fusion = bf16[128,2560]{1,0:T(8,128)(2,1)S(1)} fusion(bf16[2560,4096]{1,0:T(8,128)(2,1)} %param.11, bf16[1,64,4096]{2,1,0:T(8,128)(2,1)S(1)} %copy-done.1, s32[64]{0:T(128)S(1)} %subtract_bitcast_fusion), kind=kOutput, calls=%fused_computation.7 | convolution fusion | flops 1384620032 | bytes 22151424 | tf_op jit(solution)/shard_map/dot_general | solution.py:52
  25.3 71.6 %all-gather.10.cloned.1.call-done = bf16[1,1024,2560]{1,2,0:T(8,128)(2,1)} async-done(((bf16[1,128,2560]{1,2,0:T(8,128)(2,1)}), bf16[1,1024,2560]{1,2,0:T(8,128)(2,1)}) %all-gather.10.cloned.1.call-update) | async-done | bytes 5242896 | tf_op jit(solution)/shard_map/all_gather | solution.py:26
  96.9 4.2 multiply_reduce_fusion
  101.0 2.0 exponential_reduce_fusion
  103.1 3.9 exponential_convert_fusion
  107.0 74.2 %all-gather.12.cloned.1.call-done = bf16[1,1024,2560]{1,2,0:T(8,128)(2,1)} async-done(((bf16[1,128,2560]{1,2,0:T(8,128)(2,1)}), bf16[1,1024,2560]{1,2,0:T(8,128)(2,1)}) %all-gather.12.cloned.1.call-update) | async-done | bytes 5242896 | tf_op jit(solution)/shard_map/all_gather | solution.py:27
  181.1 5.6 multiply_reduce_fusion.1
  186.7 1.1 convolution_convert_fusion.2
  188.1 6.3 multiply_convert_fusion
  194.4 5.5 broadcast_multiply_fusion
  200.0 11.5 %copy.39 = f32[1024,2560]{1,0:T(8,128)} copy(f32[1024,2560]{0,1:T(8,128)} %bitcast.49) | data formatting | bytes 20971520 | tf_op jit(solution)/shard_map/reshape | solution.py:83
  211.5 8.0 %fusion.10 = f32[20,128,1024]{2,1,0:T(8,128)} fusion(bf16[128,20,128]{0,2,1:T(8,128)(2,1)S(1)} %bitcast.54, bf16[20,128,1024]{2,1,0:T(8,128)(2,1)} %exponential_convert_fusion), kind=kOutput, calls=%fused_computation.25 | convolution fusion | flops 671088640 | bytes 16384000 | tf_op jit(solution)/shard_map/hqk,qhd->khd/dot_general | solution.py:78
  219.5 11.5 %copy.40 = f32[1024,2560]{1,0:T(8,128)} copy(f32[1024,2560]{0,1:T(8,128)} %bitcast.48) | data formatting | bytes 20971520 | tf_op jit(solution)/shard_map/reshape | solution.py:85
  232.9 20.0 %all-gather.14.cloned.1.call-done = bf16[1,512,4096]{2,1,0:T(8,128)(2,1)} async-done(((bf16[1,64,4096]{2,1,0:T(8,128)(2,1)}), bf16[1,512,4096]{2,1,0:T(8,128)(2,1)}) %all-gather.14.cloned.1.call-update) | async-done | bytes 4194320 | tf_op jit(solution)/shard_map/all_gather | solution.py:91
  252.9 59.1 %all-gather.8.cloned.1.call-done = bf16[512,2560]{1,0:T(8,128)(2,1)} async-done(((bf16[64,2560]{1,0:T(8,128)(2,1)}), bf16[512,2560]{1,0:T(8,128)(2,1)}) %all-gather.8.cloned.1.call-update) | async-done | bytes 2621456 | tf_op jit(solution)/shard_map/all_gather | solution.py:90
  312.0 6.3 fusion.1
  318.2 96.1 %fusion = f32[24,4096]{1,0:T(8,128)S(1)} fusion(f32[320,4096]{1,0:T(8,128)} %fusion.1), kind=kCustom, calls=%all-reduce-scatter | all-reduce-scatter fusion | flops 1572865 | bytes 5636608
  414.4 17.7 %collective-permute-start.1 = (f32[24,4096]{1,0:T(8,128)S(1)}, f32[24,4096]{1,0:T(8,128)S(1)}, u32[]{:S(2)}, u32[]{:S(2)}) collective-permute-start(f32[24,4096]{1,0:T(8,128)S(1)} %fusion), channel_id=1, source_target_pairs={{0,2},{1,3},{2,4},{3,5},{4,6},{5,7},{6,8},{7,9},{8,10},{9,11},{10,... | collective-permute-start | bytes 1179656
  432.1 1.9 collective-permute-start
  434.0 1.9 collective-permute-start.2
  435.9 5.6 fusion.3
  441.5 1.1 copy.41
  442.6 15.4 %collective-permute-done.2 = f32[12,4096]{1,0:T(8,128)S(1)} collective-permute-done((f32[12,4096]{1,0:T(8,128)S(1)}, f32[12,4096]{1,0:T(8,128)S(1)}, u32[]{:S(2)}, u32[]{:S(2)}) %collective-permute-start.2) | collective-permute-done | bytes 196640
  458.0 1.1 concatenate
  459.1 0.8 constant_dynamic-slice_fusion
  459.9 48.0 %reduce-scatter.5.cloned.1.call-done = f32[128,2560]{1,0:T(8,128)} async-done(((f32[1024,2560]{1,0:T(8,128)}), f32[128,2560]{1,0:T(8,128)}) %reduce-scatter.5.cloned.1.call-update) | async-done | bytes 1310736 | tf_op jit(solution)/shard_map/reduce_scatter | solution.py:83
  507.8 2.2 convert_bitcast_fusion.1
  510.1 132.1 %reduce-scatter.7.cloned.1.call-done = f32[128,2560]{1,0:T(8,128)} async-done(((f32[1024,2560]{1,0:T(8,128)}), f32[128,2560]{1,0:T(8,128)}) %reduce-scatter.7.cloned.1.call-update) | async-done | bytes 1310736 | tf_op jit(solution)/shard_map/reduce_scatter | solution.py:84
  642.2 2.2 convert_bitcast_fusion
  (27 shorter events, 2.8 us)
Async XLA Ops:
  7.2 6.8 %copy-start.1 = (bf16[1,64,4096]{2,1,0:T(8,128)(2,1)S(1)}, bf16[1,64,4096]{2,1,0:T(8,128)(2,1)}, u32[]{:S(2)}) copy-start(bf16[1,64,4096]{2,1,0:T(8,128)(2,1)} %param.10) | copy-start | bytes 1572868
  7.2 6.7 %copy-start.3 = (s32[1,64]{1,0:T(1,128)S(1)}, s32[1,64]{1,0:T(1,128)}, u32[]{:S(2)}) copy-start(s32[1,64]{1,0:T(1,128)} %param.9) | copy-start | bytes 772
  7.2 89.7 %all-gather.10.cloned.1.call-start = ((), (), s32[]{:S(2)}) async-start(), calls=%async_computation.5 | async-start | bytes 5898240 | tf_op jit(solution)/shard_map/all_gather | solution.py:26
  9.5 171.7 %all-gather.12.cloned.1.call-start = ((), (), s32[]{:S(2)}) async-start(), calls=%async_computation.6 | async-start | bytes 5898240 | tf_op jit(solution)/shard_map/all_gather | solution.py:27
  11.7 241.2 %all-gather.14.cloned.1.call-start = ((), (), s32[]{:S(2)}) async-start(), calls=%async_computation.7 | async-start | bytes 4718592 | tf_op jit(solution)/shard_map/all_gather | solution.py:91
  12.4 299.5 %all-gather.8.cloned.1.call-start = ((), (), s32[]{:S(2)}) async-start(), calls=%async_computation.4 | async-start | bytes 2949120 | tf_op jit(solution)/shard_map/all_gather | solution.py:90
  187.9 320.0 %reduce-scatter.5.cloned.1.call-start = ((), (), s32[]{:S(2)}) async-start(), calls=%async_computation.2 | async-start | bytes 11796480 | tf_op jit(solution)/shard_map/reduce_scatter | solution.py:83
  194.4 5.6 copy-start
  211.5 430.7 %reduce-scatter.7.cloned.1.call-start = ((), (), s32[]{:S(2)}) async-start(), calls=%async_computation.3 | async-start | bytes 11796480 | tf_op jit(solution)/shard_map/reduce_scatter | solution.py:84
  231.0 0.7 copy-start.2
  414.4 43.6 %collective-permute-start.1 = (f32[24,4096]{1,0:T(8,128)S(1)}, f32[24,4096]{1,0:T(8,128)S(1)}, u32[]{:S(2)}, u32[]{:S(2)}) collective-permute-start(f32[24,4096]{1,0:T(8,128)S(1)} %fusion), channel_id=1, source_target_pairs={{0,2},{1,3},{2,4},{3,5},{4,6},{5,7},{6,8},{7,9},{8,10},{9,11},{10,... | collective-permute-start | bytes 1179656
  432.1 25.9 %collective-permute-start = (f32[24,4096]{1,0:T(8,128)S(1)}, f32[24,4096]{1,0:T(8,128)S(1)}, u32[]{:S(2)}, u32[]{:S(2)}) collective-permute-start(f32[24,4096]{1,0:T(8,128)S(1)} %fusion), channel_id=1, source_target_pairs={{0,1},{1,2},{2,3},{3,4},{4,5},{5,6},{6,7},{7,8},{8,9},{9,10},{10,1... | collective-permute-start | bytes 1179656
  434.0 24.0 %collective-permute-start.2 = (f32[12,4096]{1,0:T(8,128)S(1)}, f32[12,4096]{1,0:T(8,128)S(1)}, u32[]{:S(2)}, u32[]{:S(2)}) collective-permute-start(f32[12,4096]{1,0:T(8,128)S(1)} %slice), channel_id=1, source_target_pairs={{0,3},{1,4},{2,5},{3,6},{4,7},{5,8},{6,9},{7,10},{8,11},{9,12},{10... | collective-permute-start | bytes 589832
Sparse Core Ops, SparseCore 0:
  10.8 86.0 all-gather.9
  99.6 81.4 all-gather.11
  183.5 69.3 all-gather.13
  255.6 56.3 all-gather.7
  315.6 192.1 reduce-scatter.4
  511.5 130.6 reduce-scatter.6
where the time goes:
time: 652 us; the launch traced here: 651 us
  waiting for transfers between devices  421 us (65%)
  blocking collectives  96.1 us (15%)
  matrix products  53.6 us (8%)
  local copies, waits for them, and re-layouts  33.2 us (5%)
  starting transfers between devices  21.9 us (3%)
  between operations  14.9 us (2%)
  other arithmetic  10.4 us (2%)
    reduce_scatter x1, waiting for transfers between devices, shards(): lax.psum_scatter(value_term.reshape(all_rows, width), 'blk', scatter_dime...  132 us
    unnamed x1, blocking collectives  96.1 us
    all_gather x1, waiting for transfers between devices, shards(): lax.all_gather(value_local, 'blk', axis=0, tiled=True)  74.2 us
    all_gather x1, waiting for transfers between devices, shards(): lax.all_gather(key_local, 'blk', axis=0, tiled=True)  71.6 us
    all_gather x1, waiting for transfers between devices, shards(): attended_piece = lax.all_gather(attended_masked, 'blk', axis=0, tiled=True)  59.1 us
    reduce_scatter x1, waiting for transfers between devices, shards(): lax.psum_scatter(key_term.reshape(all_rows, width), 'blk', scatter_dimens...  48 us
    unnamed x3, starting transfers between devices  21.5 us
    all_gather x1, waiting for transfers between devices, shards(): cot_piece = lax.all_gather(cot_rows, 'blk', axis=0, tiled=True)  20 us
  transfers between devices with their start and end apart: 9, of which 7 were waited for; matrix products, arithmetic and copies ran while one was open for 29% of the time, Pallas kernels for 0%

commit v1 on v0

v1 whole, which is shorter than its diff:
```python
import functools
import math

import jax
import jax.numpy as jnp
from jax import lax
from jax.experimental import pallas as pl
from jax.experimental.pallas import tpu as pltpu
from jax.sharding import PartitionSpec as P

HEAD_DIM = 128
SCALE = 1.0 / math.sqrt(HEAD_DIM)
BF = jnp.bfloat16
F32 = jnp.float32
ORDER = [(dz, dy) for dz in range(4) for dy in range(2)]
TOK = 128
MSK = 64
HEADS_DEV = 3


def move_blk(a, dz, dy):
    pairs = [
        (z * 2 + y, ((z + dz) % 4) * 2 + (y + dy) % 2) for z in range(4) for y in range(2)
    ]
    return lax.ppermute(a, "blk", pairs)


def move_dp(a, dx, dl, dc):
    pairs = [
        (x * 4 + l * 2 + c, ((x + dx) % 4) * 4 + ((l + dl) % 2) * 2 + (c + dc) % 2)
        for x in range(4)
        for l in range(2)
        for c in range(2)
    ]
    return lax.ppermute(a, "dp", pairs)


def dot(a, b, ca, cb):
    return lax.dot_general(a, b, (((ca,), (cb,)), ((), ())), preferred_element_type=F32)


def gather_y_first(c):
    half = c.shape[0]
    pair = jnp.concatenate([c, move_blk(c, 0, 1)], axis=0)
    one = move_blk(pair, 1, 0)
    three = move_blk(pair, 3, 0)
    two_a = move_blk(one[:half], 1, 0)
    two_b = move_blk(three[half:], 3, 0)
    return jnp.concatenate([pair, one, two_a, two_b, three], axis=0)


def gather_z_first(c):
    rows = c.shape[0]
    one = move_blk(c, 1, 0)
    three = move_blk(c, 3, 0)
    two = jnp.concatenate(
        [move_blk(one[: rows // 2], 1, 0), move_blk(three[rows // 2 :], 3, 0)], axis=0
    )
    mine = [c, one, two, three]
    other = move_blk(jnp.concatenate(mine, axis=0), 0, 1)
    parts = []
    for dz in range(4):
        parts += [mine[dz], other[dz * rows : (dz + 1) * rows]]
    return jnp.concatenate(parts, axis=0)


def forward_kernel(*refs):
    blocks, (prob_ref, att_ref) = refs[:8], refs[8:]
    query = jnp.concatenate([b[0:MSK] for b in blocks], axis=0)
    key = jnp.concatenate([b[MSK : MSK + TOK] for b in blocks], axis=0)
    value = jnp.concatenate([b[MSK + TOK :] for b in blocks], axis=0)
    scores = dot(key, query, 1, 1) * SCALE
    top = jnp.max(scores, axis=0, keepdims=True)
    raised = jnp.exp(scores - top)
    total = jnp.sum(raised, axis=0, keepdims=True)
    probs = (raised * (1.0 / total)).astype(BF)
    prob_ref[0] = probs
    att_ref[...] = dot(value.T, probs, 1, 0).astype(BF)


def backward_kernel(*refs):
    blocks, (prob_ref, att_ref, grad_ref), outs = refs[:8], refs[8:11], refs[11:]
    query = jnp.concatenate([b[0:MSK] for b in blocks], axis=0)
    key = jnp.concatenate([b[MSK : MSK + TOK] for b in blocks], axis=0)
    value = jnp.concatenate([b[MSK + TOK :] for b in blocks], axis=0)
    grad = grad_ref[...]
    delta = jnp.sum(grad.T.astype(F32) * att_ref[...].astype(F32), axis=0, keepdims=True)
    probs = prob_ref[0]
    prob_grad = dot(value, grad, 1, 1)
    score_grad = (probs.astype(F32) * (prob_grad - delta)).astype(BF)
    query_grad = (dot(key.T, score_grad, 1, 0) * SCALE).T.astype(BF)
    key_grad = (dot(score_grad, query, 1, 0) * SCALE).astype(BF)
    value_grad = dot(probs, grad, 1, 0).astype(BF)
    head = pl.program_id(0)

    def store(refs_, ids):
        for i in ids:
            refs_[i][0:MSK] = query_grad[i * MSK : (i + 1) * MSK]
            refs_[i][MSK : MSK + TOK] = key_grad[i * TOK : (i + 1) * TOK]
            refs_[i][MSK + TOK :] = value_grad[i * TOK : (i + 1) * TOK]

    store(outs, [i for i, (_, dy) in enumerate(ORDER) if dy == 0])

    @pl.when(head < 2)
    def _():
        store(outs, [i for i, (_, dy) in enumerate(ORDER) if dy == 1])


ROWS = MSK + 2 * TOK
QUERIES = 8 * MSK
KEYS = 8 * TOK


def forward(blocks):
    return pl.pallas_call(
        forward_kernel,
        grid=(HEADS_DEV,),
        in_specs=[pl.BlockSpec((ROWS, HEAD_DIM), lambda h: (0, h))] * 8,
        out_specs=[
            pl.BlockSpec((1, KEYS, QUERIES), lambda h: (h, 0, 0)),
            pl.BlockSpec((HEAD_DIM, QUERIES), lambda h: (h, 0)),
        ],
        out_shape=[
            jax.ShapeDtypeStruct((HEADS_DEV, KEYS, QUERIES), BF),
            jax.ShapeDtypeStruct((HEADS_DEV * HEAD_DIM, QUERIES), BF),
        ],
        compiler_params=pltpu.CompilerParams(vmem_limit_bytes=40 * 2**20),
        cost_estimate=pl.CostEstimate(
            flops=int(1.2e9), bytes_accessed=int(6e6), transcendentals=int(1.6e6)
        ),
    )(*blocks)


def backward(blocks, probs, att, grad):
    wide = lambda h: (0, h)
    narrow = lambda h: (0, jnp.minimum(h, 1))
    return pl.pallas_call(
        backward_kernel,
        grid=(HEADS_DEV,),
        in_specs=[pl.BlockSpec((ROWS, HEAD_DIM), wide)] * 8
        + [
            pl.BlockSpec((1, KEYS, QUERIES), lambda h: (h, 0, 0)),
            pl.BlockSpec((HEAD_DIM, QUERIES), lambda h: (h, 0)),
            pl.BlockSpec((QUERIES, HEAD_DIM), wide),
        ],
        out_specs=[
            pl.BlockSpec((ROWS, HEAD_DIM), narrow if dy else wide) for _, dy in ORDER
        ],
        out_shape=[
            jax.ShapeDtypeStruct((ROWS, HEAD_DIM * (2 if dy else 3)), BF) for _, dy in ORDER
        ],
        compiler_params=pltpu.CompilerParams(vmem_limit_bytes=40 * 2**20),
        cost_estimate=pl.CostEstimate(
            flops=int(3e9), bytes_accessed=int(9e6), transcendentals=0
        ),
    )(*blocks, probs, att, grad)


def shards(query_states, key_states, value_states, mask_index, cotangent, out_weight):
    blk, dp = lax.axis_index("blk"), lax.axis_index("dp")
    z, y = blk // 2, blk % 2
    x, lo, core = dp // 4, (dp // 2) % 2, dp % 2
    steps = mask_index[0] - blk * TOK
    selector = (steps[:, None] == jnp.arange(TOK, dtype=jnp.int32)[None, :]).astype(BF)
    masked_query = dot(selector, query_states[0], 1, 0).astype(BF)
    local = jnp.concatenate([masked_query, key_states[0], value_states[0]], axis=0)

    def slab(a, axis, zz, yy):
        own = lax.dynamic_slice_in_dim(a, zz * 640 + yy * 384, 256, axis)
        shared = lax.dynamic_slice_in_dim(a, zz * 640 + 256, 128, axis)
        return jnp.concatenate([own, shared], axis=axis)

    blocks = []
    for dz, dy in ORDER:
        piece = slab(local, 1, (z + dz) % 4, (y + dy) % 2)
        blocks.append(piece if (dz, dy) == (0, 0) else move_blk(piece, dz, dy))

    cot = cotangent[0]
    half = cot.shape[1] // 2
    cots = [gather_y_first(cot[:, :half]), gather_z_first(cot[:, half:])]
    weight = slab(out_weight, 0, z, y)

    probs, att = forward(blocks)
    grad = sum(dot(c, w, 1, 1) for c, w in zip(cots, (weight[:, :half], weight[:, half:])))
    outs = backward(blocks, probs, att, grad.astype(BF))

    r = jnp.arange(320, dtype=jnp.int32)
    rc, rx, rl, rr = r // 160, (r // 40) % 4, (r // 20) % 2, r % 20
    place = ((x + rx) % 4) * 80 + ((lo + rl) % 2) * 40 + ((core + rc) % 2) * 20 + rr
    wanted = place + y * 320
    index = jnp.where(
        (wanted >= 256) & (wanted < 384), wanted, jnp.where(y == 0, wanted, wanted - 384)
    )
    pick = (index[:, None] == jnp.arange(384, dtype=jnp.int32)[None, :]).astype(BF)
    att_rows = dot(pick, att, 1, 0).astype(BF)
    finals = []
    for c in cots:
        sent = move_dp(dot(att_rows[160:], c, 1, 0).astype(BF), 0, 0, 1)
        total = (dot(att_rows[:160], c, 1, 0) + sent.astype(F32)).astype(BF)
        chunks = [total[i * 40 : (i + 1) * 40] for i in range(4)]
        acc = chunks[0].astype(F32)
        for dx in (1, 2, 3):
            acc = acc + move_dp(chunks[dx], dx, 0, 0).astype(F32)
        finals.append(acc[:20] + move_dp(acc[20:].astype(BF), 0, 1, 0).astype(F32))
    weight_grad = jnp.concatenate(finals, axis=1)

    back = {}
    for (dz, dy), o in zip(ORDER, outs):
        back[(-dz) % 4, dy] = o if (dz, dy) == (0, 0) else move_blk(o, (-dz) % 4, dy)
    groups = []
    for dz in range(4):
        mine, other = back[(-dz) % 4, 0], back[(-dz) % 4, 1]
        groups.append(
            jnp.where(
                y == 0,
                jnp.concatenate([mine, other], axis=1),
                jnp.concatenate([other, mine[:, 256:], mine[:, :256]], axis=1),
            )
        )
    ring = jnp.concatenate(groups + groups[:3], axis=1)
    local_grad = lax.dynamic_slice_in_dim(ring, ((4 - z) % 4) * 640, 2560, 1)
    query_grad = dot(selector, local_grad[:MSK], 0, 0).astype(BF)
    return (
        query_grad[None],
        local_grad[None, MSK : MSK + TOK],
        local_grad[None, MSK + TOK :],
        weight_grad,
    )


def solution(mesh):
    return jax.shard_map(
        shards,
        mesh=mesh,
        in_specs=(
            P("dp", "blk", None),
            P("dp", "blk", None),
            P("dp", "blk", None),
            P("dp", "blk"),
            P("dp", "blk", None),
            P(),
        ),
        out_specs=(
            P("dp", "blk", None),
            P("dp", "blk", None),
            P("dp", "blk", None),
            P(("blk", "dp"), None),
        ),
        check_vma=False,
    )
```

time: 652 us -> 151 us (0.23)
  waiting for transfers between devices: 421 us -> 53.7 us
  blocking collectives: 96.1 us -> 0 us
  matrix products: 53.6 us -> 6.58 us
  starting transfers between devices: 21.9 us -> 64.1 us
  local copies, waits for them, and re-layouts: 33.2 us -> 8.69 us
  between operations: 14.9 us -> 1.37 us
  Pallas kernels: 0 us -> 8.72 us
    all_gather x4 -> x0, waiting for transfers between devices: 225 us -> none  [the longest x1 74.2 us: shards(): lax.all_gather(value_local, 'blk', axis=0, tiled=True)]
    reduce_scatter x2 -> x0, waiting for transfers between devices: 180 us -> none  [the longest x1 132 us: shards(): lax.psum_scatter(value_term.reshape(all_rows, width), 'blk', scatter_dime...]
    unnamed x1 -> x0, blocking collectives: 96.1 us -> none
    ppermute x0 -> x34, starting transfers between devices: none -> 64.1 us  [the longest x24 51.7 us: move_blk(): return lax.ppermute(a, 'blk', pairs)]
    ppermute x0 -> x34, waiting for transfers between devices: none -> 53.7 us  [the longest x24 43.3 us: move_blk(): return lax.ppermute(a, 'blk', pairs)]
    dot_general x9, matrix products: 53.6 us -> 6.58 us  [dot(): lax.dot_general(a, b, (((ca,), (cb,)), ((), ())), preferred_element_type=...]
    reshape x2 -> x0, local copies, waits for them, and re-layouts: 22.9 us -> none  [the longest x1 11.5 us: shards(): key_term.reshape(all_rows, width)]
    unnamed x3 -> x0, starting transfers between devices: 21.5 us -> none
  transfers between devices with their start and end apart: 9 -> 34, of which waited for: 7 -> 15; matrix products, arithmetic and copies ran while one was open for 29% -> 10% of each run, Pallas kernels for 0% -> 3%
where the time goes in v1:
time: 151 us; the launch traced here: 150 us
  starting transfers between devices  64.1 us (42%)
  waiting for transfers between devices  53.7 us (36%)
  Pallas kernels  8.72 us (6%)
  local copies, waits for them, and re-layouts  8.69 us (6%)
  other arithmetic  7.14 us (5%)
  matrix products  6.58 us (4%)
    ppermute x24, starting transfers between devices, move_blk(): return lax.ppermute(a, 'blk', pairs)  51.7 us
    ppermute x24, waiting for transfers between devices, move_blk(): return lax.ppermute(a, 'blk', pairs)  43.3 us
    ppermute x10, starting transfers between devices, move_dp(): return lax.ppermute(a, 'dp', pairs)  12.4 us
    ppermute x10, waiting for transfers between devices, move_dp(): return lax.ppermute(a, 'dp', pairs)  10.3 us
    dot_general x9, matrix products, dot(): lax.dot_general(a, b, (((ca,), (cb,)), ((), ())), preferred_element_type=...  6.58 us
    pallas_call x1, Pallas kernels, backward(): pl.pallas_call(backward_kernel, grid=(HEADS_DEV,), in_specs=[pl.BlockSpec...  4.43 us
    pallas_call x1, Pallas kernels, forward(): pl.pallas_call(forward_kernel, grid=(HEADS_DEV,), in_specs=[pl.BlockSpec(...  4.29 us
    dynamic_slice x2, local copies, waits for them, and re-layouts, slab(): own = lax.dynamic_slice_in_dim(a, zz * 640 + yy * 384, 256, axis)  3.31 us
  transfers between devices with their start and end apart: 34, of which 15 were waited for; matrix products, arithmetic and copies ran while one was open for 10% of the time, Pallas kernels for 3%

profile of v1, /device:TPU:6, one launch (start us, length us, event | category | flops | bytes accessed | tf_op | source)
XLA Modules:
  0.0 150.2 jit_solution(12311961921857122981)
XLA Ops:
  4.5 4.0 %collective-permute-start.5 = (bf16[320,384]{1,0:T(8,128)(2,1)}, bf16[320,384]{1,0:T(8,128)(2,1)S(1)}, u32[]{:S(2)}, u32[]{:S(2)}) collective-permute-start(bf16[320,384]{1,0:T(8,128)(2,1)} %get-tuple-element.50), channel_id=1, source_target_pairs={{0,96},{16,112},{32,0},{48,16},{64,32},{80,48},{96,64},{112,80},{1... | collective-permute-start | bytes 737288 | tf_op jit(solution)/shard_map/ppermute | solution.py:25
  8.6 3.0 %collective-permute-start.6 = (bf16[320,384]{1,0:T(8,128)(2,1)}, bf16[320,384]{1,0:T(8,128)(2,1)S(1)}, u32[]{:S(2)}, u32[]{:S(2)}) collective-permute-start(bf16[320,384]{1,0:T(8,128)(2,1)} %get-tuple-element.49), channel_id=1, source_target_pairs={{0,112},{16,96},{32,16},{48,0},{64,48},{80,32},{96,80},{112,64},{1... | collective-permute-start | bytes 737288 | tf_op jit(solution)/shard_map/ppermute | solution.py:25
  12.4 3.3 %collective-permute-start.4 = (bf16[320,384]{1,0:T(8,128)(2,1)}, bf16[320,384]{1,0:T(8,128)(2,1)S(1)}, u32[]{:S(2)}, u32[]{:S(2)}) collective-permute-start(bf16[320,384]{1,0:T(8,128)(2,1)} %get-tuple-element.51), channel_id=1, source_target_pairs={{0,80},{16,64},{32,112},{48,96},{64,16},{80,0},{96,48},{112,32},{1... | collective-permute-start | bytes 737288 | tf_op jit(solution)/shard_map/ppermute | solution.py:25
  18.1 3.2 %constant_dynamic-slice_fusion.1 = bf16[256,4096]{1,0:T(8,128)(2,1)} fusion(bf16[2560,4096]{1,0:T(8,128)(2,1)} %param.11, s32[]{:T(128)S(6)} %select_n.255), kind=kLoop, calls=%fused_computation.85 | loop fusion | bytes 4194308 | tf_op jit(solution)/shard_map/dynamic_slice | solution.py:169
  23.0 6.9 %collective-permute-done.5.refs_6_ = bf16[320,384]{1,0:T(8,128)(2,1)S(1)} collective-permute-done((bf16[320,384]{1,0:T(8,128)(2,1)}, bf16[320,384]{1,0:T(8,128)(2,1)S(1)}, u32[]{:S(2)}, u32[]{:S(2)}) %collective-permute-start.5) | collective-permute-done | bytes 245792 | tf_op jit(solution)/shard_map/ppermute | solution.py:25
  29.9 3.2 %collective-permute-start = (bf16[320,384]{1,0:T(8,128)(2,1)}, bf16[320,384]{1,0:T(8,128)(2,1)S(1)}, u32[]{:S(2)}, u32[]{:S(2)}) collective-permute-start(bf16[320,384]{1,0:T(8,128)(2,1)} %get-tuple-element.55), channel_id=1, source_target_pairs={{0,16},{16,0},{32,48},{48,32},{64,80},{80,64},{96,112},{112,96},{1... | collective-permute-start | bytes 737288 | tf_op jit(solution)/shard_map/ppermute | solution.py:25
  33.1 2.4 %constant_dynamic-slice_fusion = bf16[128,4096]{1,0:T(8,128)(2,1)} fusion(bf16[2560,4096]{1,0:T(8,128)(2,1)} %param.11, s32[]{:T(128)S(6)} %select_n.256), kind=kLoop, calls=%fused_computation.84 | loop fusion | bytes 2097156 | tf_op jit(solution)/shard_map/dynamic_slice | solution.py:170
  35.6 3.7 %collective-permute-start.14 = (bf16[64,2048]{1,0:T(8,128)(2,1)S(1)}, bf16[64,2048]{1,0:T(8,128)(2,1)S(1)}, u32[]{:S(2)}, u32[]{:S(2)}) collective-permute-start(bf16[64,2048]{1,0:T(8,128)(2,1)S(1)} %get-tuple-element.48), channel_id=1, source_target_pairs={{0,96},{16,112},{32,0},{48,16},{64,32},{80,48},{96,64},{112,80},{1... | collective-permute-start | bytes 786440 | tf_op jit(solution)/shard_map/ppermute | solution.py:25
  39.2 2.6 %collective-permute-start.7 = (bf16[64,2048]{1,0:T(8,128)(2,1)S(1)}, bf16[64,2048]{1,0:T(8,128)(2,1)S(1)}, u32[]{:S(2)}, u32[]{:S(2)}) collective-permute-start(bf16[64,2048]{1,0:T(8,128)(2,1)S(1)} %get-tuple-element.44), channel_id=1, source_target_pairs={{0,16},{16,0},{32,48},{48,32},{64,80},{80,64},{96,112},{112,96},{1... | collective-permute-start | bytes 786440 | tf_op jit(solution)/shard_map/ppermute | solution.py:25
  43.0 1.8 %collective-permute-done.refs_1_ = bf16[320,384]{1,0:T(8,128)(2,1)S(1)} collective-permute-done((bf16[320,384]{1,0:T(8,128)(2,1)}, bf16[320,384]{1,0:T(8,128)(2,1)S(1)}, u32[]{:S(2)}, u32[]{:S(2)}) %collective-permute-start) | collective-permute-done | bytes 245792 | tf_op jit(solution)/shard_map/ppermute | solution.py:25
  44.8 4.3 %shard_map.93 = (bf16[3,1024,512]{2,1,0:T(8,128)(2,1)S(1)}, bf16[384,512]{1,0:T(8,128)(2,1)S(1)}) custom-call(bf16[320,384]{1,0:T(8,128)(2,1)S(1)} %get-tuple-element.56.refs_0_, bf16[320,384]{1,0:T(8,128)(2,1)S(1)} %collective-permute-done.refs_1_, bf16[320,384]{1,0:T(8,128)(2,1)S(1)} %collective-permute-done.1.refs_2_, ...), custom_call_target="tpu_custom_call" | custom-call | flops 1200000000 | bytes 6000000 | tf_op jit(solution)/shard_map/pallas_call | solution.py:115
  49.6 4.1 %collective-permute-start.10 = (bf16[128,2048]{1,0:T(8,128)(2,1)S(1)}, bf16[128,2048]{1,0:T(8,128)(2,1)S(1)}, u32[]{:S(2)}, u32[]{:S(2)}) collective-permute-start(bf16[128,2048]{1,0:T(8,128)(2,1)S(1)} %pad_maximum_fusion.3), channel_id=1, source_target_pairs={{0,96},{16,112},{32,0},{48,16},{64,32},{80,48},{96,64},{112,80},{1... | collective-permute-start | bytes 1572872 | tf_op jit(solution)/shard_map/ppermute | solution.py:25
  54.9 2.2 %collective-permute-start.15 = (bf16[32,2048]{1,0:T(8,128)(2,1)S(1)}, bf16[32,2048]{1,0:T(8,128)(2,1)S(1)}, u32[]{:S(2)}, u32[]{:S(2)}) collective-permute-start(bf16[32,2048]{1,0:T(8,128)(2,1)S(1)} %slice.159), channel_id=1, source_target_pairs={{0,96},{16,112},{32,0},{48,16},{64,32},{80,48},{96,64},{112,80},{1... | collective-permute-start | bytes 393224 | tf_op jit(solution)/shard_map/ppermute | solution.py:25
  57.2 8.8 %collective-permute-done.13 = bf16[32,2048]{1,0:T(8,128)(2,1)S(1)} collective-permute-done((bf16[32,2048]{1,0:T(8,128)(2,1)S(1)}, bf16[32,2048]{1,0:T(8,128)(2,1)S(1)}, u32[]{:S(2)}, u32[]{:S(2)}) %collective-permute-start.13) | collective-permute-done | bytes 131104 | tf_op jit(solution)/shard_map/ppermute | solution.py:25
  66.4 1.8 %collective-permute-start.9 = (bf16[64,2048]{1,0:T(8,128)(2,1)S(1)}, bf16[64,2048]{1,0:T(8,128)(2,1)S(1)}, u32[]{:S(2)}, u32[]{:S(2)}) collective-permute-start(bf16[64,2048]{1,0:T(8,128)(2,1)S(1)} %slice.153), channel_id=1, source_target_pairs={{0,32},{16,48},{32,64},{48,80},{64,96},{80,112},{96,0},{112,16},{1... | collective-permute-start | bytes 786440 | tf_op jit(solution)/shard_map/ppermute | solution.py:25
  68.2 3.3 %collective-permute-start.16 = (bf16[256,2048]{1,0:T(8,128)(2,1)S(1)}, bf16[256,2048]{1,0:T(8,128)(2,1)S(1)}, u32[]{:S(2)}, u32[]{:S(2)}) collective-permute-start(bf16[256,2048]{1,0:T(8,128)(2,1)S(1)} %constant_dynamic-update-slice_fusion.6), channel_id=1, source_target_pairs={{0,16},{16,0},{32,48},{48,32},{64,80},{80,64},{96,112},{112,96},{1... | collective-permute-start | bytes 3145736 | tf_op jit(solution)/shard_map/ppermute | solution.py:25
  74.0 4.1 %collective-permute-done.11 = bf16[64,2048]{1,0:T(8,128)(2,1)S(1)} collective-permute-done((bf16[64,2048]{1,0:T(8,128)(2,1)S(1)}, bf16[64,2048]{1,0:T(8,128)(2,1)S(1)}, u32[]{:S(2)}, u32[]{:S(2)}) %collective-permute-start.11) | collective-permute-done | bytes 262176 | tf_op jit(solution)/shard_map/ppermute | solution.py:25
  78.7 11.5 %collective-permute-done.16 = bf16[256,2048]{1,0:T(8,128)(2,1)S(1)} collective-permute-done((bf16[256,2048]{1,0:T(8,128)(2,1)S(1)}, bf16[256,2048]{1,0:T(8,128)(2,1)S(1)}, u32[]{:S(2)}, u32[]{:S(2)}) %collective-permute-start.16) | collective-permute-done | bytes 1048608 | tf_op jit(solution)/shard_map/ppermute | solution.py:25
  93.0 4.4 %shard_map.94 = (bf16[320,384]{1,0:T(8,128)(2,1)S(1)}, bf16[320,256]{1,0:T(8,128)(2,1)S(1)}, bf16[320,384]{1,0:T(8,128)(2,1)S(1)}, bf16[320,256]{1,0:T(8,128)(2,...) custom-call(bf16[320,384]{1,0:T(8,128)(2,1)S(1)} %get-tuple-element., ...), custom_call_target="tpu_custom_call" | custom-call | flops 3000000000 | bytes 9000000 | tf_op jit(solution)/shard_map/pallas_call | solution.py:137
  97.5 3.3 %collective-permute-start.17 = (bf16[320,256]{1,0:T(8,128)(2,1)S(1)}, bf16[320,256]{1,0:T(8,128)(2,1)S(1)}, u32[]{:S(2)}, u32[]{:S(2)}) collective-permute-start(bf16[320,256]{1,0:T(8,128)(2,1)S(1)} %get-tuple-element.17), channel_id=1, source_target_pairs={{0,16},{16,0},{32,48},{48,32},{64,80},{80,64},{96,112},{112,96},{1... | collective-permute-start | bytes 491528 | tf_op jit(solution)/shard_map/ppermute | solution.py:25
  100.7 1.8 %collective-permute-start.18 = (bf16[320,384]{1,0:T(8,128)(2,1)S(1)}, bf16[320,384]{1,0:T(8,128)(2,1)S(1)}, u32[]{:S(2)}, u32[]{:S(2)}) collective-permute-start(bf16[320,384]{1,0:T(8,128)(2,1)S(1)} %get-tuple-element.18), channel_id=1, source_target_pairs={{0,96},{16,112},{32,0},{48,16},{64,32},{80,48},{96,64},{112,80},{1... | collective-permute-start | bytes 737288 | tf_op jit(solution)/shard_map/ppermute | solution.py:25
  102.5 1.8 %collective-permute-start.19 = (bf16[320,256]{1,0:T(8,128)(2,1)S(1)}, bf16[320,256]{1,0:T(8,128)(2,1)S(1)}, u32[]{:S(2)}, u32[]{:S(2)}) collective-permute-start(bf16[320,256]{1,0:T(8,128)(2,1)S(1)} %get-tuple-element.19), channel_id=1, source_target_pairs={{0,112},{16,96},{32,16},{48,0},{64,48},{80,32},{96,80},{112,64},{1... | collective-permute-start | bytes 491528 | tf_op jit(solution)/shard_map/ppermute | solution.py:25
  105.9 5.8 %collective-permute-start.21 = (bf16[320,256]{1,0:T(8,128)(2,1)S(1)}, bf16[320,256]{1,0:T(8,128)(2,1)S(1)}, u32[]{:S(2)}, u32[]{:S(2)}) collective-permute-start(bf16[320,256]{1,0:T(8,128)(2,1)S(1)} %get-tuple-element.21), channel_id=1, source_target_pairs={{0,80},{16,64},{32,112},{48,96},{64,16},{80,0},{96,48},{112,32},{1... | collective-permute-start | bytes 491528 | tf_op jit(solution)/shard_map/ppermute | solution.py:25
  112.0 2.1 %collective-permute-start.23 = (bf16[320,256]{1,0:T(8,128)(2,1)S(1)}, bf16[320,256]{1,0:T(8,128)(2,1)S(1)}, u32[]{:S(2)}, u32[]{:S(2)}) collective-permute-start(bf16[320,256]{1,0:T(8,128)(2,1)S(1)} %get-tuple-element.23), channel_id=1, source_target_pairs={{0,48},{16,32},{32,80},{48,64},{64,112},{80,96},{96,16},{112,0},{1... | collective-permute-start | bytes 491528 | tf_op jit(solution)/shard_map/ppermute | solution.py:25
  114.5 2.1 %collective-permute-done.22 = bf16[320,384]{1,0:T(8,128)(2,1)S(1)} collective-permute-done((bf16[320,384]{1,0:T(8,128)(2,1)S(1)}, bf16[320,384]{1,0:T(8,128)(2,1)S(1)}, u32[]{:S(2)}, u32[]{:S(2)}) %collective-permute-start.22) | collective-permute-done | bytes 245792 | tf_op jit(solution)/shard_map/ppermute | solution.py:25
  116.8 6.0 %collective-permute-done.23 = bf16[320,256]{1,0:T(8,128)(2,1)S(1)} collective-permute-done((bf16[320,256]{1,0:T(8,128)(2,1)S(1)}, bf16[320,256]{1,0:T(8,128)(2,1)S(1)}, u32[]{:S(2)}, u32[]{:S(2)}) %collective-permute-start.23) | collective-permute-done | bytes 163872 | tf_op jit(solution)/shard_map/ppermute | solution.py:25
  126.8 2.4 %collective-permute-start.26 = (bf16[40,2048]{1,0:T(8,128)(2,1)S(1)}, bf16[40,2048]{1,0:T(8,128)(2,1)S(1)}, u32[]{:S(2)}, u32[]{:S(2)}) collective-permute-start(bf16[40,2048]{1,0:T(8,128)(2,1)S(1)} %get-tuple-element.40), channel_id=1, source_target_pairs={{0,8},{1,9},{2,10},{3,11},{4,12},{5,13},{6,14},{7,15},{8,0},{9,1},... | collective-permute-start | bytes 491528 | tf_op jit(solution)/shard_map/ppermute | solution.py:35
  129.8 3.3 %collective-permute-start.30 = (bf16[40,2048]{1,0:T(8,128)(2,1)S(1)}, bf16[40,2048]{1,0:T(8,128)(2,1)S(1)}, u32[]{:S(2)}, u32[]{:S(2)}) collective-permute-start(bf16[40,2048]{1,0:T(8,128)(2,1)S(1)} %get-tuple-element.41), channel_id=1, source_target_pairs={{0,4},{1,5},{2,6},{3,7},{4,8},{5,9},{6,10},{7,11},{8,12},{9,13},{1... | collective-permute-start | bytes 491528 | tf_op jit(solution)/shard_map/ppermute | solution.py:35
  133.4 3.2 %collective-permute-start.32 = (bf16[40,2048]{1,0:T(8,128)(2,1)S(1)}, bf16[40,2048]{1,0:T(8,128)(2,1)S(1)}, u32[]{:S(2)}, u32[]{:S(2)}) collective-permute-start(bf16[40,2048]{1,0:T(8,128)(2,1)S(1)} %get-tuple-element.42), channel_id=1, source_target_pairs={{0,12},{1,13},{2,14},{3,15},{4,0},{5,1},{6,2},{7,3},{8,4},{9,5},{1... | collective-permute-start | bytes 491528 | tf_op jit(solution)/shard_map/ppermute | solution.py:35
  136.6 4.5 %collective-permute-done.27 = bf16[40,2048]{1,0:T(8,128)(2,1)S(1)} collective-permute-done((bf16[40,2048]{1,0:T(8,128)(2,1)S(1)}, bf16[40,2048]{1,0:T(8,128)(2,1)S(1)}, u32[]{:S(2)}, u32[]{:S(2)}) %collective-permute-start.27) | collective-permute-done | bytes 163872 | tf_op jit(solution)/shard_map/ppermute | solution.py:35
  142.6 2.0 %collective-permute-done.32 = bf16[40,2048]{1,0:T(8,128)(2,1)S(1)} collective-permute-done((bf16[40,2048]{1,0:T(8,128)(2,1)S(1)}, bf16[40,2048]{1,0:T(8,128)(2,1)S(1)}, u32[]{:S(2)}, u32[]{:S(2)}) %collective-permute-start.32) | collective-permute-done | bytes 163872 | tf_op jit(solution)/shard_map/ppermute | solution.py:35
  146.0 3.5 %collective-permute-done.33 = bf16[20,2048]{1,0:T(8,128)(2,1)S(1)} collective-permute-done((bf16[20,2048]{1,0:T(8,128)(2,1)S(1)}, bf16[20,2048]{1,0:T(8,128)(2,1)S(1)}, u32[]{:S(2)}, u32[]{:S(2)}) %collective-permute-start.33) | collective-permute-done | bytes 81952 | tf_op jit(solution)/shard_map/ppermute | solution.py:35
  (120 shorter events, 28.7 us)
Async XLA Ops:
  4.5 25.4 %collective-permute-start.5 = (bf16[320,384]{1,0:T(8,128)(2,1)}, bf16[320,384]{1,0:T(8,128)(2,1)S(1)}, u32[]{:S(2)}, u32[]{:S(2)}) collective-permute-start(bf16[320,384]{1,0:T(8,128)(2,1)} %get-tuple-element.50), channel_id=1, source_target_pairs={{0,96},{16,112},{32,0},{48,16},{64,32},{80,48},{96,64},{112,80},{1... | collective-permute-start | bytes 737288 | tf_op jit(solution)/shard_map/ppermute | solution.py:25
  8.6 21.3 %collective-permute-start.6 = (bf16[320,384]{1,0:T(8,128)(2,1)}, bf16[320,384]{1,0:T(8,128)(2,1)S(1)}, u32[]{:S(2)}, u32[]{:S(2)}) collective-permute-start(bf16[320,384]{1,0:T(8,128)(2,1)} %get-tuple-element.49), channel_id=1, source_target_pairs={{0,112},{16,96},{32,16},{48,0},{64,48},{80,32},{96,80},{112,64},{1... | collective-permute-start | bytes 737288 | tf_op jit(solution)/shard_map/ppermute | solution.py:25
  12.4 23.1 %collective-permute-start.3 = (bf16[320,384]{1,0:T(8,128)(2,1)}, bf16[320,384]{1,0:T(8,128)(2,1)S(1)}, u32[]{:S(2)}, u32[]{:S(2)}) collective-permute-start(bf16[320,384]{1,0:T(8,128)(2,1)} %get-tuple-element.52), channel_id=1, source_target_pairs={{0,64},{16,80},{32,96},{48,112},{64,0},{80,16},{96,32},{112,48},{1... | collective-permute-start | bytes 737288 | tf_op jit(solution)/shard_map/ppermute | solution.py:25
  12.4 23.2 %collective-permute-start.4 = (bf16[320,384]{1,0:T(8,128)(2,1)}, bf16[320,384]{1,0:T(8,128)(2,1)S(1)}, u32[]{:S(2)}, u32[]{:S(2)}) collective-permute-start(bf16[320,384]{1,0:T(8,128)(2,1)} %get-tuple-element.51), channel_id=1, source_target_pairs={{0,80},{16,64},{32,112},{48,96},{64,16},{80,0},{96,48},{112,32},{1... | collective-permute-start | bytes 737288 | tf_op jit(solution)/shard_map/ppermute | solution.py:25
  16.4 22.8 %collective-permute-start.1 = (bf16[320,384]{1,0:T(8,128)(2,1)}, bf16[320,384]{1,0:T(8,128)(2,1)S(1)}, u32[]{:S(2)}, u32[]{:S(2)}) collective-permute-start(bf16[320,384]{1,0:T(8,128)(2,1)} %get-tuple-element.54), channel_id=1, source_target_pairs={{0,32},{16,48},{32,64},{48,80},{64,96},{80,112},{96,0},{112,16},{1... | collective-permute-start | bytes 737288 | tf_op jit(solution)/shard_map/ppermute | solution.py:25
  29.9 13.1 %collective-permute-start.2 = (bf16[320,384]{1,0:T(8,128)(2,1)S(1)}, bf16[320,384]{1,0:T(8,128)(2,1)S(1)}, u32[]{:S(2)}, u32[]{:S(2)}) collective-permute-start(bf16[320,384]{1,0:T(8,128)(2,1)S(1)} %get-tuple-element.53), channel_id=1, source_target_pairs={{0,48},{16,32},{32,80},{48,64},{64,112},{80,96},{96,16},{112,0},{1... | collective-permute-start | bytes 737288 | tf_op jit(solution)/shard_map/ppermute | solution.py:25
  29.9 14.9 %collective-permute-start = (bf16[320,384]{1,0:T(8,128)(2,1)}, bf16[320,384]{1,0:T(8,128)(2,1)S(1)}, u32[]{:S(2)}, u32[]{:S(2)}) collective-permute-start(bf16[320,384]{1,0:T(8,128)(2,1)} %get-tuple-element.55), channel_id=1, source_target_pairs={{0,16},{16,0},{32,48},{48,32},{64,80},{80,64},{96,112},{112,96},{1... | collective-permute-start | bytes 737288 | tf_op jit(solution)/shard_map/ppermute | solution.py:25
  35.5 18.2 %collective-permute-start.12 = (bf16[64,2048]{1,0:T(8,128)(2,1)S(1)}, bf16[64,2048]{1,0:T(8,128)(2,1)S(1)}, u32[]{:S(2)}, u32[]{:S(2)}) collective-permute-start(bf16[64,2048]{1,0:T(8,128)(2,1)S(1)} %get-tuple-element.48), channel_id=1, source_target_pairs={{0,32},{16,48},{32,64},{48,80},{64,96},{80,112},{96,0},{112,16},{1... | collective-permute-start | bytes 786440 | tf_op jit(solution)/shard_map/ppermute | solution.py:25
  35.6 19.3 %collective-permute-start.14 = (bf16[64,2048]{1,0:T(8,128)(2,1)S(1)}, bf16[64,2048]{1,0:T(8,128)(2,1)S(1)}, u32[]{:S(2)}, u32[]{:S(2)}) collective-permute-start(bf16[64,2048]{1,0:T(8,128)(2,1)S(1)} %get-tuple-element.48), channel_id=1, source_target_pairs={{0,96},{16,112},{32,0},{48,16},{64,32},{80,48},{96,64},{112,80},{1... | collective-permute-start | bytes 786440 | tf_op jit(solution)/shard_map/ppermute | solution.py:25
  39.2 10.2 %collective-permute-start.7 = (bf16[64,2048]{1,0:T(8,128)(2,1)S(1)}, bf16[64,2048]{1,0:T(8,128)(2,1)S(1)}, u32[]{:S(2)}, u32[]{:S(2)}) collective-permute-start(bf16[64,2048]{1,0:T(8,128)(2,1)S(1)} %get-tuple-element.44), channel_id=1, source_target_pairs={{0,16},{16,0},{32,48},{48,32},{64,80},{80,64},{96,112},{112,96},{1... | collective-permute-start | bytes 786440 | tf_op jit(solution)/shard_map/ppermute | solution.py:25
  49.5 16.8 %collective-permute-start.8 = (bf16[128,2048]{1,0:T(8,128)(2,1)S(1)}, bf16[128,2048]{1,0:T(8,128)(2,1)S(1)}, u32[]{:S(2)}, u32[]{:S(2)}) collective-permute-start(bf16[128,2048]{1,0:T(8,128)(2,1)S(1)} %pad_maximum_fusion.3), channel_id=1, source_target_pairs={{0,32},{16,48},{32,64},{48,80},{64,96},{80,112},{96,0},{112,16},{1... | collective-permute-start | bytes 1572872 | tf_op jit(solution)/shard_map/ppermute | solution.py:25
  49.6 21.9 %collective-permute-start.10 = (bf16[128,2048]{1,0:T(8,128)(2,1)S(1)}, bf16[128,2048]{1,0:T(8,128)(2,1)S(1)}, u32[]{:S(2)}, u32[]{:S(2)}) collective-permute-start(bf16[128,2048]{1,0:T(8,128)(2,1)S(1)} %pad_maximum_fusion.3), channel_id=1, source_target_pairs={{0,96},{16,112},{32,0},{48,16},{64,32},{80,48},{96,64},{112,80},{1... | collective-permute-start | bytes 1572872 | tf_op jit(solution)/shard_map/ppermute | solution.py:25
  53.7 12.2 %collective-permute-start.13 = (bf16[32,2048]{1,0:T(8,128)(2,1)S(1)}, bf16[32,2048]{1,0:T(8,128)(2,1)S(1)}, u32[]{:S(2)}, u32[]{:S(2)}) collective-permute-start(bf16[32,2048]{1,0:T(8,128)(2,1)S(1)} %slice.158), channel_id=1, source_target_pairs={{0,32},{16,48},{32,64},{48,80},{64,96},{80,112},{96,0},{112,16},{1... | collective-permute-start | bytes 393224 | tf_op jit(solution)/shard_map/ppermute | solution.py:25
  54.9 11.4 %collective-permute-start.15 = (bf16[32,2048]{1,0:T(8,128)(2,1)S(1)}, bf16[32,2048]{1,0:T(8,128)(2,1)S(1)}, u32[]{:S(2)}, u32[]{:S(2)}) collective-permute-start(bf16[32,2048]{1,0:T(8,128)(2,1)S(1)} %slice.159), channel_id=1, source_target_pairs={{0,96},{16,112},{32,0},{48,16},{64,32},{80,48},{96,64},{112,80},{1... | collective-permute-start | bytes 393224 | tf_op jit(solution)/shard_map/ppermute | solution.py:25
  66.4 7.7 %collective-permute-start.9 = (bf16[64,2048]{1,0:T(8,128)(2,1)S(1)}, bf16[64,2048]{1,0:T(8,128)(2,1)S(1)}, u32[]{:S(2)}, u32[]{:S(2)}) collective-permute-start(bf16[64,2048]{1,0:T(8,128)(2,1)S(1)} %slice.153), channel_id=1, source_target_pairs={{0,32},{16,48},{32,64},{48,80},{64,96},{80,112},{96,0},{112,16},{1... | collective-permute-start | bytes 786440 | tf_op jit(solution)/shard_map/ppermute | solution.py:25
  68.2 22.0 %collective-permute-start.16 = (bf16[256,2048]{1,0:T(8,128)(2,1)S(1)}, bf16[256,2048]{1,0:T(8,128)(2,1)S(1)}, u32[]{:S(2)}, u32[]{:S(2)}) collective-permute-start(bf16[256,2048]{1,0:T(8,128)(2,1)S(1)} %constant_dynamic-update-slice_fusion.6), channel_id=1, source_target_pairs={{0,16},{16,0},{32,48},{48,32},{64,80},{80,64},{96,112},{112,96},{1... | collective-permute-start | bytes 3145736 | tf_op jit(solution)/shard_map/ppermute | solution.py:25
  71.5 6.6 %collective-permute-start.11 = (bf16[64,2048]{1,0:T(8,128)(2,1)S(1)}, bf16[64,2048]{1,0:T(8,128)(2,1)S(1)}, u32[]{:S(2)}, u32[]{:S(2)}) collective-permute-start(bf16[64,2048]{1,0:T(8,128)(2,1)S(1)} %slice.154), channel_id=1, source_target_pairs={{0,96},{16,112},{32,0},{48,16},{64,32},{80,48},{96,64},{112,80},{1... | collective-permute-start | bytes 786440 | tf_op jit(solution)/shard_map/ppermute | solution.py:25
  97.5 8.4 %collective-permute-start.17 = (bf16[320,256]{1,0:T(8,128)(2,1)S(1)}, bf16[320,256]{1,0:T(8,128)(2,1)S(1)}, u32[]{:S(2)}, u32[]{:S(2)}) collective-permute-start(bf16[320,256]{1,0:T(8,128)(2,1)S(1)} %get-tuple-element.17), channel_id=1, source_target_pairs={{0,16},{16,0},{32,48},{48,32},{64,80},{80,64},{96,112},{112,96},{1... | collective-permute-start | bytes 491528 | tf_op jit(solution)/shard_map/ppermute | solution.py:25
  100.7 11.1 %collective-permute-start.18 = (bf16[320,384]{1,0:T(8,128)(2,1)S(1)}, bf16[320,384]{1,0:T(8,128)(2,1)S(1)}, u32[]{:S(2)}, u32[]{:S(2)}) collective-permute-start(bf16[320,384]{1,0:T(8,128)(2,1)S(1)} %get-tuple-element.18), channel_id=1, source_target_pairs={{0,96},{16,112},{32,0},{48,16},{64,32},{80,48},{96,64},{112,80},{1... | collective-permute-start | bytes 737288 | tf_op jit(solution)/shard_map/ppermute | solution.py:25
  102.5 9.5 %collective-permute-start.19 = (bf16[320,256]{1,0:T(8,128)(2,1)S(1)}, bf16[320,256]{1,0:T(8,128)(2,1)S(1)}, u32[]{:S(2)}, u32[]{:S(2)}) collective-permute-start(bf16[320,256]{1,0:T(8,128)(2,1)S(1)} %get-tuple-element.19), channel_id=1, source_target_pairs={{0,112},{16,96},{32,16},{48,0},{64,48},{80,32},{96,80},{112,64},{1... | collective-permute-start | bytes 491528 | tf_op jit(solution)/shard_map/ppermute | solution.py:25
  104.3 9.9 %collective-permute-start.20 = (bf16[320,384]{1,0:T(8,128)(2,1)S(1)}, bf16[320,384]{1,0:T(8,128)(2,1)S(1)}, u32[]{:S(2)}, u32[]{:S(2)}) collective-permute-start(bf16[320,384]{1,0:T(8,128)(2,1)S(1)} %get-tuple-element.20), channel_id=1, source_target_pairs={{0,64},{16,80},{32,96},{48,112},{64,0},{80,16},{96,32},{112,48},{1... | collective-permute-start | bytes 737288 | tf_op jit(solution)/shard_map/ppermute | solution.py:25
  104.6 12.0 %collective-permute-start.22 = (bf16[320,384]{1,0:T(8,128)(2,1)S(1)}, bf16[320,384]{1,0:T(8,128)(2,1)S(1)}, u32[]{:S(2)}, u32[]{:S(2)}) collective-permute-start(bf16[320,384]{1,0:T(8,128)(2,1)S(1)} %get-tuple-element.22), channel_id=1, source_target_pairs={{0,32},{16,48},{32,64},{48,80},{64,96},{80,112},{96,0},{112,16},{1... | collective-permute-start | bytes 737288 | tf_op jit(solution)/shard_map/ppermute | solution.py:25
  105.9 10.7 %collective-permute-start.21 = (bf16[320,256]{1,0:T(8,128)(2,1)S(1)}, bf16[320,256]{1,0:T(8,128)(2,1)S(1)}, u32[]{:S(2)}, u32[]{:S(2)}) collective-permute-start(bf16[320,256]{1,0:T(8,128)(2,1)S(1)} %get-tuple-element.21), channel_id=1, source_target_pairs={{0,80},{16,64},{32,112},{48,96},{64,16},{80,0},{96,48},{112,32},{1... | collective-permute-start | bytes 491528 | tf_op jit(solution)/shard_map/ppermute | solution.py:25
  111.8 13.9 %collective-permute-start.24 = (bf16[160,2048]{1,0:T(8,128)(2,1)S(1)}, bf16[160,2048]{1,0:T(8,128)(2,1)S(1)}, u32[]{:S(2)}, u32[]{:S(2)}) collective-permute-start(bf16[160,2048]{1,0:T(8,128)(2,1)S(1)} %convolution_convert_fusion.3), channel_id=1, source_target_pairs={{0,1},{1,0},{2,3},{3,2},{4,5},{5,4},{6,7},{7,6},{8,9},{9,8},{10,11... | collective-permute-start | bytes 1966088 | tf_op jit(solution)/shard_map/ppermute | solution.py:35
  112.0 10.8 %collective-permute-start.23 = (bf16[320,256]{1,0:T(8,128)(2,1)S(1)}, bf16[320,256]{1,0:T(8,128)(2,1)S(1)}, u32[]{:S(2)}, u32[]{:S(2)}) collective-permute-start(bf16[320,256]{1,0:T(8,128)(2,1)S(1)} %get-tuple-element.23), channel_id=1, source_target_pairs={{0,48},{16,32},{32,80},{48,64},{64,112},{80,96},{96,16},{112,0},{1... | collective-permute-start | bytes 491528 | tf_op jit(solution)/shard_map/ppermute | solution.py:25
  114.2 15.0 %collective-permute-start.29 = (bf16[160,2048]{1,0:T(8,128)(2,1)S(1)}, bf16[160,2048]{1,0:T(8,128)(2,1)S(1)}, u32[]{:S(2)}, u32[]{:S(2)}) collective-permute-start(bf16[160,2048]{1,0:T(8,128)(2,1)S(1)} %convolution_convert_fusion.2), channel_id=1, source_target_pairs={{0,1},{1,0},{2,3},{3,2},{4,5},{5,4},{6,7},{7,6},{8,9},{9,8},{10,11... | collective-permute-start | bytes 1966088 | tf_op jit(solution)/shard_map/ppermute | solution.py:35
  126.3 7.1 %collective-permute-start.25 = (bf16[40,2048]{1,0:T(8,128)(2,1)S(1)}, bf16[40,2048]{1,0:T(8,128)(2,1)S(1)}, u32[]{:S(2)}, u32[]{:S(2)}) collective-permute-start(bf16[40,2048]{1,0:T(8,128)(2,1)S(1)} %get-tuple-element.38), channel_id=1, source_target_pairs={{0,4},{1,5},{2,6},{3,7},{4,8},{5,9},{6,10},{7,11},{8,12},{9,13},{1... | collective-permute-start | bytes 491528 | tf_op jit(solution)/shard_map/ppermute | solution.py:35
  126.8 9.8 %collective-permute-start.26 = (bf16[40,2048]{1,0:T(8,128)(2,1)S(1)}, bf16[40,2048]{1,0:T(8,128)(2,1)S(1)}, u32[]{:S(2)}, u32[]{:S(2)}) collective-permute-start(bf16[40,2048]{1,0:T(8,128)(2,1)S(1)} %get-tuple-element.40), channel_id=1, source_target_pairs={{0,8},{1,9},{2,10},{3,11},{4,12},{5,13},{6,14},{7,15},{8,0},{9,1},... | collective-permute-start | bytes 491528 | tf_op jit(solution)/shard_map/ppermute | solution.py:35
  129.2 11.9 %collective-permute-start.27 = (bf16[40,2048]{1,0:T(8,128)(2,1)S(1)}, bf16[40,2048]{1,0:T(8,128)(2,1)S(1)}, u32[]{:S(2)}, u32[]{:S(2)}) collective-permute-start(bf16[40,2048]{1,0:T(8,128)(2,1)S(1)} %get-tuple-element.39), channel_id=1, source_target_pairs={{0,12},{1,13},{2,14},{3,15},{4,0},{5,1},{6,2},{7,3},{8,4},{9,5},{1... | collective-permute-start | bytes 491528 | tf_op jit(solution)/shard_map/ppermute | solution.py:35
  129.8 12.8 %collective-permute-start.30 = (bf16[40,2048]{1,0:T(8,128)(2,1)S(1)}, bf16[40,2048]{1,0:T(8,128)(2,1)S(1)}, u32[]{:S(2)}, u32[]{:S(2)}) collective-permute-start(bf16[40,2048]{1,0:T(8,128)(2,1)S(1)} %get-tuple-element.41), channel_id=1, source_target_pairs={{0,4},{1,5},{2,6},{3,7},{4,8},{5,9},{6,10},{7,11},{8,12},{9,13},{1... | collective-permute-start | bytes 491528 | tf_op jit(solution)/shard_map/ppermute | solution.py:35
  133.1 9.5 %collective-permute-start.31 = (bf16[40,2048]{1,0:T(8,128)(2,1)S(1)}, bf16[40,2048]{1,0:T(8,128)(2,1)S(1)}, u32[]{:S(2)}, u32[]{:S(2)}) collective-permute-start(bf16[40,2048]{1,0:T(8,128)(2,1)S(1)} %get-tuple-element.43), channel_id=1, source_target_pairs={{0,8},{1,9},{2,10},{3,11},{4,12},{5,13},{6,14},{7,15},{8,0},{9,1},... | collective-permute-start | bytes 491528 | tf_op jit(solution)/shard_map/ppermute | solution.py:35
  133.4 11.2 %collective-permute-start.32 = (bf16[40,2048]{1,0:T(8,128)(2,1)S(1)}, bf16[40,2048]{1,0:T(8,128)(2,1)S(1)}, u32[]{:S(2)}, u32[]{:S(2)}) collective-permute-start(bf16[40,2048]{1,0:T(8,128)(2,1)S(1)} %get-tuple-element.42), channel_id=1, source_target_pairs={{0,12},{1,13},{2,14},{3,15},{4,0},{5,1},{6,2},{7,3},{8,4},{9,5},{1... | collective-permute-start | bytes 491528 | tf_op jit(solution)/shard_map/ppermute | solution.py:35
  (9 other events, 69.7 us)

commit v2 on v0

v2 whole, which is shorter than its diff:
```python
import math

import jax
import jax.numpy as jnp
from jax import lax
from jax.experimental import pallas as pl
from jax.experimental.pallas import tpu as pltpu
from jax.sharding import PartitionSpec as P

HEAD_DIM = 128
SCALE = 1.0 / math.sqrt(HEAD_DIM)
BF = jnp.bfloat16
F32 = jnp.float32
TOK = 128
MSK = 64
WIDTH = 2560
HEADS_DEV = 3
SLAB = HEADS_DEV * HEAD_DIM
QUERIES = 8 * MSK
KEYS = 8 * TOK
ROWS_OUT = MSK + 2 * TOK
ROWS_BACK = ROWS_OUT + 80
ROWS_IN = 2 * MSK + 2 * TOK
PARAMS = pltpu.CompilerParams(vmem_limit_bytes=40 * 2**20)


def exchange(a):
    return lax.all_to_all(a, "blk", 0, 0, tiled=True)


def move_x(a, dx):
    return lax.ppermute(a, "dp", [(i, (i + 4 * dx) % 16) for i in range(16)])


def move_y(a, dl, dh):
    pairs = []
    for i in range(128):
        b, d = i // 16, i % 16
        pairs.append((i, (b ^ dh) * 16 + (d ^ (2 * dl))))
    return lax.ppermute(a, ("blk", "dp"), pairs)


def move_z(a, dz):
    return lax.ppermute(a, "blk", [(i, (i + 2 * dz) % 8) for i in range(8)])


def swap_y(a):
    return lax.ppermute(a, "blk", [(i, i ^ 1) for i in range(8)])


def swap_core(a):
    return lax.ppermute(a, "dp", [(i, i ^ 1) for i in range(16)])


def dot(a, b, ca, cb):
    return lax.dot_general(a, b, (((ca,), (cb,)), ((), ())), preferred_element_type=F32)


def cost(flops, moved, exps=0):
    return pl.CostEstimate(flops=int(flops), bytes_accessed=int(moved), transcendentals=int(exps))


def slabs_of(query, grad, key, value):
    def kernel(*refs):
        out_ref = refs[4]
        for j in range(8):
            pair = (j // 2) * 640 + (j % 2) * 384
            shared = (j // 2) * 640 + 256
            row = 0
            for ref in refs[:4]:
                at = pl.ds(row, ref.shape[0])
                out_ref[j, at, 0:256] = ref[:, pair : pair + 256]
                out_ref[j, at, 256:SLAB] = ref[:, shared : shared + HEAD_DIM]
                row += ref.shape[0]

    return pl.pallas_call(
        kernel,
        out_shape=jax.ShapeDtypeStruct((8, ROWS_IN, SLAB), BF),
        compiler_params=PARAMS,
        cost_estimate=cost(0, ROWS_IN * WIDTH * 4.4),
    )(query, grad, key, value)


def outer(columns, att_rows, cot_parts):
    width = cot_parts[0].shape[1]
    rows = att_rows.shape[0] // 2
    tile = 512

    def kernel(column_ref, att_ref, *refs):
        att = jnp.concatenate(
            [
                att_ref[:, pl.ds(pl.multiple_of(column_ref[i], 2 * MSK), 2 * MSK)]
                for i in range(4)
            ],
            axis=1,
        )
        cots = jnp.concatenate([r[...] for r in refs[:4]], axis=0)
        refs[4][...] = dot(att[:rows], cots, 1, 0)
        refs[5][...] = dot(att[rows:], cots, 1, 0).astype(BF)

    out = pl.BlockSpec((rows, tile), lambda i, *_: (0, i))
    return pl.pallas_call(
        kernel,
        grid_spec=pltpu.PrefetchScalarGridSpec(
            num_scalar_prefetch=1,
            grid=(width // tile,),
            in_specs=[pl.BlockSpec((2 * rows, QUERIES), lambda i, *_: (0, 0))]
            + [pl.BlockSpec((2 * MSK, tile), lambda i, *_: (0, i))] * 4,
            out_specs=[out, out],
        ),
        out_shape=[
            jax.ShapeDtypeStruct((rows, width), F32),
            jax.ShapeDtypeStruct((rows, width), BF),
        ],
        compiler_params=PARAMS,
        cost_estimate=cost(1.4e9, 8e6),
    )(columns, att_rows, *cot_parts)


def finish(back, selector):
    def kernel(back_ref, selector_ref, query_ref, key_ref, value_ref):
        def put(to, query, key, value):
            query_ref[:, to] = dot(selector_ref[...], query, 0, 0).astype(BF)
            key_ref[:, to] = key
            value_ref[:, to] = value

        for j in range(8):
            at = (j // 2) * 640 + (j % 2) * 384
            put(
                slice(at, at + 256),
                back_ref[j, 0:MSK],
                back_ref[j, MSK : MSK + TOK],
                back_ref[j, MSK + TOK : ROWS_OUT],
            )
        for j in range(0, 8, 2):
            at = (j // 2) * 640 + 256
            halves = [
                jnp.concatenate(
                    [back_ref[k, ROWS_OUT:, 0:HEAD_DIM], back_ref[k, ROWS_OUT:, HEAD_DIM:]], axis=0
                )
                for k in (j, j + 1)
            ]
            query = jnp.concatenate([h[TOK:] for h in halves], axis=0)
            put(slice(at, at + HEAD_DIM), query, halves[0][0:TOK], halves[1][0:TOK])

    return pl.pallas_call(
        kernel,
        out_shape=[jax.ShapeDtypeStruct((TOK, WIDTH), BF)] * 3,
        compiler_params=PARAMS,
        cost_estimate=cost(5e7, 4e6),
    )(back, selector)


def forward_kernel(in_ref, prob_ref, att_ref):
    key = in_ref[:, 2 * MSK : 2 * MSK + TOK].reshape(KEYS, HEAD_DIM)
    value = in_ref[:, 2 * MSK + TOK :].reshape(KEYS, HEAD_DIM)
    query = in_ref[:, 0:MSK].reshape(QUERIES, HEAD_DIM)
    scores = dot(key, query, 1, 1) * SCALE
    top = jnp.max(scores, axis=0, keepdims=True)
    raised = jnp.exp(scores - top)
    total = jnp.sum(raised, axis=0, keepdims=True)
    probs = (raised * (1.0 / total)).astype(BF)
    prob_ref[0] = probs
    att_ref[...] = dot(value.T, probs, 1, 0).astype(BF)


def backward_kernel(place_ref, in_ref, prob_ref, att_ref, out_ref):
    key = in_ref[:, 2 * MSK : 2 * MSK + TOK].reshape(KEYS, HEAD_DIM)
    value = in_ref[:, 2 * MSK + TOK :].reshape(KEYS, HEAD_DIM)
    query = in_ref[:, 0:MSK].reshape(QUERIES, HEAD_DIM)
    grad = in_ref[:, MSK : 2 * MSK].reshape(QUERIES, HEAD_DIM)
    delta = jnp.sum(grad.T.astype(F32) * att_ref[...].astype(F32), axis=0, keepdims=True)
    probs = prob_ref[0]
    prob_grad = dot(value, grad, 1, 1)
    score_grad = (probs.astype(F32) * (prob_grad - delta)).astype(BF)
    query_grad = (dot(key.T, score_grad, 1, 0) * SCALE).T.astype(BF)
    key_grad = (dot(score_grad, query, 1, 0) * SCALE).astype(BF)
    value_grad = dot(probs, grad, 1, 0).astype(BF)
    head = pl.program_id(0)
    query_grad = query_grad.reshape(8, MSK, HEAD_DIM)
    key_grad = key_grad.reshape(8, TOK, HEAD_DIM)
    value_grad = value_grad.reshape(8, TOK, HEAD_DIM)

    def own(at):
        out_ref[:, 0:MSK, at] = query_grad
        out_ref[:, MSK : MSK + TOK, at] = key_grad
        out_ref[:, MSK + TOK : ROWS_OUT, at] = value_grad

    @pl.when(head == 0)
    def _():
        own(slice(0, HEAD_DIM))

    @pl.when(head == 1)
    def _():
        own(slice(HEAD_DIM, 2 * HEAD_DIM))

    def half(grad, query):
        out_ref[:, ROWS_OUT:, 0:HEAD_DIM] = grad[:, 0:80]
        out_ref[:, ROWS_OUT : ROWS_OUT + 48, HEAD_DIM:] = grad[:, 80:]
        out_ref[:, ROWS_OUT + 48 :, HEAD_DIM:] = query

    @pl.when((head == 2) & (place_ref[0] == 0))
    def _():
        half(key_grad, query_grad[:, 0:32])

    @pl.when((head == 2) & (place_ref[0] == 1))
    def _():
        half(value_grad, query_grad[:, 32:])


def head_block(rows):
    return pl.BlockSpec((8, rows, HEAD_DIM), lambda h, *_: (0, 0, h))


PROB_BLOCK = pl.BlockSpec((1, KEYS, QUERIES), lambda h, *_: (h, 0, 0))
ATT_BLOCK = pl.BlockSpec((HEAD_DIM, QUERIES), lambda h, *_: (h, 0))


def forward(sent):
    return pl.pallas_call(
        forward_kernel,
        grid=(HEADS_DEV,),
        in_specs=[head_block(ROWS_IN)],
        out_specs=[PROB_BLOCK, ATT_BLOCK],
        out_shape=[
            jax.ShapeDtypeStruct((HEADS_DEV, KEYS, QUERIES), BF),
            jax.ShapeDtypeStruct((SLAB, QUERIES), BF),
        ],
        compiler_params=PARAMS,
        cost_estimate=cost(1.2e9, 6e6, 1.6e6),
    )(sent)


def backward(place, sent, probs, att):
    return pl.pallas_call(
        backward_kernel,
        grid_spec=pltpu.PrefetchScalarGridSpec(
            num_scalar_prefetch=1,
            grid=(HEADS_DEV,),
            in_specs=[head_block(ROWS_IN), PROB_BLOCK, ATT_BLOCK],
            out_specs=pl.BlockSpec((8, ROWS_BACK, 2 * HEAD_DIM), lambda h, *_: (0, 0, 0)),
        ),
        out_shape=jax.ShapeDtypeStruct((8, ROWS_BACK, 2 * HEAD_DIM), BF),
        compiler_params=PARAMS,
        cost_estimate=cost(3e9, 9e6),
    )(place, sent, probs, att)


def shards(query_states, key_states, value_states, mask_index, cotangent, out_weight):
    blk, dp = lax.axis_index("blk"), lax.axis_index("dp")
    z, y, core = blk // 2, blk % 2, dp % 2
    x, low = dp // 4, (dp // 2) % 2
    steps = mask_index[0] - blk * TOK

    cot = cotangent[0]
    half = cot.shape[1] // 2
    cot_kept = lax.dynamic_slice_in_dim(cot, y * half, half, 1)
    cot_got = swap_y(lax.dynamic_slice_in_dim(cot, (1 - y) * half, half, 1))
    steps, cot_got = lax.optimization_barrier((steps, cot_got))
    cot_pair = jnp.where(
        y == 0,
        jnp.concatenate([cot_kept, cot_got], axis=0),
        jnp.concatenate([cot_got, cot_kept], axis=0),
    )

    selector = (steps[:, None] == jnp.arange(TOK, dtype=jnp.int32)[None, :]).astype(BF)
    masked_query = dot(selector, query_states[0], 1, 0).astype(BF)
    masked_grad = dot(cot, out_weight, 1, 1).astype(BF)
    heads_in = exchange(
        slabs_of(masked_query, masked_grad, key_states[0], value_states[0])
    )
    cot_parts = [cot_pair] + [move_z(cot_pair, dz) for dz in (3, 2, 1)]
    probs, att = forward(heads_in)
    att_got = swap_y(att[:256])
    outs = backward(y[None].astype(jnp.int32), heads_in, probs, att)

    back = exchange(outs)
    cot_parts, att_got, _ = lax.optimization_barrier((cot_parts, att_got, outs))
    r = jnp.arange(640, dtype=jnp.int32)
    rc, rx, rl, rh, rr = r // 320, (r // 80) % 4, (r // 40) % 2, (r // 20) % 2, r % 20
    wanted = (
        ((y + rh) % 2) * 320
        + ((x + rx) % 4) * 80
        + ((low + rl) % 2) * 40
        + ((core + rc) % 2) * 20
        + rr
    )
    low_place = jnp.where(y == 0, wanted, wanted + 384)
    high_place = jnp.where(y == 0, wanted, wanted - 384)
    index = jnp.where(wanted < 256, low_place, jnp.where(wanted < 384, wanted, high_place))
    pick = (index[:, None] == r[None, :]).astype(BF)
    att_rows = (dot(pick[:, :SLAB], att, 1, 0) + dot(pick[:, SLAB:], att_got, 1, 0)).astype(BF)
    columns = (z + jnp.arange(4, dtype=jnp.int32)) % 4 * (2 * MSK)
    kept, sent = outer(columns, att_rows, cot_parts)
    sent = swap_core(sent)
    chunks = [
        kept[i * 80 : (i + 1) * 80] + sent[i * 80 : (i + 1) * 80].astype(F32) for i in range(4)
    ]
    acc = chunks[0]
    for dx in (1, 2, 3):
        acc = acc + move_x(chunks[dx].astype(BF), dx).astype(F32)
    back, acc = lax.optimization_barrier((back, acc))
    quarter = acc.astype(BF)
    own_half = acc[:20] + move_y(quarter[40:60], 1, 0).astype(F32)
    other_half = move_y(quarter[20:40], 0, 1).astype(F32) + move_y(quarter[60:], 1, 1).astype(F32)
    weight_grad = jnp.where(
        y == 0,
        jnp.concatenate([own_half, other_half], axis=1),
        jnp.concatenate([other_half, own_half], axis=1),
    )

    grads = finish(back, selector)
    return (*(g[None] for g in grads), weight_grad)


def solution(mesh):
    return jax.shard_map(
        shards,
        mesh=mesh,
        in_specs=(
            P("dp", "blk", None),
            P("dp", "blk", None),
            P("dp", "blk", None),
            P("dp", "blk"),
            P("dp", "blk", None),
            P(),
        ),
        out_specs=(
            P("dp", "blk", None),
            P("dp", "blk", None),
            P("dp", "blk", None),
            P(("blk", "dp"), None),
        ),
        check_vma=False,
    )
```

time: 652 us -> 124 us (0.19)
  waiting for transfers between devices: 421 us -> 53.5 us
  blocking collectives: 96.1 us -> 0 us
  matrix products: 53.6 us -> 11.7 us
  local copies, waits for them, and re-layouts: 33.2 us -> 4.14 us
  Pallas kernels: 0 us -> 17.1 us
  between operations: 14.9 us -> 0.89 us
  starting transfers between devices: 21.9 us -> 28.9 us
    all_gather x4 -> x0, waiting for transfers between devices: 225 us -> none  [the longest x1 74.2 us: shards(): lax.all_gather(value_local, 'blk', axis=0, tiled=True)]
    reduce_scatter x2 -> x0, waiting for transfers between devices: 180 us -> none  [the longest x1 132 us: shards(): lax.psum_scatter(value_term.reshape(all_rows, width), 'blk', scatter_dime...]
    unnamed x1 -> x0, blocking collectives: 96.1 us -> none
    dot_general x9 -> x4, matrix products: 53.6 us -> 11.7 us  [dot(): lax.dot_general(a, b, (((ca,), (cb,)), ((), ())), preferred_element_type=...]
    all_to_all x0 -> x2, waiting for transfers between devices: none -> 34.5 us  [exchange(): return lax.all_to_all(a, 'blk', 0, 0, tiled=True)]
    reshape x2 -> x0, local copies, waits for them, and re-layouts: 22.9 us -> none  [the longest x1 11.5 us: shards(): key_term.reshape(all_rows, width)]
    unnamed x3 -> x0, starting transfers between devices: 21.5 us -> none
    ppermute x0 -> x12, starting transfers between devices: none -> 19.7 us  [the longest x2 6.89 us: swap_y(): return lax.ppermute(a, 'blk', [(i, i ^ 1) for i in range(8)])]
  transfers between devices with their start and end apart: 9 -> 14, of which waited for: 7 -> 7; matrix products, arithmetic and copies ran while one was open for 29% -> 14% of each run, Pallas kernels for 0% -> 8%
where the time goes in v2:
time: 124 us; the launch traced here: 123 us
  waiting for transfers between devices  53.5 us (43%)
  starting transfers between devices  28.9 us (23%)
  Pallas kernels  17.1 us (14%)
  matrix products  11.7 us (9%)
  other arithmetic  6.81 us (5%)
  local copies, waits for them, and re-layouts  4.14 us (3%)
    all_to_all x2, waiting for transfers between devices, exchange(): return lax.all_to_all(a, 'blk', 0, 0, tiled=True)  34.5 us
    ppermute x3, waiting for transfers between devices, move_x(): return lax.ppermute(a, 'dp', [(i, (i + 4 * dx) % 16) for i in range(16)])  15.7 us
    dot_general x4, matrix products, dot(): lax.dot_general(a, b, (((ca,), (cb,)), ((), ())), preferred_element_type=...  11.7 us
    all_to_all x2, starting transfers between devices, exchange(): return lax.all_to_all(a, 'blk', 0, 0, tiled=True)  9.18 us
    ppermute x2, starting transfers between devices, swap_y(): return lax.ppermute(a, 'blk', [(i, i ^ 1) for i in range(8)])  6.89 us
    pallas_call x1, Pallas kernels, outer(): pl.pallas_call(kernel, grid_spec=pltpu.PrefetchScalarGridSpec(num_scalar_...  5.28 us
    ppermute x3, starting transfers between devices, move_z(): return lax.ppermute(a, 'blk', [(i, (i + 2 * dz) % 8) for i in range(8)])  5.02 us
    ppermute x3, starting transfers between devices, move_y(): return lax.ppermute(a, ('blk', 'dp'), pairs)  4.84 us
  transfers between devices with their start and end apart: 14, of which 7 were waited for; matrix products, arithmetic and copies ran while one was open for 14% of the time, Pallas kernels for 8%

profile of v2, /device:TPU:6, one launch (start us, length us, event | category | flops | bytes accessed | tf_op | source)
XLA Modules:
  0.0 123.1 jit_solution(12669900055327635229)
XLA Ops:
  0.7 1.9 %dynamic-slice_bitcast_fusion = (bf16[64,2048]{1,0:T(8,128)(2,1)}, bf16[64,2048]{1,0:T(8,128)(2,1)S(1)}) fusion(bf16[1,64,4096]{2,1,0:T(8,128)(2,1)} %param.10, s32[]{:T(128)S(6)} %select_n.209, s32[]{:T(128)S(6)} %select_n.184), kind=kLoop, calls=%fused_computation.16 | loop fusion | bytes 1048584 | tf_op jit(solution)/shard_map/dynamic_slice | solution.py:257
  2.6 3.2 %collective-permute-start = (bf16[64,2048]{1,0:T(8,128)(2,1)S(1)}, bf16[64,2048]{1,0:T(8,128)(2,1)S(1)}, u32[]{:S(2)}, u32[]{:S(2)}) collective-permute-start(bf16[64,2048]{1,0:T(8,128)(2,1)S(1)} %get-tuple-element.40), channel_id=1, source_target_pairs={{0,16},{16,0},{32,48},{48,32},{64,80},{80,64},{96,112},{112,96},{1... | collective-permute-start | bytes 786440 | tf_op jit(solution)/shard_map/ppermute | solution.py:48
  5.8 10.6 %convolution_convert_fusion.refs_1_ = bf16[64,2560]{1,0:T(8,128)(2,1)S(1)} fusion(bf16[2560,4096]{1,0:T(8,128)(2,1)} %param.11, bf16[1,64,4096]{2,1,0:T(8,128)(2,1)S(1)} %copy-done.5), kind=kOutput, calls=%fused_computation | convolution fusion | flops 1342341120 | bytes 21823488 | tf_op jit(solution)/shard_map/dot_general | solution.py:56
  16.7 1.6 %shard_map.93 = bf16[8,384,384]{2,1,0:T(8,128)(2,1)} custom-call(bf16[64,2560]{1,0:T(8,128)(2,1)S(1)} %convolution_convert_fusion.1.refs_0_, bf16[64,2560]{1,0:T(8,128)(2,1)S(1)} %convolution_convert_fusion.refs_1_, bf16[128,2560]{1,0:T(8,128)(2,1)S(1)} %bitcast.21, bf16[128,2560]{1,0:T(8,128)(2,1)S(1)} %bitcast.22), custom_call_target="tpu_custom_call" | custom-call | bytes 4325376 | tf_op jit(solution)/shard_map/pallas_call | solution.py:76
  18.4 5.3 %all-to-all-start = ((bf16[8,384,384]{2,1,0:T(8,128)(2,1)}), bf16[8,384,384]{2,1,0:T(8,128)(2,1)S(1)}, u32[]{:S(2)}, u32[]{:S(2)}) async-start(bf16[8,384,384]{2,1,0:T(8,128)(2,1)} %shard_map.93), calls=%async_computation | async-start | bytes 4718592 | tf_op jit(solution)/shard_map/all_to_all | solution.py:28
  23.7 1.1 iota_compare_fusion
  24.8 1.4 %maximum_select_fusion.refs_0_ = bf16[128,2048]{1,0:T(8,128)(2,1)S(1)} fusion(bf16[64,2048]{1,0:T(8,128)(2,1)} %copy-done.7, bf16[64,2048]{1,0:T(8,128)(2,1)} %get-tuple-element.39, pred[]{:T(512)S(6)} %eq.50), kind=kLoop, calls=%fused_computation.13 | loop fusion | flops 2359296 | bytes 1048577 | tf_op jit(solution)/shard_map/jit(_where)/select_n | solution.py:260
  26.2 3.3 %collective-permute-start.1 = (bf16[128,2048]{1,0:T(8,128)(2,1)S(1)}, bf16[128,2048]{1,0:T(8,128)(2,1)}, u32[]{:S(2)}, u32[]{:S(2)}) collective-permute-start(bf16[128,2048]{1,0:T(8,128)(2,1)S(1)} %maximum_select_fusion.refs_0_), channel_id=1, source_target_pairs={{0,96},{16,112},{32,0},{48,16},{64,32},{80,48},{96,64},{112,80},{1... | collective-permute-start | bytes 1572872 | tf_op jit(solution)/shard_map/ppermute | solution.py:44
  29.5 0.9 collective-permute-start.2
  30.3 0.9 collective-permute-start.3
  31.2 32.3 %all-to-all-done.in_ref = bf16[8,384,384]{2,1,0:T(8,128)(2,1)S(1)} async-done(((bf16[8,384,384]{2,1,0:T(8,128)(2,1)}), bf16[8,384,384]{2,1,0:T(8,128)(2,1)S(1)}, u32[]{:S(2)}, u32[]{:S(2)}) %all-to-all-start) | async-done | bytes 2359328 | tf_op jit(solution)/shard_map/all_to_all | solution.py:28
  63.5 4.3 %shard_map.94 = (bf16[3,1024,512]{2,1,0:T(8,128)(2,1)S(1)}, bf16[384,512]{1,0:T(8,128)(2,1)S(1)}) custom-call(bf16[8,384,384]{2,1,0:T(8,128)(2,1)S(1)} %all-to-all-done.in_ref), custom_call_target="tpu_custom_call" | custom-call | flops 1200000000 | bytes 6000000 | tf_op jit(solution)/shard_map/pallas_call | solution.py:220
  67.8 3.7 %collective-permute-start.4 = (bf16[256,512]{1,0:T(8,128)(2,1)S(1)}, bf16[256,512]{1,0:T(8,128)(2,1)S(1)}, u32[]{:S(2)}, u32[]{:S(2)}) collective-permute-start(bf16[256,512]{1,0:T(8,128)(2,1)S(1)} %slice.47), channel_id=1, source_target_pairs={{0,16},{16,0},{32,48},{48,32},{64,80},{80,64},{96,112},{112,96},{1... | collective-permute-start | bytes 786440 | tf_op jit(solution)/shard_map/ppermute | solution.py:48
  71.5 4.3 %shard_map.95 = bf16[8,400,256]{2,1,0:T(8,128)(2,1)S(1)} custom-call(s32[1]{0:T(128)} %bitcast.place_ref, bf16[8,384,384]{2,1,0:T(8,128)(2,1)S(1)} %all-to-all-done.in_ref, bf16[3,1024,512]{2,1,0:T(8,128)(2,1)S(1)} %get-tuple-element.21.prob_ref, bf16[384,512]{1,0:T(8,128)(2,1)S(1)} %get-tuple-element.22.att_ref), custom_call_target="tpu_custom_call" | custom-call | flops 3000000000 | bytes 9000000 | tf_op jit(solution)/shard_map/pallas_call | solution.py:235
  76.4 0.6 copy-done.2
  77.4 5.3 %shard_map.96 = (f32[320,2048]{1,0:T(8,128)S(1)}, bf16[320,2048]{1,0:T(8,128)(2,1)}) custom-call(s32[4]{0:T(128)S(1)} %fusion.41.column_ref, bf16[640,512]{1,0:T(8,128)(2,1)S(1)} %fusion.att_ref, bf16[128,2048]{1,0:T(8,128)(2,1)S(1)} %maximum_select_fusion.refs_0_, bf16[128,2048]{1,0:T(8,128)(2,1)} %collective-permute-done.1.refs_1_, ...), custom_call_target="tpu_custom_call" | custom-call | flops 1400000000 | bytes 8000000 | tf_op jit(solution)/shard_map/pallas_call | solution.py:102
  82.6 1.5 %copy-done.1 = f32[320,2048]{1,0:T(8,128)} copy-done((f32[320,2048]{1,0:T(8,128)}, f32[320,2048]{1,0:T(8,128)S(1)}, u32[]{:S(2)}) %copy-start.1) | copy-done | bytes 2621464
  84.2 3.9 %all-to-all-start.1 = ((bf16[8,400,256]{2,1,0:T(8,128)(2,1)}), bf16[8,400,256]{2,1,0:T(8,128)(2,1)S(1)}, u32[]{:S(2)}, u32[]{:S(2)}) async-start(bf16[8,400,256]{2,1,0:T(8,128)(2,1)} %copy-done.2), calls=%async_computation.1 | async-start | bytes 3276800 | tf_op jit(solution)/shard_map/all_to_all | solution.py:28
  88.0 2.0 %add_convert_fusion.2 = (bf16[80,2048]{1,0:T(8,128)(2,1)S(1)}, bf16[80,2048]{1,0:T(8,128)(2,1)S(1)}, bf16[80,2048]{1,0:T(8,128)(2,1)S(1)}) fusion(f32[320,2048]{1,0:T(8,128)} %copy-done.1, bf16[320,2048]{1,0:T(8,128)(2,1)} %collective-permute-done.5), kind=kLoop, calls=%fused_computation.11 | loop fusion | flops 1474560 | bytes 3932160 | tf_op jit(solution)/shard_map/convert_element_type | solution.py:301
  90.6 2.4 %collective-permute-start.7 = (bf16[80,2048]{1,0:T(8,128)(2,1)S(1)}, bf16[80,2048]{1,0:T(8,128)(2,1)S(1)}, u32[]{:S(2)}, u32[]{:S(2)}) collective-permute-start(bf16[80,2048]{1,0:T(8,128)(2,1)S(1)} %get-tuple-element.38), channel_id=1, source_target_pairs={{0,8},{1,9},{2,10},{3,11},{4,12},{5,13},{6,14},{7,15},{8,0},{9,1},... | collective-permute-start | bytes 983048 | tf_op jit(solution)/shard_map/ppermute | solution.py:32
  93.0 7.6 %collective-permute-done.6 = bf16[80,2048]{1,0:T(8,128)(2,1)S(1)} collective-permute-done((bf16[80,2048]{1,0:T(8,128)(2,1)S(1)}, bf16[80,2048]{1,0:T(8,128)(2,1)S(1)}, u32[]{:S(2)}, u32[]{:S(2)}) %collective-permute-start.6) | collective-permute-done | bytes 327712 | tf_op jit(solution)/shard_map/ppermute | solution.py:32
  100.7 2.1 %collective-permute-done.7 = bf16[80,2048]{1,0:T(8,128)(2,1)S(1)} collective-permute-done((bf16[80,2048]{1,0:T(8,128)(2,1)S(1)}, bf16[80,2048]{1,0:T(8,128)(2,1)S(1)}, u32[]{:S(2)}, u32[]{:S(2)}) %collective-permute-start.7) | collective-permute-done | bytes 327712 | tf_op jit(solution)/shard_map/ppermute | solution.py:32
  102.8 6.0 %collective-permute-done.8 = bf16[80,2048]{1,0:T(8,128)(2,1)S(1)} collective-permute-done((bf16[80,2048]{1,0:T(8,128)(2,1)S(1)}, bf16[80,2048]{1,0:T(8,128)(2,1)S(1)}, u32[]{:S(2)}, u32[]{:S(2)}) %collective-permute-start.8) | collective-permute-done | bytes 327712 | tf_op jit(solution)/shard_map/ppermute | solution.py:32
  108.7 1.4 %convert_add_fusion = f32[80,2048]{1,0:T(8,128)S(1)} fusion(bf16[80,2048]{1,0:T(8,128)(2,1)S(1)} %collective-permute-done.8, bf16[80,2048]{1,0:T(8,128)(2,1)S(1)} %collective-permute-done.7, bf16[80,2048]{1,0:T(8,128)(2,1)S(1)} %collective-permute-done.6, f32[320,2048]{1,0:T(8,128)} %copy-done.1, bf16[320,2048]{1,0:T(8,128)(2,1)} %collective-permute-done.5), kind=kLoop, calls=%fused_computation.8 | loop fusion | flops 1310720 | bytes 2621440 | tf_op jit(solution)/shard_map/add | solution.py:301
  110.1 2.2 %all-to-all-done.1.back_ref = bf16[8,400,256]{2,1,0:T(8,128)(2,1)S(1)} async-done(((bf16[8,400,256]{2,1,0:T(8,128)(2,1)}), bf16[8,400,256]{2,1,0:T(8,128)(2,1)S(1)}, u32[]{:S(2)}, u32[]{:S(2)}) %all-to-all-start.1) | async-done | bytes 1638432 | tf_op jit(solution)/shard_map/all_to_all | solution.py:28
  112.4 1.4 %collective-permute-start.9 = (bf16[20,2048]{1,0:T(8,128)(2,1)S(1)}, bf16[20,2048]{1,0:T(8,128)(2,1)S(1)}, u32[]{:S(2)}, u32[]{:S(2)}) collective-permute-start(bf16[20,2048]{1,0:T(8,128)(2,1)S(1)} %get-tuple-element.41), channel_id=1, source_target_pairs={{0,2},{1,3},{2,0},{3,1},{4,6},{5,7},{6,4},{7,5},{8,10},{9,11},{10,... | collective-permute-start | bytes 245768 | tf_op jit(solution)/shard_map/ppermute | solution.py:40
  113.9 1.7 %collective-permute-start.10 = (bf16[20,2048]{1,0:T(8,128)(2,1)S(1)}, bf16[20,2048]{1,0:T(8,128)(2,1)S(1)}, u32[]{:S(2)}, u32[]{:S(2)}) collective-permute-start(bf16[20,2048]{1,0:T(8,128)(2,1)S(1)} %get-tuple-element.43), channel_id=1, source_target_pairs={{0,16},{1,17},{2,18},{3,19},{4,20},{5,21},{6,22},{7,23},{8,24},{9,... | collective-permute-start | bytes 245768 | tf_op jit(solution)/shard_map/ppermute | solution.py:40
  115.6 1.7 %collective-permute-start.11 = (bf16[20,2048]{1,0:T(8,128)(2,1)S(1)}, bf16[20,2048]{1,0:T(8,128)(2,1)S(1)}, u32[]{:S(2)}, u32[]{:S(2)}) collective-permute-start(bf16[20,2048]{1,0:T(8,128)(2,1)S(1)} %get-tuple-element.42), channel_id=1, source_target_pairs={{0,18},{1,19},{2,16},{3,17},{4,22},{5,23},{6,20},{7,21},{8,26},{9,... | collective-permute-start | bytes 245768 | tf_op jit(solution)/shard_map/ppermute | solution.py:40
  117.3 1.6 %shard_map.97 = (bf16[128,2560]{1,0:T(8,128)(2,1)}, bf16[128,2560]{1,0:T(8,128)(2,1)}, bf16[128,2560]{1,0:T(8,128)(2,1)}) custom-call(bf16[8,400,256]{2,1,0:T(8,128)(2,1)S(1)} %all-to-all-done.1.back_ref, bf16[64,128]{1,0:T(8,128)(2,1)S(1)} %fusion.6.selector_ref), custom_call_target="tpu_custom_call" | custom-call | flops 50000000 | bytes 4000000 | tf_op jit(solution)/shard_map/pallas_call | solution.py:146
  118.9 1.4 %collective-permute-done.10 = bf16[20,2048]{1,0:T(8,128)(2,1)S(1)} collective-permute-done((bf16[20,2048]{1,0:T(8,128)(2,1)S(1)}, bf16[20,2048]{1,0:T(8,128)(2,1)S(1)}, u32[]{:S(2)}, u32[]{:S(2)}) %collective-permute-start.10) | collective-permute-done | bytes 81952 | tf_op jit(solution)/shard_map/ppermute | solution.py:40
  120.4 1.9 %collective-permute-done.11 = bf16[20,2048]{1,0:T(8,128)(2,1)S(1)} collective-permute-done((bf16[20,2048]{1,0:T(8,128)(2,1)S(1)}, bf16[20,2048]{1,0:T(8,128)(2,1)S(1)}, u32[]{:S(2)}, u32[]{:S(2)}) %collective-permute-start.11) | collective-permute-done | bytes 81952 | tf_op jit(solution)/shard_map/ppermute | solution.py:40
  122.3 0.8 maximum_select_fusion.1
  (38 shorter events, 2.0 us)
Async XLA Ops:
  0.6 15.8 %copy-start = (bf16[1,128,2560]{2,1,0:T(8,128)(2,1)S(1)}, bf16[1,128,2560]{2,1,0:T(8,128)(2,1)}, u32[]{:S(2)}) copy-start(bf16[1,128,2560]{2,1,0:T(8,128)(2,1)} %param.6) | copy-start | bytes 1966084
  0.6 5.1 %copy-start.5 = (bf16[1,64,4096]{2,1,0:T(8,128)(2,1)S(1)}, bf16[1,64,4096]{2,1,0:T(8,128)(2,1)}, u32[]{:S(2)}) copy-start(bf16[1,64,4096]{2,1,0:T(8,128)(2,1)} %param.10) | copy-start | bytes 1572868
  2.5 13.8 %copy-start.8 = (s32[1,64]{1,0:T(1,128)S(1)}, s32[1,64]{1,0:T(1,128)}, u32[]{:S(2)}) copy-start(s32[1,64]{1,0:T(1,128)} %param.9) | copy-start | bytes 772
  2.5 14.2 %copy-start.3 = (bf16[1,128,2560]{2,1,0:T(8,128)(2,1)S(1)}, bf16[1,128,2560]{2,1,0:T(8,128)(2,1)}, u32[]{:S(2)}) copy-start(bf16[1,128,2560]{2,1,0:T(8,128)(2,1)} %param.7) | copy-start | bytes 1966084
  2.6 14.2 %copy-start.4 = (bf16[1,128,2560]{2,1,0:T(8,128)(2,1)S(1)}, bf16[1,128,2560]{2,1,0:T(8,128)(2,1)}, u32[]{:S(2)}) copy-start(bf16[1,128,2560]{2,1,0:T(8,128)(2,1)} %param.8) | copy-start | bytes 1966084
  2.6 13.8 %collective-permute-start = (bf16[64,2048]{1,0:T(8,128)(2,1)S(1)}, bf16[64,2048]{1,0:T(8,128)(2,1)S(1)}, u32[]{:S(2)}, u32[]{:S(2)}) collective-permute-start(bf16[64,2048]{1,0:T(8,128)(2,1)S(1)} %get-tuple-element.40), channel_id=1, source_target_pairs={{0,16},{16,0},{32,48},{48,32},{64,80},{80,64},{96,112},{112,96},{1... | collective-permute-start | bytes 786440 | tf_op jit(solution)/shard_map/ppermute | solution.py:48
  16.4 2.0 %copy-start.7 = (bf16[64,2048]{1,0:T(8,128)(2,1)}, bf16[64,2048]{1,0:T(8,128)(2,1)S(1)}, u32[]{:S(2)}) copy-start(bf16[64,2048]{1,0:T(8,128)(2,1)S(1)} %collective-permute-done) | copy-start | bytes 786436
  18.4 45.1 %all-to-all-start = ((bf16[8,384,384]{2,1,0:T(8,128)(2,1)}), bf16[8,384,384]{2,1,0:T(8,128)(2,1)S(1)}, u32[]{:S(2)}, u32[]{:S(2)}) async-start(bf16[8,384,384]{2,1,0:T(8,128)(2,1)} %shard_map.93), calls=%async_computation | async-start | bytes 4718592 | tf_op jit(solution)/shard_map/all_to_all | solution.py:28
  26.2 50.2 %collective-permute-start.1 = (bf16[128,2048]{1,0:T(8,128)(2,1)S(1)}, bf16[128,2048]{1,0:T(8,128)(2,1)}, u32[]{:S(2)}, u32[]{:S(2)}) collective-permute-start(bf16[128,2048]{1,0:T(8,128)(2,1)S(1)} %maximum_select_fusion.refs_0_), channel_id=1, source_target_pairs={{0,96},{16,112},{32,0},{48,16},{64,32},{80,48},{96,64},{112,80},{1... | collective-permute-start | bytes 1572872 | tf_op jit(solution)/shard_map/ppermute | solution.py:44
  29.5 46.9 %collective-permute-start.2 = (bf16[128,2048]{1,0:T(8,128)(2,1)S(1)}, bf16[128,2048]{1,0:T(8,128)(2,1)}, u32[]{:S(2)}, u32[]{:S(2)}) collective-permute-start(bf16[128,2048]{1,0:T(8,128)(2,1)S(1)} %maximum_select_fusion.refs_0_), channel_id=1, source_target_pairs={{0,64},{16,80},{32,96},{48,112},{64,0},{80,16},{96,32},{112,48},{1... | collective-permute-start | bytes 1572872 | tf_op jit(solution)/shard_map/ppermute | solution.py:44
  30.3 46.0 %collective-permute-start.3 = (bf16[128,2048]{1,0:T(8,128)(2,1)S(1)}, bf16[128,2048]{1,0:T(8,128)(2,1)}, u32[]{:S(2)}, u32[]{:S(2)}) collective-permute-start(bf16[128,2048]{1,0:T(8,128)(2,1)S(1)} %maximum_select_fusion.refs_0_), channel_id=1, source_target_pairs={{0,32},{16,48},{32,64},{48,80},{64,96},{80,112},{96,0},{112,16},{1... | collective-permute-start | bytes 1572872 | tf_op jit(solution)/shard_map/ppermute | solution.py:44
  67.8 8.6 %collective-permute-start.4 = (bf16[256,512]{1,0:T(8,128)(2,1)S(1)}, bf16[256,512]{1,0:T(8,128)(2,1)S(1)}, u32[]{:S(2)}, u32[]{:S(2)}) collective-permute-start(bf16[256,512]{1,0:T(8,128)(2,1)S(1)} %slice.47), channel_id=1, source_target_pairs={{0,16},{16,0},{32,48},{48,32},{64,80},{80,64},{96,112},{112,96},{1... | collective-permute-start | bytes 786440 | tf_op jit(solution)/shard_map/ppermute | solution.py:48
  71.5 4.3 %copy-start.6 = (pred[640,640]{1,0:T(32,128)(4,1)S(1)}, pred[640,640]{1,0:T(32,128)(4,1)}, u32[]{:S(2)}) copy-start(pred[640,640]{1,0:T(32,128)(4,1)} %iota_compare_fusion) | copy-start | bytes 1228804
  75.8 1.2 copy-start.2
  82.6 1.5 %copy-start.1 = (f32[320,2048]{1,0:T(8,128)}, f32[320,2048]{1,0:T(8,128)S(1)}, u32[]{:S(2)}) copy-start(f32[320,2048]{1,0:T(8,128)S(1)} %get-tuple-element.29) | copy-start | bytes 7864324
  84.2 3.9 %collective-permute-start.5 = (bf16[320,2048]{1,0:T(8,128)(2,1)}, bf16[320,2048]{1,0:T(8,128)(2,1)}, u32[]{:S(2)}, u32[]{:S(2)}) collective-permute-start(bf16[320,2048]{1,0:T(8,128)(2,1)} %get-tuple-element.30), channel_id=1, source_target_pairs={{0,1},{1,0},{2,3},{3,2},{4,5},{5,4},{6,7},{7,6},{8,9},{9,8},{10,11... | collective-permute-start | bytes 3932168 | tf_op jit(solution)/shard_map/ppermute | solution.py:52
  84.2 28.1 %all-to-all-start.1 = ((bf16[8,400,256]{2,1,0:T(8,128)(2,1)}), bf16[8,400,256]{2,1,0:T(8,128)(2,1)S(1)}, u32[]{:S(2)}, u32[]{:S(2)}) async-start(bf16[8,400,256]{2,1,0:T(8,128)(2,1)} %copy-done.2), calls=%async_computation.1 | async-start | bytes 3276800 | tf_op jit(solution)/shard_map/all_to_all | solution.py:28
  90.1 10.6 %collective-permute-start.6 = (bf16[80,2048]{1,0:T(8,128)(2,1)S(1)}, bf16[80,2048]{1,0:T(8,128)(2,1)S(1)}, u32[]{:S(2)}, u32[]{:S(2)}) collective-permute-start(bf16[80,2048]{1,0:T(8,128)(2,1)S(1)} %get-tuple-element.36), channel_id=1, source_target_pairs={{0,4},{1,5},{2,6},{3,7},{4,8},{5,9},{6,10},{7,11},{8,12},{9,13},{1... | collective-permute-start | bytes 983048 | tf_op jit(solution)/shard_map/ppermute | solution.py:32
  90.6 12.1 %collective-permute-start.7 = (bf16[80,2048]{1,0:T(8,128)(2,1)S(1)}, bf16[80,2048]{1,0:T(8,128)(2,1)S(1)}, u32[]{:S(2)}, u32[]{:S(2)}) collective-permute-start(bf16[80,2048]{1,0:T(8,128)(2,1)S(1)} %get-tuple-element.38), channel_id=1, source_target_pairs={{0,8},{1,9},{2,10},{3,11},{4,12},{5,13},{6,14},{7,15},{8,0},{9,1},... | collective-permute-start | bytes 983048 | tf_op jit(solution)/shard_map/ppermute | solution.py:32
  93.0 15.7 %collective-permute-start.8 = (bf16[80,2048]{1,0:T(8,128)(2,1)S(1)}, bf16[80,2048]{1,0:T(8,128)(2,1)S(1)}, u32[]{:S(2)}, u32[]{:S(2)}) collective-permute-start(bf16[80,2048]{1,0:T(8,128)(2,1)S(1)} %get-tuple-element.37), channel_id=1, source_target_pairs={{0,12},{1,13},{2,14},{3,15},{4,0},{5,1},{6,2},{7,3},{8,4},{9,5},{1... | collective-permute-start | bytes 983048 | tf_op jit(solution)/shard_map/ppermute | solution.py:32
  112.4 6.5 %collective-permute-start.9 = (bf16[20,2048]{1,0:T(8,128)(2,1)S(1)}, bf16[20,2048]{1,0:T(8,128)(2,1)S(1)}, u32[]{:S(2)}, u32[]{:S(2)}) collective-permute-start(bf16[20,2048]{1,0:T(8,128)(2,1)S(1)} %get-tuple-element.41), channel_id=1, source_target_pairs={{0,2},{1,3},{2,0},{3,1},{4,6},{5,7},{6,4},{7,5},{8,10},{9,11},{10,... | collective-permute-start | bytes 245768 | tf_op jit(solution)/shard_map/ppermute | solution.py:40
  113.9 6.5 %collective-permute-start.10 = (bf16[20,2048]{1,0:T(8,128)(2,1)S(1)}, bf16[20,2048]{1,0:T(8,128)(2,1)S(1)}, u32[]{:S(2)}, u32[]{:S(2)}) collective-permute-start(bf16[20,2048]{1,0:T(8,128)(2,1)S(1)} %get-tuple-element.43), channel_id=1, source_target_pairs={{0,16},{1,17},{2,18},{3,19},{4,20},{5,21},{6,22},{7,23},{8,24},{9,... | collective-permute-start | bytes 245768 | tf_op jit(solution)/shard_map/ppermute | solution.py:40
  115.6 6.7 %collective-permute-start.11 = (bf16[20,2048]{1,0:T(8,128)(2,1)S(1)}, bf16[20,2048]{1,0:T(8,128)(2,1)S(1)}, u32[]{:S(2)}, u32[]{:S(2)}) collective-permute-start(bf16[20,2048]{1,0:T(8,128)(2,1)S(1)} %get-tuple-element.42), channel_id=1, source_target_pairs={{0,18},{1,19},{2,16},{3,17},{4,22},{5,23},{6,20},{7,21},{8,26},{9,... | collective-permute-start | bytes 245768 | tf_op jit(solution)/shard_map/ppermute | solution.py:40

commit v3 on v2

--- a/solution.py
+++ b/solution.py
@@ -20,7 +20,6 @@
 KEYS = 8 * TOK
 ROWS_OUT = MSK + 2 * TOK
 ROWS_BACK = ROWS_OUT + 80
-ROWS_IN = 2 * MSK + 2 * TOK
 PARAMS = pltpu.CompilerParams(vmem_limit_bytes=40 * 2**20)
 
 
@@ -60,14 +59,14 @@
     return pl.CostEstimate(flops=int(flops), bytes_accessed=int(moved), transcendentals=int(exps))
 
 
-def slabs_of(query, grad, key, value):
+def slabs_of(query, key, value):
     def kernel(*refs):
-        out_ref = refs[4]
+        out_ref = refs[3]
         for j in range(8):
             pair = (j // 2) * 640 + (j % 2) * 384
             shared = (j // 2) * 640 + 256
             row = 0
-            for ref in refs[:4]:
+            for ref in refs[:3]:
                 at = pl.ds(row, ref.shape[0])
                 out_ref[j, at, 0:256] = ref[:, pair : pair + 256]
                 out_ref[j, at, 256:SLAB] = ref[:, shared : shared + HEAD_DIM]
@@ -75,46 +74,52 @@
 
     return pl.pallas_call(
         kernel,
-        out_shape=jax.ShapeDtypeStruct((8, ROWS_IN, SLAB), BF),
-        compiler_params=PARAMS,
-        cost_estimate=cost(0, ROWS_IN * WIDTH * 4.4),
-    )(query, grad, key, value)
-
-
-def outer(columns, att_rows, cot_parts):
+        out_shape=jax.ShapeDtypeStruct((8, ROWS_OUT, SLAB), BF),
+        compiler_params=PARAMS,
+        cost_estimate=cost(0, ROWS_OUT * WIDTH * 4.4),
+    )(query, key, value)
+
+
+def pack_grads(starts, grad):
+    def kernel(start_ref, grad_ref, *outs):
+        for i, out_ref in enumerate(outs):
+            out_ref[...] = grad_ref[:, pl.ds(pl.multiple_of(start_ref[i], HEAD_DIM), 640)]
+
+    vmem = pl.BlockSpec(memory_space=pltpu.VMEM)
+    return pl.pallas_call(
+        kernel,
+        in_specs=[pl.BlockSpec(memory_space=pltpu.SMEM), vmem],
+        out_shape=[jax.ShapeDtypeStruct((MSK, 640), BF)] * 4,
+        compiler_params=PARAMS,
+        cost_estimate=cost(0, MSK * WIDTH * 4),
+    )(starts, grad)
+
+
+def outer(att_rows, cot_parts):
     width = cot_parts[0].shape[1]
     rows = att_rows.shape[0] // 2
-    tile = 512
-
-    def kernel(column_ref, att_ref, *refs):
-        att = jnp.concatenate(
-            [
-                att_ref[:, pl.ds(pl.multiple_of(column_ref[i], 2 * MSK), 2 * MSK)]
-                for i in range(4)
-            ],
-            axis=1,
-        )
+    tile = 1024
+
+    def kernel(att_ref, *refs):
+        att = att_ref[...]
         cots = jnp.concatenate([r[...] for r in refs[:4]], axis=0)
-        refs[4][...] = dot(att[:rows], cots, 1, 0)
+        refs[4][...] = dot(att[:rows], cots, 1, 0).astype(BF)
         refs[5][...] = dot(att[rows:], cots, 1, 0).astype(BF)
 
-    out = pl.BlockSpec((rows, tile), lambda i, *_: (0, i))
+    out = pl.BlockSpec((rows, tile), lambda i: (0, i))
     return pl.pallas_call(
         kernel,
-        grid_spec=pltpu.PrefetchScalarGridSpec(
-            num_scalar_prefetch=1,
-            grid=(width // tile,),
-            in_specs=[pl.BlockSpec((2 * rows, QUERIES), lambda i, *_: (0, 0))]
-            + [pl.BlockSpec((2 * MSK, tile), lambda i, *_: (0, i))] * 4,
-            out_specs=[out, out],
-        ),
+        grid=(width // tile,),
+        in_specs=[pl.BlockSpec((2 * rows, QUERIES), lambda i: (0, 0))]
+        + [pl.BlockSpec((2 * MSK, tile), lambda i: (0, i))] * 4,
+        out_specs=[out, out],
         out_shape=[
-            jax.ShapeDtypeStruct((rows, width), F32),
             jax.ShapeDtypeStruct((rows, width), BF),
+            pltpu.HBM((rows, width), BF),
         ],
         compiler_params=PARAMS,
         cost_estimate=cost(1.4e9, 8e6),
-    )(columns, att_rows, *cot_parts)
+    )(att_rows, *cot_parts)
 
 
 def finish(back, selector):
@@ -147,13 +152,13 @@
         kernel,
         out_shape=[jax.ShapeDtypeStruct((TOK, WIDTH), BF)] * 3,
         compiler_params=PARAMS,
-        cost_estimate=cost(5e7, 4e6),
+        cost_estimate=cost(2e10, 4e6),
     )(back, selector)
 
 
 def forward_kernel(in_ref, prob_ref, att_ref):
-    key = in_ref[:, 2 * MSK : 2 * MSK + TOK].reshape(KEYS, HEAD_DIM)
-    value = in_ref[:, 2 * MSK + TOK :].reshape(KEYS, HEAD_DIM)
+    key = in_ref[:, MSK : MSK + TOK].reshape(KEYS, HEAD_DIM)
+    value = in_ref[:, MSK + TOK :].reshape(KEYS, HEAD_DIM)
     query = in_ref[:, 0:MSK].reshape(QUERIES, HEAD_DIM)
     scores = dot(key, query, 1, 1) * SCALE
     top = jnp.max(scores, axis=0, keepdims=True)
@@ -164,11 +169,17 @@
     att_ref[...] = dot(value.T, probs, 1, 0).astype(BF)
 
 
-def backward_kernel(place_ref, in_ref, prob_ref, att_ref, out_ref):
-    key = in_ref[:, 2 * MSK : 2 * MSK + TOK].reshape(KEYS, HEAD_DIM)
-    value = in_ref[:, 2 * MSK + TOK :].reshape(KEYS, HEAD_DIM)
+def backward_kernel(place_ref, in_ref, *refs):
+    own_refs, (got_ref, prob_ref, att_ref, out_ref, grad_ref) = refs[:4], refs[4:]
+    key = in_ref[:, MSK : MSK + TOK].reshape(KEYS, HEAD_DIM)
+    value = in_ref[:, MSK + TOK :].reshape(KEYS, HEAD_DIM)
     query = in_ref[:, 0:MSK].reshape(QUERIES, HEAD_DIM)
-    grad = in_ref[:, MSK : 2 * MSK].reshape(QUERIES, HEAD_DIM)
+    for i in range(4):
+        mine = pl.multiple_of(place_ref[4 + i] + place_ref[0] * MSK, MSK)
+        other = pl.multiple_of(place_ref[4 + i] + (1 - place_ref[0]) * MSK, MSK)
+        grad_ref[pl.ds(mine, MSK)] = own_refs[i][...]
+        grad_ref[pl.ds(other, MSK)] = got_ref[i * MSK : (i + 1) * MSK]
+    grad = grad_ref[...]
     delta = jnp.sum(grad.T.astype(F32) * att_ref[...].astype(F32), axis=0, keepdims=True)
     probs = prob_ref[0]
     prob_grad = dot(value, grad, 1, 1)
@@ -220,30 +231,37 @@
     return pl.pallas_call(
         forward_kernel,
         grid=(HEADS_DEV,),
-        in_specs=[head_block(ROWS_IN)],
+        in_specs=[head_block(ROWS_OUT)],
         out_specs=[PROB_BLOCK, ATT_BLOCK],
         out_shape=[
             jax.ShapeDtypeStruct((HEADS_DEV, KEYS, QUERIES), BF),
             jax.ShapeDtypeStruct((SLAB, QUERIES), BF),
         ],
         compiler_params=PARAMS,
-        cost_estimate=cost(1.2e9, 6e6, 1.6e6),
+        cost_estimate=cost(1e6, 1e5),
     )(sent)
 
 
-def backward(place, sent, probs, att):
+def backward(place, sent, own, got, probs, att):
     return pl.pallas_call(
         backward_kernel,
         grid_spec=pltpu.PrefetchScalarGridSpec(
             num_scalar_prefetch=1,
             grid=(HEADS_DEV,),
-            in_specs=[head_block(ROWS_IN), PROB_BLOCK, ATT_BLOCK],
+            in_specs=[
+                head_block(ROWS_OUT),
+                *[pl.BlockSpec((MSK, HEAD_DIM), lambda h, place: (0, place[1 + h]))] * 4,
+                pl.BlockSpec((4 * MSK, HEAD_DIM), lambda h, *_: (0, h)),
+                PROB_BLOCK,
+                ATT_BLOCK,
+            ],
             out_specs=pl.BlockSpec((8, ROWS_BACK, 2 * HEAD_DIM), lambda h, *_: (0, 0, 0)),
+            scratch_shapes=[pltpu.VMEM((QUERIES, HEAD_DIM), BF)],
         ),
         out_shape=jax.ShapeDtypeStruct((8, ROWS_BACK, 2 * HEAD_DIM), BF),
         compiler_params=PARAMS,
-        cost_estimate=cost(3e9, 9e6),
-    )(place, sent, probs, att)
+        cost_estimate=cost(1e6, 1e5),
+    )(place, sent, *own, got, probs, att)
 
 
 def shards(query_states, key_states, value_states, mask_index, cotangent, out_weight):
@@ -256,7 +274,6 @@
     half = cot.shape[1] // 2
     cot_kept = lax.dynamic_slice_in_dim(cot, y * half, half, 1)
     cot_got = swap_y(lax.dynamic_slice_in_dim(cot, (1 - y) * half, half, 1))
-    steps, cot_got = lax.optimization_barrier((steps, cot_got))
     cot_pair = jnp.where(
         y == 0,
         jnp.concatenate([cot_kept, cot_got], axis=0),
@@ -265,14 +282,24 @@
 
     selector = (steps[:, None] == jnp.arange(TOK, dtype=jnp.int32)[None, :]).astype(BF)
     masked_query = dot(selector, query_states[0], 1, 0).astype(BF)
+    packed = slabs_of(masked_query, key_states[0], value_states[0])
+    heads_in = exchange(packed)
     masked_grad = dot(cot, out_weight, 1, 1).astype(BF)
-    heads_in = exchange(
-        slabs_of(masked_query, masked_grad, key_states[0], value_states[0])
-    )
+    ring = (z + jnp.arange(4, dtype=jnp.int32)) % 4
+    columns = ring * (2 * MSK)
+    grads_out = pack_grads(ring * 640, masked_grad)
+    own_grad = [grads_out[0]] + [move_z(grads_out[4 - dz], 4 - dz) for dz in (1, 2, 3)]
+    own_all = jnp.concatenate(own_grad, axis=0)
+    got_grad = swap_y(
+        jnp.concatenate(
+            [lax.dynamic_slice_in_dim(own_all, (1 - y) * 384, 256, 1), own_all[:, 256:384]], axis=1
+        )
+    )
+    place = jnp.concatenate([jnp.stack([y, 3 * y, 3 * y + 1, 0 * y + 2]), columns]).astype(jnp.int32)
     cot_parts = [cot_pair] + [move_z(cot_pair, dz) for dz in (3, 2, 1)]
     probs, att = forward(heads_in)
     att_got = swap_y(att[:256])
-    outs = backward(y[None].astype(jnp.int32), heads_in, probs, att)
+    outs = backward(place, heads_in, own_grad, got_grad, probs, att)
 
     back = exchange(outs)
     cot_parts, att_got, _ = lax.optimization_barrier((cot_parts, att_got, outs))
@@ -290,16 +317,18 @@
     index = jnp.where(wanted < 256, low_place, jnp.where(wanted < 384, wanted, high_place))
     pick = (index[:, None] == r[None, :]).astype(BF)
     att_rows = (dot(pick[:, :SLAB], att, 1, 0) + dot(pick[:, SLAB:], att_got, 1, 0)).astype(BF)
-    columns = (z + jnp.arange(4, dtype=jnp.int32)) % 4 * (2 * MSK)
-    kept, sent = outer(columns, att_rows, cot_parts)
+    att_rows = lax.dynamic_slice_in_dim(
+        jnp.concatenate([att_rows, att_rows], axis=1), z * 2 * MSK, QUERIES, 1
+    )
+    kept, sent = outer(att_rows, cot_parts)
     sent = swap_core(sent)
     chunks = [
-        kept[i * 80 : (i + 1) * 80] + sent[i * 80 : (i + 1) * 80].astype(F32) for i in range(4)
+        kept[i * 80 : (i + 1) * 80].astype(F32) + sent[i * 80 : (i + 1) * 80].astype(F32) for i in range(4)
     ]
     acc = chunks[0]
     for dx in (1, 2, 3):
         acc = acc + move_x(chunks[dx].astype(BF), dx).astype(F32)
-    back, acc = lax.optimization_barrier((back, acc))
+    back, _ = lax.optimization_barrier((back, acc))
     quarter = acc.astype(BF)
     own_half = acc[:20] + move_y(quarter[40:60], 1, 0).astype(F32)
     other_half = move_y(quarter[20:40], 0, 1).astype(F32) + move_y(quarter[60:], 1, 1).astype(F32)

time: 124 us -> 116 us (0.935)
  waiting for transfers between devices: 53.5 us -> 36.8 us
  starting transfers between devices: 28.9 us -> 35.5 us
  other arithmetic: 6.81 us -> 9.05 us
  local copies, waits for them, and re-layouts: 4.14 us -> 5.82 us
    all_to_all x2, waiting for transfers between devices: 34.5 us -> 0.01 us  [exchange(): return lax.all_to_all(a, 'blk', 0, 0, tiled=True)]
    ppermute x3 -> x6, waiting for transfers between devices: 0.01 us -> 14.1 us  [move_z(): return lax.ppermute(a, 'blk', [(i, (i + 2 * dz) % 8) for i in range(8)])]
    ppermute x3 -> x6, starting transfers between devices: 5.02 us -> 9.33 us  [move_z(): return lax.ppermute(a, 'blk', [(i, (i + 2 * dz) % 8) for i in range(8)])]
    ppermute x2 -> x3, waiting for transfers between devices: 0.01 us -> 3.02 us  [swap_y(): return lax.ppermute(a, 'blk', [(i, i ^ 1) for i in range(8)])]
    all_to_all x2, starting transfers between devices: 9.18 us -> 11.7 us  [exchange(): return lax.all_to_all(a, 'blk', 0, 0, tiled=True)]
    pallas_call x2 -> x3, Pallas kernels: 6.91 us -> 4.57 us  [the longest x1 3.83 us: outer(): pl.pallas_call(kernel, grid=(width // tile,), in_specs=[pl.BlockSpec((2 *...]
    unnamed x18 -> x19, local copies, waits for them, and re-layouts: 2.2 us -> 3.85 us
    pallas_call x1, Pallas kernels: 4.28 us -> 5.66 us  [backward(): pl.pallas_call(backward_kernel, grid_spec=pltpu.PrefetchScalarGridSpec(nu...]
  transfers between devices with their start and end apart: 14 -> 18, of which waited for: 7 -> 10; matrix products, arithmetic and copies ran while one was open for 14% -> 18% of each run, Pallas kernels for 8% -> 10%
where the time goes in v3:
time: 116 us
  waiting for transfers between devices  36.8 us (32%)
  starting transfers between devices  35.5 us (31%)
  Pallas kernels  16.1 us (14%)
  matrix products  11.8 us (10%)
  other arithmetic  9.05 us (8%)
  local copies, waits for them, and re-layouts  5.82 us (5%)
    ppermute x3, waiting for transfers between devices, move_x(): return lax.ppermute(a, 'dp', [(i, (i + 4 * dx) % 16) for i in range(16)])  15.9 us
    ppermute x6, waiting for transfers between devices, move_z(): return lax.ppermute(a, 'blk', [(i, (i + 2 * dz) % 8) for i in range(8)])  14.1 us
    dot_general x4, matrix products, dot(): lax.dot_general(a, b, (((ca,), (cb,)), ((), ())), preferred_element_type=...  11.8 us
    all_to_all x2, starting transfers between devices, exchange(): return lax.all_to_all(a, 'blk', 0, 0, tiled=True)  11.7 us
    ppermute x6, starting transfers between devices, move_z(): return lax.ppermute(a, 'blk', [(i, (i + 2 * dz) % 8) for i in range(8)])  9.33 us
    ppermute x3, starting transfers between devices, swap_y(): return lax.ppermute(a, 'blk', [(i, i ^ 1) for i in range(8)])  6.57 us
    pallas_call x1, Pallas kernels, backward(): pl.pallas_call(backward_kernel, grid_spec=pltpu.PrefetchScalarGridSpec(nu...  5.66 us
    ppermute x3, starting transfers between devices, move_y(): return lax.ppermute(a, ('blk', 'dp'), pairs)  4.78 us
  transfers between devices with their start and end apart: 18, of which 10 were waited for; matrix products, arithmetic and copies ran while one was open for 18% of the time, Pallas kernels for 10%

profile of v3, /device:TPU:6, one launch (start us, length us, event | category | flops | bytes accessed | tf_op | source)
XLA Modules:
  0.0 115.9 jit_solution(7392716579073818778)
XLA Ops:
  2.1 1.1 copy-done.5
  3.3 1.3 %copy-done.1 = bf16[8,320,384]{2,1,0:T(8,128)(2,1)} copy-done((bf16[8,320,384]{2,1,0:T(8,128)(2,1)}, bf16[8,320,384]{2,1,0:T(8,128)(2,1)S(1)}, u32[]{:S(2)}) %copy-start.1) | copy-done | bytes 1966104
  4.6 8.1 %all-to-all-start = ((bf16[8,320,384]{2,1,0:T(8,128)(2,1)}), bf16[8,320,384]{2,1,0:T(8,128)(2,1)S(1)}, u32[]{:S(2)}, u32[]{:S(2)}) async-start(bf16[8,320,384]{2,1,0:T(8,128)(2,1)} %copy-done.1), calls=%async_computation | async-start | bytes 3932160 | tf_op jit(solution)/shard_map/all_to_all | solution.py:27
  12.7 10.6 %convolution_convert_fusion.grad_ref = bf16[64,2560]{1,0:T(8,128)(2,1)S(1)} fusion(bf16[2560,4096]{1,0:T(8,128)(2,1)} %param.11, bf16[1,64,4096]{2,1,0:T(8,128)(2,1)S(1)} %copy-done.6), kind=kOutput, calls=%fused_computation | convolution fusion | flops 1342341120 | bytes 21823488 | tf_op jit(solution)/shard_map/dot_general | solution.py:55
  23.9 3.3 %collective-permute-start = (bf16[64,640]{1,0:T(8,128)(2,1)S(1)}, bf16[64,640]{1,0:T(8,128)(2,1)S(1)}, u32[]{:S(2)}, u32[]{:S(2)}) collective-permute-start(bf16[64,640]{1,0:T(8,128)(2,1)S(1)} %get-tuple-element.22), channel_id=1, source_target_pairs={{0,96},{16,112},{32,0},{48,16},{64,32},{80,48},{96,64},{112,80},{1... | collective-permute-start | bytes 245768 | tf_op jit(solution)/shard_map/ppermute | solution.py:43
  28.9 1.8 %dynamic-slice_bitcast_fusion.1 = (bf16[64,2048]{1,0:T(8,128)(2,1)}, bf16[64,2048]{1,0:T(8,128)(2,1)S(1)}) fusion(bf16[1,64,4096]{2,1,0:T(8,128)(2,1)} %param.10, s32[]{:T(128)S(6)} %select_n.215, s32[]{:T(128)S(6)} %select_n.216), kind=kLoop, calls=%fused_computation.20 | loop fusion | bytes 1048584 | tf_op jit(solution)/shard_map/dynamic_slice | solution.py:275
  30.7 3.0 %collective-permute-start.4 = (bf16[64,2048]{1,0:T(8,128)(2,1)S(1)}, bf16[64,2048]{1,0:T(8,128)(2,1)}, u32[]{:S(2)}, u32[]{:S(2)}) collective-permute-start(bf16[64,2048]{1,0:T(8,128)(2,1)S(1)} %get-tuple-element.44), channel_id=1, source_target_pairs={{0,16},{16,0},{32,48},{48,32},{64,80},{80,64},{96,112},{112,96},{1... | collective-permute-start | bytes 786440 | tf_op jit(solution)/shard_map/ppermute | solution.py:47
  33.8 4.9 %collective-permute-done.refs_1_ = bf16[64,640]{1,0:T(8,128)(2,1)S(1)} collective-permute-done((bf16[64,640]{1,0:T(8,128)(2,1)S(1)}, bf16[64,640]{1,0:T(8,128)(2,1)S(1)}, u32[]{:S(2)}, u32[]{:S(2)}) %collective-permute-start) | collective-permute-done | bytes 81952 | tf_op jit(solution)/shard_map/ppermute | solution.py:43
  38.8 2.2 %collective-permute-done.2.refs_3_ = bf16[64,640]{1,0:T(8,128)(2,1)S(1)} collective-permute-done((bf16[64,640]{1,0:T(8,128)(2,1)S(1)}, bf16[64,640]{1,0:T(8,128)(2,1)S(1)}, u32[]{:S(2)}, u32[]{:S(2)}) %collective-permute-start.2) | collective-permute-done | bytes 81952 | tf_op jit(solution)/shard_map/ppermute | solution.py:43
  41.0 3.0 %collective-permute-done.4 = bf16[64,2048]{1,0:T(8,128)(2,1)} collective-permute-done((bf16[64,2048]{1,0:T(8,128)(2,1)S(1)}, bf16[64,2048]{1,0:T(8,128)(2,1)}, u32[]{:S(2)}, u32[]{:S(2)}) %collective-permute-start.4) | collective-permute-done | bytes 262176 | tf_op jit(solution)/shard_map/ppermute | solution.py:47
  44.0 1.3 %maximum_select_fusion.refs_0_ = bf16[128,2048]{1,0:T(8,128)(2,1)S(1)} fusion(bf16[64,2048]{1,0:T(8,128)(2,1)} %collective-permute-done.4, bf16[64,2048]{1,0:T(8,128)(2,1)} %get-tuple-element.43, pred[]{:T(512)S(6)} %eq.50), kind=kLoop, calls=%fused_computation.16 | loop fusion | flops 2359296 | bytes 1048577 | tf_op jit(solution)/shard_map/jit(_where)/select_n | solution.py:277
  45.3 2.2 %collective-permute-start.5 = (bf16[128,2048]{1,0:T(8,128)(2,1)S(1)}, bf16[128,2048]{1,0:T(8,128)(2,1)}, u32[]{:S(2)}, u32[]{:S(2)}) collective-permute-start(bf16[128,2048]{1,0:T(8,128)(2,1)S(1)} %maximum_select_fusion.refs_0_), channel_id=1, source_target_pairs={{0,96},{16,112},{32,0},{48,16},{64,32},{80,48},{96,64},{112,80},{1... | collective-permute-start | bytes 1572872 | tf_op jit(solution)/shard_map/ppermute | solution.py:43
  48.3 1.3 %collective-permute-start.7 = (bf16[128,2048]{1,0:T(8,128)(2,1)S(1)}, bf16[128,2048]{1,0:T(8,128)(2,1)}, u32[]{:S(2)}, u32[]{:S(2)}) collective-permute-start(bf16[128,2048]{1,0:T(8,128)(2,1)S(1)} %maximum_select_fusion.refs_0_), channel_id=1, source_target_pairs={{0,32},{16,48},{32,64},{48,80},{64,96},{80,112},{96,0},{112,16},{1... | collective-permute-start | bytes 1572872 | tf_op jit(solution)/shard_map/ppermute | solution.py:43
  50.5 1.0 iota_compare_fusion
  51.5 4.2 %shard_map.95 = (bf16[3,1024,512]{2,1,0:T(8,128)(2,1)S(1)}, bf16[384,512]{1,0:T(8,128)(2,1)S(1)}) custom-call(bf16[8,320,384]{2,1,0:T(8,128)(2,1)S(1)} %all-to-all-done.in_ref), custom_call_target="tpu_custom_call" | custom-call | flops 1000000 | bytes 100000 | tf_op jit(solution)/shard_map/pallas_call | solution.py:231
  55.8 3.5 %collective-permute-start.8 = (bf16[256,512]{1,0:T(8,128)(2,1)S(1)}, bf16[256,512]{1,0:T(8,128)(2,1)S(1)}, u32[]{:S(2)}, u32[]{:S(2)}) collective-permute-start(bf16[256,512]{1,0:T(8,128)(2,1)S(1)} %slice.51), channel_id=1, source_target_pairs={{0,16},{16,0},{32,48},{48,32},{64,80},{80,64},{96,112},{112,96},{1... | collective-permute-start | bytes 786440 | tf_op jit(solution)/shard_map/ppermute | solution.py:47
  59.3 5.7 %shard_map.96 = bf16[8,400,256]{2,1,0:T(8,128)(2,1)S(1)} custom-call(s32[8]{0:T(128)S(1)} %concatenate.24.place_ref, bf16[8,320,384]{2,1,0:T(8,128)(2,1)S(1)} %all-to-all-done.in_ref, bf16[64,640]{1,0:T(8,128)(2,1)S(1)} %get-tuple-element.21.refs_0_, bf16[64,640]{1,0:T(8,128)(2,1)S(1)} %collective-permute-done.refs_1_, ...), custom_call_target="tpu_custom_call" | custom-call | flops 1000000 | bytes 100000 | tf_op jit(solution)/shard_map/pallas_call | solution.py:246
  65.5 3.2 %collective-permute-done.5.refs_1_ = bf16[128,2048]{1,0:T(8,128)(2,1)} collective-permute-done((bf16[128,2048]{1,0:T(8,128)(2,1)S(1)}, bf16[128,2048]{1,0:T(8,128)(2,1)}, u32[]{:S(2)}, u32[]{:S(2)}) %collective-permute-start.5) | collective-permute-done | bytes 524320 | tf_op jit(solution)/shard_map/ppermute | solution.py:43
  68.7 3.8 %collective-permute-done.7.refs_3_ = bf16[128,2048]{1,0:T(8,128)(2,1)} collective-permute-done((bf16[128,2048]{1,0:T(8,128)(2,1)S(1)}, bf16[128,2048]{1,0:T(8,128)(2,1)}, u32[]{:S(2)}, u32[]{:S(2)}) %collective-permute-start.7) | collective-permute-done | bytes 524320 | tf_op jit(solution)/shard_map/ppermute | solution.py:43
  73.1 3.8 %shard_map.97 = (bf16[320,2048]{1,0:T(8,128)(2,1)S(1)}, bf16[320,2048]{1,0:T(8,128)(2,1)}) custom-call(bf16[640,512]{1,0:T(8,128)(2,1)S(1)} %fusion.3.att_ref, bf16[128,2048]{1,0:T(8,128)(2,1)S(1)} %maximum_select_fusion.refs_0_, bf16[128,2048]{1,0:T(8,128)(2,1)} %collective-permute-done.5.refs_1_, bf16[128,2048]{1,0:T(8,128)(2,1)} %collective-permute-done.6.refs_2_, ...), custom_call_target="tpu_custom_call" | custom-call | flops 1400000000 | bytes 8000000 | tf_op jit(solution)/shard_map/pallas_call | solution.py:110
  76.9 1.1 copy-done.3
  78.1 3.6 %all-to-all-start.1 = ((bf16[8,400,256]{2,1,0:T(8,128)(2,1)}), bf16[8,400,256]{2,1,0:T(8,128)(2,1)S(1)}, u32[]{:S(2)}, u32[]{:S(2)}) async-start(bf16[8,400,256]{2,1,0:T(8,128)(2,1)} %copy-done.2), calls=%async_computation.1 | async-start | bytes 3276800 | tf_op jit(solution)/shard_map/all_to_all | solution.py:27
  81.7 1.8 %add_convert_fusion.2 = (bf16[80,2048]{1,0:T(8,128)(2,1)S(1)}, bf16[80,2048]{1,0:T(8,128)(2,1)S(1)}, bf16[80,2048]{1,0:T(8,128)(2,1)S(1)}) fusion(bf16[320,2048]{1,0:T(8,128)(2,1)} %collective-permute-done.9, bf16[320,2048]{1,0:T(8,128)(2,1)} %copy-done.3), kind=kLoop, calls=%fused_computation.14 | loop fusion | flops 1966080 | bytes 2949120 | tf_op jit(solution)/shard_map/convert_element_type | solution.py:330
  84.2 2.4 %collective-permute-start.11 = (bf16[80,2048]{1,0:T(8,128)(2,1)S(1)}, bf16[80,2048]{1,0:T(8,128)(2,1)S(1)}, u32[]{:S(2)}, u32[]{:S(2)}) collective-permute-start(bf16[80,2048]{1,0:T(8,128)(2,1)S(1)} %get-tuple-element.42), channel_id=1, source_target_pairs={{0,8},{1,9},{2,10},{3,11},{4,12},{5,13},{6,14},{7,15},{8,0},{9,1},... | collective-permute-start | bytes 983048 | tf_op jit(solution)/shard_map/ppermute | solution.py:31
  86.7 7.5 %collective-permute-done.10 = bf16[80,2048]{1,0:T(8,128)(2,1)S(1)} collective-permute-done((bf16[80,2048]{1,0:T(8,128)(2,1)S(1)}, bf16[80,2048]{1,0:T(8,128)(2,1)S(1)}, u32[]{:S(2)}, u32[]{:S(2)}) %collective-permute-start.10) | collective-permute-done | bytes 327712 | tf_op jit(solution)/shard_map/ppermute | solution.py:31
  94.2 2.1 %collective-permute-done.11 = bf16[80,2048]{1,0:T(8,128)(2,1)S(1)} collective-permute-done((bf16[80,2048]{1,0:T(8,128)(2,1)S(1)}, bf16[80,2048]{1,0:T(8,128)(2,1)S(1)}, u32[]{:S(2)}, u32[]{:S(2)}) %collective-permute-start.11) | collective-permute-done | bytes 327712 | tf_op jit(solution)/shard_map/ppermute | solution.py:31
  96.3 6.3 %collective-permute-done.12 = bf16[80,2048]{1,0:T(8,128)(2,1)S(1)} collective-permute-done((bf16[80,2048]{1,0:T(8,128)(2,1)S(1)}, bf16[80,2048]{1,0:T(8,128)(2,1)S(1)}, u32[]{:S(2)}, u32[]{:S(2)}) %collective-permute-start.12) | collective-permute-done | bytes 327712 | tf_op jit(solution)/shard_map/ppermute | solution.py:31
  102.6 1.3 %fusion.43 = (bf16[80,2048]{1,0:T(8,128)(2,1)S(1)}, f32[80,2048]{1,0:T(8,128)S(1)}) fusion(bf16[80,2048]{1,0:T(8,128)(2,1)S(1)} %collective-permute-done.12, bf16[80,2048]{1,0:T(8,128)(2,1)S(1)} %collective-permute-done.11, bf16[80,2048]{1,0:T(8,128)(2,1)S(1)} %collective-permute-done.10, bf16[320,2048]{1,0:T(8,128)(2,1)} %collective-permute-done.9, ...), kind=kLoop, calls=%fused_computation.108 | loop fusion | flops 1638400 | bytes 2621440 | tf_op jit(solution)/shard_map/convert_element_type | solution.py:332
  104.7 3.7 %collective-permute-start.14 = (bf16[20,2048]{1,0:T(8,128)(2,1)S(1)}, bf16[20,2048]{1,0:T(8,128)(2,1)S(1)}, u32[]{:S(2)}, u32[]{:S(2)}) collective-permute-start(bf16[20,2048]{1,0:T(8,128)(2,1)S(1)} %get-tuple-element.47), channel_id=1, source_target_pairs={{0,16},{1,17},{2,18},{3,19},{4,20},{5,21},{6,22},{7,23},{8,24},{9,... | collective-permute-start | bytes 245768 | tf_op jit(solution)/shard_map/ppermute | solution.py:39
  108.7 1.6 %shard_map.98 = (bf16[128,2560]{1,0:T(8,128)(2,1)}, bf16[128,2560]{1,0:T(8,128)(2,1)}, bf16[128,2560]{1,0:T(8,128)(2,1)}) custom-call(bf16[8,400,256]{2,1,0:T(8,128)(2,1)S(1)} %all-to-all-done.1.back_ref, bf16[64,128]{1,0:T(8,128)(2,1)S(1)} %fusion.7.selector_ref), custom_call_target="tpu_custom_call" | custom-call | flops 20000000000 | bytes 4000000 | tf_op jit(solution)/shard_map/pallas_call | solution.py:151
  111.3 2.0 %collective-permute-done.14 = bf16[20,2048]{1,0:T(8,128)(2,1)S(1)} collective-permute-done((bf16[20,2048]{1,0:T(8,128)(2,1)S(1)}, bf16[20,2048]{1,0:T(8,128)(2,1)S(1)}, u32[]{:S(2)}, u32[]{:S(2)}) %collective-permute-start.14) | collective-permute-done | bytes 81952 | tf_op jit(solution)/shard_map/ppermute | solution.py:39
  113.3 1.8 %collective-permute-done.15 = bf16[20,2048]{1,0:T(8,128)(2,1)S(1)} collective-permute-done((bf16[20,2048]{1,0:T(8,128)(2,1)S(1)}, bf16[20,2048]{1,0:T(8,128)(2,1)S(1)}, u32[]{:S(2)}, u32[]{:S(2)}) %collective-permute-start.15) | collective-permute-done | bytes 81952 | tf_op jit(solution)/shard_map/ppermute | solution.py:39
  (54 shorter events, 10.5 us)
Async XLA Ops:
  0.6 1.1 copy-start
  0.6 1.4 %copy-start.4 = (bf16[1,128,2560]{2,1,0:T(8,128)(2,1)S(1)}, bf16[1,128,2560]{2,1,0:T(8,128)(2,1)}, u32[]{:S(2)}) copy-start(bf16[1,128,2560]{2,1,0:T(8,128)(2,1)} %param.7) | copy-start | bytes 1966084
  2.0 1.1 copy-start.5
  3.3 1.3 %copy-start.1 = (bf16[8,320,384]{2,1,0:T(8,128)(2,1)}, bf16[8,320,384]{2,1,0:T(8,128)(2,1)S(1)}, u32[]{:S(2)}) copy-start(bf16[8,320,384]{2,1,0:T(8,128)(2,1)S(1)} %shard_map.93) | copy-start | bytes 5898244
  4.6 8.1 %copy-start.6 = (bf16[1,64,4096]{2,1,0:T(8,128)(2,1)S(1)}, bf16[1,64,4096]{2,1,0:T(8,128)(2,1)}, u32[]{:S(2)}) copy-start(bf16[1,64,4096]{2,1,0:T(8,128)(2,1)} %param.10) | copy-start | bytes 1572868
  4.6 46.9 %all-to-all-start = ((bf16[8,320,384]{2,1,0:T(8,128)(2,1)}), bf16[8,320,384]{2,1,0:T(8,128)(2,1)S(1)}, u32[]{:S(2)}, u32[]{:S(2)}) async-start(bf16[8,320,384]{2,1,0:T(8,128)(2,1)} %copy-done.1), calls=%async_computation | async-start | bytes 3932160 | tf_op jit(solution)/shard_map/all_to_all | solution.py:27
  23.9 14.8 %collective-permute-start = (bf16[64,640]{1,0:T(8,128)(2,1)S(1)}, bf16[64,640]{1,0:T(8,128)(2,1)S(1)}, u32[]{:S(2)}, u32[]{:S(2)}) collective-permute-start(bf16[64,640]{1,0:T(8,128)(2,1)S(1)} %get-tuple-element.22), channel_id=1, source_target_pairs={{0,96},{16,112},{32,0},{48,16},{64,32},{80,48},{96,64},{112,80},{1... | collective-permute-start | bytes 245768 | tf_op jit(solution)/shard_map/ppermute | solution.py:43
  27.2 11.6 %collective-permute-start.1 = (bf16[64,640]{1,0:T(8,128)(2,1)S(1)}, bf16[64,640]{1,0:T(8,128)(2,1)S(1)}, u32[]{:S(2)}, u32[]{:S(2)}) collective-permute-start(bf16[64,640]{1,0:T(8,128)(2,1)S(1)} %get-tuple-element.23), channel_id=1, source_target_pairs={{0,64},{16,80},{32,96},{48,112},{64,0},{80,16},{96,32},{112,48},{1... | collective-permute-start | bytes 245768 | tf_op jit(solution)/shard_map/ppermute | solution.py:43
  28.0 12.9 %collective-permute-start.2 = (bf16[64,640]{1,0:T(8,128)(2,1)S(1)}, bf16[64,640]{1,0:T(8,128)(2,1)S(1)}, u32[]{:S(2)}, u32[]{:S(2)}) collective-permute-start(bf16[64,640]{1,0:T(8,128)(2,1)S(1)} %get-tuple-element.24), channel_id=1, source_target_pairs={{0,32},{16,48},{32,64},{48,80},{64,96},{80,112},{96,0},{112,16},{1... | collective-permute-start | bytes 245768 | tf_op jit(solution)/shard_map/ppermute | solution.py:43
  30.7 13.3 %collective-permute-start.4 = (bf16[64,2048]{1,0:T(8,128)(2,1)S(1)}, bf16[64,2048]{1,0:T(8,128)(2,1)}, u32[]{:S(2)}, u32[]{:S(2)}) collective-permute-start(bf16[64,2048]{1,0:T(8,128)(2,1)S(1)} %get-tuple-element.44), channel_id=1, source_target_pairs={{0,16},{16,0},{32,48},{48,32},{64,80},{80,64},{96,112},{112,96},{1... | collective-permute-start | bytes 786440 | tf_op jit(solution)/shard_map/ppermute | solution.py:47
  45.3 23.4 %collective-permute-start.5 = (bf16[128,2048]{1,0:T(8,128)(2,1)S(1)}, bf16[128,2048]{1,0:T(8,128)(2,1)}, u32[]{:S(2)}, u32[]{:S(2)}) collective-permute-start(bf16[128,2048]{1,0:T(8,128)(2,1)S(1)} %maximum_select_fusion.refs_0_), channel_id=1, source_target_pairs={{0,96},{16,112},{32,0},{48,16},{64,32},{80,48},{96,64},{112,80},{1... | collective-permute-start | bytes 1572872 | tf_op jit(solution)/shard_map/ppermute | solution.py:43
  47.5 21.2 %collective-permute-start.6 = (bf16[128,2048]{1,0:T(8,128)(2,1)S(1)}, bf16[128,2048]{1,0:T(8,128)(2,1)}, u32[]{:S(2)}, u32[]{:S(2)}) collective-permute-start(bf16[128,2048]{1,0:T(8,128)(2,1)S(1)} %maximum_select_fusion.refs_0_), channel_id=1, source_target_pairs={{0,64},{16,80},{32,96},{48,112},{64,0},{80,16},{96,32},{112,48},{1... | collective-permute-start | bytes 1572872 | tf_op jit(solution)/shard_map/ppermute | solution.py:43
  48.3 24.1 %collective-permute-start.7 = (bf16[128,2048]{1,0:T(8,128)(2,1)S(1)}, bf16[128,2048]{1,0:T(8,128)(2,1)}, u32[]{:S(2)}, u32[]{:S(2)}) collective-permute-start(bf16[128,2048]{1,0:T(8,128)(2,1)S(1)} %maximum_select_fusion.refs_0_), channel_id=1, source_target_pairs={{0,32},{16,48},{32,64},{48,80},{64,96},{80,112},{96,0},{112,16},{1... | collective-permute-start | bytes 1572872 | tf_op jit(solution)/shard_map/ppermute | solution.py:43
  50.4 8.9 %collective-permute-start.3 = (bf16[256,384]{1,0:T(8,128)(2,1)}, bf16[256,384]{1,0:T(8,128)(2,1)}, u32[]{:S(2)}, u32[]{:S(2)}) collective-permute-start(bf16[256,384]{1,0:T(8,128)(2,1)} %pad_maximum_fusion), channel_id=1, source_target_pairs={{0,16},{16,0},{32,48},{48,32},{64,80},{80,64},{96,112},{112,96},{1... | collective-permute-start | bytes 589832 | tf_op jit(solution)/shard_map/ppermute | solution.py:47
  55.8 16.7 %collective-permute-start.8 = (bf16[256,512]{1,0:T(8,128)(2,1)S(1)}, bf16[256,512]{1,0:T(8,128)(2,1)S(1)}, u32[]{:S(2)}, u32[]{:S(2)}) collective-permute-start(bf16[256,512]{1,0:T(8,128)(2,1)S(1)} %slice.51), channel_id=1, source_target_pairs={{0,16},{16,0},{32,48},{48,32},{64,80},{80,64},{96,112},{112,96},{1... | collective-permute-start | bytes 786440 | tf_op jit(solution)/shard_map/ppermute | solution.py:47
  59.3 5.7 %copy-start.7 = (pred[640,640]{1,0:T(32,128)(4,1)S(1)}, pred[640,640]{1,0:T(32,128)(4,1)}, u32[]{:S(2)}) copy-start(pred[640,640]{1,0:T(32,128)(4,1)} %iota_compare_fusion) | copy-start | bytes 1228804
  65.0 7.8 %copy-start.2 = (bf16[8,400,256]{2,1,0:T(8,128)(2,1)}, bf16[8,400,256]{2,1,0:T(8,128)(2,1)S(1)}, u32[]{:S(2)}) copy-start(bf16[8,400,256]{2,1,0:T(8,128)(2,1)S(1)} %shard_map.96) | copy-start | bytes 4915204
  76.9 1.1 copy-start.3
  78.0 3.6 %collective-permute-start.9 = (bf16[320,2048]{1,0:T(8,128)(2,1)}, bf16[320,2048]{1,0:T(8,128)(2,1)}, u32[]{:S(2)}, u32[]{:S(2)}) collective-permute-start(bf16[320,2048]{1,0:T(8,128)(2,1)} %get-tuple-element.33), channel_id=1, source_target_pairs={{0,1},{1,0},{2,3},{3,2},{4,5},{5,4},{6,7},{7,6},{8,9},{9,8},{10,11... | collective-permute-start | bytes 3932168 | tf_op jit(solution)/shard_map/ppermute | solution.py:51
  78.1 30.7 %all-to-all-start.1 = ((bf16[8,400,256]{2,1,0:T(8,128)(2,1)}), bf16[8,400,256]{2,1,0:T(8,128)(2,1)S(1)}, u32[]{:S(2)}, u32[]{:S(2)}) async-start(bf16[8,400,256]{2,1,0:T(8,128)(2,1)} %copy-done.2), calls=%async_computation.1 | async-start | bytes 3276800 | tf_op jit(solution)/shard_map/all_to_all | solution.py:27
  83.5 10.8 %collective-permute-start.10 = (bf16[80,2048]{1,0:T(8,128)(2,1)S(1)}, bf16[80,2048]{1,0:T(8,128)(2,1)S(1)}, u32[]{:S(2)}, u32[]{:S(2)}) collective-permute-start(bf16[80,2048]{1,0:T(8,128)(2,1)S(1)} %get-tuple-element.40), channel_id=1, source_target_pairs={{0,4},{1,5},{2,6},{3,7},{4,8},{5,9},{6,10},{7,11},{8,12},{9,13},{1... | collective-permute-start | bytes 983048 | tf_op jit(solution)/shard_map/ppermute | solution.py:31
  84.2 12.1 %collective-permute-start.11 = (bf16[80,2048]{1,0:T(8,128)(2,1)S(1)}, bf16[80,2048]{1,0:T(8,128)(2,1)S(1)}, u32[]{:S(2)}, u32[]{:S(2)}) collective-permute-start(bf16[80,2048]{1,0:T(8,128)(2,1)S(1)} %get-tuple-element.42), channel_id=1, source_target_pairs={{0,8},{1,9},{2,10},{3,11},{4,12},{5,13},{6,14},{7,15},{8,0},{9,1},... | collective-permute-start | bytes 983048 | tf_op jit(solution)/shard_map/ppermute | solution.py:31
  86.6 15.9 %collective-permute-start.12 = (bf16[80,2048]{1,0:T(8,128)(2,1)S(1)}, bf16[80,2048]{1,0:T(8,128)(2,1)S(1)}, u32[]{:S(2)}, u32[]{:S(2)}) collective-permute-start(bf16[80,2048]{1,0:T(8,128)(2,1)S(1)} %get-tuple-element.41), channel_id=1, source_target_pairs={{0,12},{1,13},{2,14},{3,15},{4,0},{5,1},{6,2},{7,3},{8,4},{9,5},{1... | collective-permute-start | bytes 983048 | tf_op jit(solution)/shard_map/ppermute | solution.py:31
  104.0 6.4 %collective-permute-start.13 = (bf16[20,2048]{1,0:T(8,128)(2,1)S(1)}, bf16[20,2048]{1,0:T(8,128)(2,1)}, u32[]{:S(2)}, u32[]{:S(2)}) collective-permute-start(bf16[20,2048]{1,0:T(8,128)(2,1)S(1)} %get-tuple-element.45), channel_id=1, source_target_pairs={{0,2},{1,3},{2,0},{3,1},{4,6},{5,7},{6,4},{7,5},{8,10},{9,11},{10,... | collective-permute-start | bytes 245768 | tf_op jit(solution)/shard_map/ppermute | solution.py:39
  104.7 8.6 %collective-permute-start.14 = (bf16[20,2048]{1,0:T(8,128)(2,1)S(1)}, bf16[20,2048]{1,0:T(8,128)(2,1)S(1)}, u32[]{:S(2)}, u32[]{:S(2)}) collective-permute-start(bf16[20,2048]{1,0:T(8,128)(2,1)S(1)} %get-tuple-element.47), channel_id=1, source_target_pairs={{0,16},{1,17},{2,18},{3,19},{4,20},{5,21},{6,22},{7,23},{8,24},{9,... | collective-permute-start | bytes 245768 | tf_op jit(solution)/shard_map/ppermute | solution.py:39
  108.4 6.7 %collective-permute-start.15 = (bf16[20,2048]{1,0:T(8,128)(2,1)S(1)}, bf16[20,2048]{1,0:T(8,128)(2,1)S(1)}, u32[]{:S(2)}, u32[]{:S(2)}) collective-permute-start(bf16[20,2048]{1,0:T(8,128)(2,1)S(1)} %get-tuple-element.46), channel_id=1, source_target_pairs={{0,18},{1,19},{2,16},{3,17},{4,22},{5,23},{6,20},{7,21},{8,26},{9,... | collective-permute-start | bytes 245768 | tf_op jit(solution)/shard_map/ppermute | solution.py:39

commit v4 on v3

--- a/solution.py
+++ b/solution.py
@@ -95,31 +95,38 @@
     )(starts, grad)
 
 
-def outer(att_rows, cot_parts):
-    width = cot_parts[0].shape[1]
+def outer(place, att_rows, own_parts, other_parts):
+    width = other_parts[0].shape[1]
     rows = att_rows.shape[0] // 2
     tile = 1024
 
-    def kernel(att_ref, *refs):
-        att = att_ref[...]
-        cots = jnp.concatenate([r[...] for r in refs[:4]], axis=0)
-        refs[4][...] = dot(att[:rows], cots, 1, 0).astype(BF)
-        refs[5][...] = dot(att[rows:], cots, 1, 0).astype(BF)
-
-    out = pl.BlockSpec((rows, tile), lambda i: (0, i))
+    def kernel(place_ref, att_ref, *refs):
+        first = place_ref[0] == 0
+        blocks = []
+        for own, other in zip(refs[:4], refs[4:8]):
+            blocks.append(jnp.where(first, own[...], other[...]))
+            blocks.append(jnp.where(first, other[...], own[...]))
+        cots = jnp.concatenate(blocks, axis=0)
+        refs[8][...] = dot(att_ref[:rows], cots, 1, 0).astype(BF)
+        refs[9][...] = dot(att_ref[rows:], cots, 1, 0).astype(BF)
+
+    out = pl.BlockSpec((rows, tile), lambda i, *_: (0, i))
     return pl.pallas_call(
         kernel,
-        grid=(width // tile,),
-        in_specs=[pl.BlockSpec((2 * rows, QUERIES), lambda i: (0, 0))]
-        + [pl.BlockSpec((2 * MSK, tile), lambda i: (0, i))] * 4,
-        out_specs=[out, out],
+        grid_spec=pltpu.PrefetchScalarGridSpec(
+            num_scalar_prefetch=1,
+            grid=(width // tile,),
+            in_specs=[pl.BlockSpec((2 * rows, QUERIES), lambda i, *_: (0, 0))]
+            + [pl.BlockSpec((MSK, tile), lambda i, *_: (0, i))] * 8,
+            out_specs=[out, out],
+        ),
         out_shape=[
-            jax.ShapeDtypeStruct((rows, width), BF),
+            pltpu.HBM((rows, width), BF),
             pltpu.HBM((rows, width), BF),
         ],
         compiler_params=PARAMS,
         cost_estimate=cost(1.4e9, 8e6),
-    )(att_rows, *cot_parts)
+    )(place, att_rows, *own_parts, *other_parts)
 
 
 def finish(back, selector):
@@ -258,7 +265,7 @@
             out_specs=pl.BlockSpec((8, ROWS_BACK, 2 * HEAD_DIM), lambda h, *_: (0, 0, 0)),
             scratch_shapes=[pltpu.VMEM((QUERIES, HEAD_DIM), BF)],
         ),
-        out_shape=jax.ShapeDtypeStruct((8, ROWS_BACK, 2 * HEAD_DIM), BF),
+        out_shape=pltpu.HBM((8, ROWS_BACK, 2 * HEAD_DIM), BF),
         compiler_params=PARAMS,
         cost_estimate=cost(1e6, 1e5),
     )(place, sent, *own, got, probs, att)
@@ -274,12 +281,6 @@
     half = cot.shape[1] // 2
     cot_kept = lax.dynamic_slice_in_dim(cot, y * half, half, 1)
     cot_got = swap_y(lax.dynamic_slice_in_dim(cot, (1 - y) * half, half, 1))
-    cot_pair = jnp.where(
-        y == 0,
-        jnp.concatenate([cot_kept, cot_got], axis=0),
-        jnp.concatenate([cot_got, cot_kept], axis=0),
-    )
-
     selector = (steps[:, None] == jnp.arange(TOK, dtype=jnp.int32)[None, :]).astype(BF)
     masked_query = dot(selector, query_states[0], 1, 0).astype(BF)
     packed = slabs_of(masked_query, key_states[0], value_states[0])
@@ -290,19 +291,24 @@
     grads_out = pack_grads(ring * 640, masked_grad)
     own_grad = [grads_out[0]] + [move_z(grads_out[4 - dz], 4 - dz) for dz in (1, 2, 3)]
     own_all = jnp.concatenate(own_grad, axis=0)
+    own_all, cot_got = lax.optimization_barrier((own_all, cot_got))
     got_grad = swap_y(
         jnp.concatenate(
             [lax.dynamic_slice_in_dim(own_all, (1 - y) * 384, 256, 1), own_all[:, 256:384]], axis=1
         )
     )
     place = jnp.concatenate([jnp.stack([y, 3 * y, 3 * y + 1, 0 * y + 2]), columns]).astype(jnp.int32)
-    cot_parts = [cot_pair] + [move_z(cot_pair, dz) for dz in (3, 2, 1)]
+    own_parts = [cot_kept] + [move_z(cot_kept, dz) for dz in (3, 2, 1)]
+    other_parts = [cot_got] + [move_z(cot_got, dz) for dz in (3, 2, 1)]
     probs, att = forward(heads_in)
     att_got = swap_y(att[:256])
-    outs = backward(place, heads_in, own_grad, got_grad, probs, att)
+    place_back, own_parts = lax.optimization_barrier((place, own_parts))
+    outs = backward(place_back, heads_in, own_grad, got_grad, probs, att)
 
     back = exchange(outs)
-    cot_parts, att_got, _ = lax.optimization_barrier((cot_parts, att_got, outs))
+    own_parts, other_parts, att_got, _ = lax.optimization_barrier(
+        (own_parts, other_parts, att_got, outs)
+    )
     r = jnp.arange(640, dtype=jnp.int32)
     rc, rx, rl, rh, rr = r // 320, (r // 80) % 4, (r // 40) % 2, (r // 20) % 2, r % 20
     wanted = (
@@ -320,7 +326,7 @@
     att_rows = lax.dynamic_slice_in_dim(
         jnp.concatenate([att_rows, att_rows], axis=1), z * 2 * MSK, QUERIES, 1
     )
-    kept, sent = outer(att_rows, cot_parts)
+    kept, sent = outer(place, att_rows, own_parts, other_parts)
     sent = swap_core(sent)
     chunks = [
         kept[i * 80 : (i + 1) * 80].astype(F32) + sent[i * 80 : (i + 1) * 80].astype(F32) for i in range(4)

time: 116 us -> 115 us (level)
  waiting for transfers between devices: 36.8 us -> 24.5 us
  starting transfers between devices: 35.5 us -> 45.3 us
    ppermute x6 -> x9, waiting for transfers between devices: 14.1 us -> 4.11 us  [move_z(): return lax.ppermute(a, 'blk', [(i, (i + 2 * dz) % 8) for i in range(8)])]
    ppermute x6 -> x9, starting transfers between devices: 9.33 us -> 17.3 us  [move_z(): return lax.ppermute(a, 'blk', [(i, (i + 2 * dz) % 8) for i in range(8)])]
    all_to_all x2, starting transfers between devices: 11.7 us -> 14.1 us  [exchange(): return lax.all_to_all(a, 'blk', 0, 0, tiled=True)]
    ppermute x3, waiting for transfers between devices: 3.02 us -> 0.84 us  [swap_y(): return lax.ppermute(a, 'blk', [(i, i ^ 1) for i in range(8)])]
    select_n x1 -> x0, other arithmetic: 1.31 us -> none  [shards(): jnp.where(y == 0, jnp.concatenate([cot_kept, cot_got], axis=0), jnp.conca...]
    unnamed x19 -> x20, local copies, waits for them, and re-layouts: 3.85 us -> 4.5 us
  transfers between devices with their start and end apart: 18 -> 21, of which waited for: 10 -> 8; matrix products, arithmetic and copies ran while one was open for 18% -> 17% of each run, Pallas kernels for 10% -> 11%
where the time goes in v4:
time: 115 us
  starting transfers between devices  45.3 us (39%)
  waiting for transfers between devices  24.5 us (21%)
  Pallas kernels  17.2 us (15%)
  matrix products  11.7 us (10%)
  other arithmetic  8.62 us (7%)
  local copies, waits for them, and re-layouts  6.45 us (6%)
    ppermute x9, starting transfers between devices, move_z(): return lax.ppermute(a, 'blk', [(i, (i + 2 * dz) % 8) for i in range(8)])  17.3 us
    ppermute x3, waiting for transfers between devices, move_x(): return lax.ppermute(a, 'dp', [(i, (i + 4 * dx) % 16) for i in range(16)])  15.6 us
    all_to_all x2, starting transfers between devices, exchange(): return lax.all_to_all(a, 'blk', 0, 0, tiled=True)  14.1 us
    dot_general x4, matrix products, dot(): lax.dot_general(a, b, (((ca,), (cb,)), ((), ())), preferred_element_type=...  11.7 us
    pallas_call x1, Pallas kernels, backward(): pl.pallas_call(backward_kernel, grid_spec=pltpu.PrefetchScalarGridSpec(nu...  6.21 us
    ppermute x3, starting transfers between devices, swap_y(): return lax.ppermute(a, 'blk', [(i, i ^ 1) for i in range(8)])  6.1 us
    ppermute x3, starting transfers between devices, move_y(): return lax.ppermute(a, ('blk', 'dp'), pairs)  4.78 us
    unnamed x20, local copies, waits for them, and re-layouts  4.5 us
  transfers between devices with their start and end apart: 21, of which 8 were waited for; matrix products, arithmetic and copies ran while one was open for 17% of the time, Pallas kernels for 11%

profile of v4, /device:TPU:6, one launch (start us, length us, event | category | flops | bytes accessed | tf_op | source)
XLA Modules:
  0.0 114.6 jit_solution(7944614894574836361)
XLA Ops:
  2.1 1.1 copy-done.3
  3.3 1.3 %copy-done.1 = bf16[8,320,384]{2,1,0:T(8,128)(2,1)} copy-done((bf16[8,320,384]{2,1,0:T(8,128)(2,1)}, bf16[8,320,384]{2,1,0:T(8,128)(2,1)S(1)}, u32[]{:S(2)}) %copy-start.1) | copy-done | bytes 1966104
  4.6 8.1 %all-to-all-start = ((bf16[8,320,384]{2,1,0:T(8,128)(2,1)}), bf16[8,320,384]{2,1,0:T(8,128)(2,1)S(1)}, u32[]{:S(2)}, u32[]{:S(2)}) async-start(bf16[8,320,384]{2,1,0:T(8,128)(2,1)} %copy-done.1), calls=%async_computation | async-start | bytes 3932160 | tf_op jit(solution)/shard_map/all_to_all | solution.py:27
  12.7 10.6 %convolution_convert_fusion.grad_ref = bf16[64,2560]{1,0:T(8,128)(2,1)S(1)} fusion(bf16[2560,4096]{1,0:T(8,128)(2,1)} %param.11, bf16[1,64,4096]{2,1,0:T(8,128)(2,1)S(1)} %copy-done.8), kind=kOutput, calls=%fused_computation | convolution fusion | flops 1342341120 | bytes 21823488 | tf_op jit(solution)/shard_map/dot_general | solution.py:55
  23.9 3.3 %collective-permute-start.3 = (bf16[64,640]{1,0:T(8,128)(2,1)S(1)}, bf16[64,640]{1,0:T(8,128)(2,1)S(1)}, u32[]{:S(2)}, u32[]{:S(2)}) collective-permute-start(bf16[64,640]{1,0:T(8,128)(2,1)S(1)} %get-tuple-element.34), channel_id=1, source_target_pairs={{0,96},{16,112},{32,0},{48,16},{64,32},{80,48},{96,64},{112,80},{1... | collective-permute-start | bytes 245768 | tf_op jit(solution)/shard_map/ppermute | solution.py:43
  28.1 0.9 collective-permute-start.5
  28.9 1.8 %dynamic-slice_bitcast_fusion = (bf16[64,2048]{1,0:T(8,128)(2,1)}, bf16[64,2048]{1,0:T(8,128)(2,1)S(1)}) fusion(bf16[1,64,4096]{2,1,0:T(8,128)(2,1)} %param.10, s32[]{:T(128)S(6)} %select_n.185, s32[]{:T(128)S(6)} %select_n.184), kind=kLoop, calls=%fused_computation.19 | loop fusion | bytes 1048584 | tf_op jit(solution)/shard_map/dynamic_slice | solution.py:283
  30.7 3.0 %collective-permute-start.6 = (bf16[64,2048]{1,0:T(8,128)(2,1)}, bf16[64,2048]{1,0:T(8,128)(2,1)}, u32[]{:S(2)}, u32[]{:S(2)}) collective-permute-start(bf16[64,2048]{1,0:T(8,128)(2,1)} %get-tuple-element.65), channel_id=1, source_target_pairs={{0,16},{16,0},{32,48},{48,32},{64,80},{80,64},{96,112},{112,96},{1... | collective-permute-start | bytes 786440 | tf_op jit(solution)/shard_map/ppermute | solution.py:47
  33.7 2.4 %collective-permute-start = (bf16[64,2048]{1,0:T(8,128)(2,1)S(1)}, bf16[64,2048]{1,0:T(8,128)(2,1)}, u32[]{:S(2)}, u32[]{:S(2)}) collective-permute-start(bf16[64,2048]{1,0:T(8,128)(2,1)S(1)} %get-tuple-element.46.refs_0_), channel_id=1, source_target_pairs={{0,96},{16,112},{32,0},{48,16},{64,32},{80,48},{96,64},{112,80},{1... | collective-permute-start | bytes 786440 | tf_op jit(solution)/shard_map/ppermute | solution.py:43
  36.2 3.2 %collective-permute-done.3.refs_1_ = bf16[64,640]{1,0:T(8,128)(2,1)S(1)} collective-permute-done((bf16[64,640]{1,0:T(8,128)(2,1)S(1)}, bf16[64,640]{1,0:T(8,128)(2,1)S(1)}, u32[]{:S(2)}, u32[]{:S(2)}) %collective-permute-start.3) | collective-permute-done | bytes 81952 | tf_op jit(solution)/shard_map/ppermute | solution.py:43
  39.4 2.7 %collective-permute-start.1 = (bf16[64,2048]{1,0:T(8,128)(2,1)S(1)}, bf16[64,2048]{1,0:T(8,128)(2,1)S(1)}, u32[]{:S(2)}, u32[]{:S(2)}) collective-permute-start(bf16[64,2048]{1,0:T(8,128)(2,1)S(1)} %get-tuple-element.46.refs_0_), channel_id=1, source_target_pairs={{0,64},{16,80},{32,96},{48,112},{64,0},{80,16},{96,32},{112,48},{1... | collective-permute-start | bytes 786440 | tf_op jit(solution)/shard_map/ppermute | solution.py:43
  42.0 1.1 %collective-permute-start.2 = (bf16[64,2048]{1,0:T(8,128)(2,1)S(1)}, bf16[64,2048]{1,0:T(8,128)(2,1)S(1)}, u32[]{:S(2)}, u32[]{:S(2)}) collective-permute-start(bf16[64,2048]{1,0:T(8,128)(2,1)S(1)} %get-tuple-element.46.refs_0_), channel_id=1, source_target_pairs={{0,32},{16,48},{32,64},{48,80},{64,96},{80,112},{96,0},{112,16},{1... | collective-permute-start | bytes 786440 | tf_op jit(solution)/shard_map/ppermute | solution.py:43
  45.6 1.0 iota_compare_fusion
  47.2 2.7 %collective-permute-start.8 = (bf16[64,2048]{1,0:T(8,128)(2,1)}, bf16[64,2048]{1,0:T(8,128)(2,1)}, u32[]{:S(2)}, u32[]{:S(2)}) collective-permute-start(bf16[64,2048]{1,0:T(8,128)(2,1)} %collective-permute-done.6.refs_4_), channel_id=1, source_target_pairs={{0,96},{16,112},{32,0},{48,16},{64,32},{80,48},{96,64},{112,80},{1... | collective-permute-start | bytes 786440 | tf_op jit(solution)/shard_map/ppermute | solution.py:43
  50.6 2.9 %collective-permute-start.9 = (bf16[64,2048]{1,0:T(8,128)(2,1)}, bf16[64,2048]{1,0:T(8,128)(2,1)}, u32[]{:S(2)}, u32[]{:S(2)}) collective-permute-start(bf16[64,2048]{1,0:T(8,128)(2,1)} %collective-permute-done.6.refs_4_), channel_id=1, source_target_pairs={{0,64},{16,80},{32,96},{48,112},{64,0},{80,16},{96,32},{112,48},{1... | collective-permute-start | bytes 786440 | tf_op jit(solution)/shard_map/ppermute | solution.py:43
  53.5 0.9 collective-permute-done.2.refs_3_
  55.1 4.2 %shard_map.95 = (bf16[3,1024,512]{2,1,0:T(8,128)(2,1)S(1)}, bf16[384,512]{1,0:T(8,128)(2,1)S(1)}) custom-call(bf16[8,320,384]{2,1,0:T(8,128)(2,1)S(1)} %all-to-all-done.in_ref), custom_call_target="tpu_custom_call" | custom-call | flops 1000000 | bytes 100000 | tf_op jit(solution)/shard_map/pallas_call | solution.py:238
  59.4 2.3 %collective-permute-start.11 = (bf16[256,512]{1,0:T(8,128)(2,1)S(1)}, bf16[256,512]{1,0:T(8,128)(2,1)S(1)}, u32[]{:S(2)}, u32[]{:S(2)}) collective-permute-start(bf16[256,512]{1,0:T(8,128)(2,1)S(1)} %slice.51), channel_id=1, source_target_pairs={{0,16},{16,0},{32,48},{48,32},{64,80},{80,64},{96,112},{112,96},{1... | collective-permute-start | bytes 786440 | tf_op jit(solution)/shard_map/ppermute | solution.py:47
  61.7 6.2 %shard_map.96 = bf16[8,400,256]{2,1,0:T(8,128)(2,1)} custom-call(s32[8]{0:T(128)S(1)} %concatenate.18.place_ref, bf16[8,320,384]{2,1,0:T(8,128)(2,1)S(1)} %all-to-all-done.in_ref, bf16[64,640]{1,0:T(8,128)(2,1)S(1)} %get-tuple-element.33.refs_0_, bf16[64,640]{1,0:T(8,128)(2,1)S(1)} %collective-permute-done.3.refs_1_, ...), custom_call_target="tpu_custom_call" | custom-call | flops 1000000 | bytes 100000 | tf_op jit(solution)/shard_map/pallas_call | solution.py:253
  69.4 4.4 %shard_map.97 = (bf16[320,2048]{1,0:T(8,128)(2,1)}, bf16[320,2048]{1,0:T(8,128)(2,1)}) custom-call(s32[8]{0:T(128)S(1)} %concatenate.18.place_ref, bf16[640,512]{1,0:T(8,128)(2,1)S(1)} %fusion.3.att_ref, bf16[64,2048]{1,0:T(8,128)(2,1)S(1)} %get-tuple-element.46.refs_0_, bf16[64,2048]{1,0:T(8,128)(2,1)} %collective-permute-done.refs_1_, ...), custom_call_target="tpu_custom_call" | custom-call | flops 1400000000 | bytes 8000000 | tf_op jit(solution)/shard_map/pallas_call | solution.py:114
  73.8 6.0 %all-to-all-start.1 = ((bf16[8,400,256]{2,1,0:T(8,128)(2,1)}), bf16[8,400,256]{2,1,0:T(8,128)(2,1)S(1)}, u32[]{:S(2)}, u32[]{:S(2)}) async-start(bf16[8,400,256]{2,1,0:T(8,128)(2,1)} %shard_map.96), calls=%async_computation.1 | async-start | bytes 3276800 | tf_op jit(solution)/shard_map/all_to_all | solution.py:27
  79.8 1.8 %add_convert_fusion.2 = (bf16[80,2048]{1,0:T(8,128)(2,1)S(1)}, bf16[80,2048]{1,0:T(8,128)(2,1)S(1)}, bf16[80,2048]{1,0:T(8,128)(2,1)S(1)}) fusion(bf16[320,2048]{1,0:T(8,128)(2,1)} %collective-permute-done.12, bf16[320,2048]{1,0:T(8,128)(2,1)} %get-tuple-element.54), kind=kLoop, calls=%fused_computation.14 | loop fusion | flops 1966080 | bytes 2949120 | tf_op jit(solution)/shard_map/convert_element_type | solution.py:336
  82.2 2.4 %collective-permute-start.14 = (bf16[80,2048]{1,0:T(8,128)(2,1)S(1)}, bf16[80,2048]{1,0:T(8,128)(2,1)S(1)}, u32[]{:S(2)}, u32[]{:S(2)}) collective-permute-start(bf16[80,2048]{1,0:T(8,128)(2,1)S(1)} %get-tuple-element.64), channel_id=1, source_target_pairs={{0,8},{1,9},{2,10},{3,11},{4,12},{5,13},{6,14},{7,15},{8,0},{9,1},... | collective-permute-start | bytes 983048 | tf_op jit(solution)/shard_map/ppermute | solution.py:31
  84.7 7.6 %collective-permute-done.13 = bf16[80,2048]{1,0:T(8,128)(2,1)S(1)} collective-permute-done((bf16[80,2048]{1,0:T(8,128)(2,1)S(1)}, bf16[80,2048]{1,0:T(8,128)(2,1)S(1)}, u32[]{:S(2)}, u32[]{:S(2)}) %collective-permute-start.13) | collective-permute-done | bytes 327712 | tf_op jit(solution)/shard_map/ppermute | solution.py:31
  92.3 2.1 %collective-permute-done.14 = bf16[80,2048]{1,0:T(8,128)(2,1)S(1)} collective-permute-done((bf16[80,2048]{1,0:T(8,128)(2,1)S(1)}, bf16[80,2048]{1,0:T(8,128)(2,1)S(1)}, u32[]{:S(2)}, u32[]{:S(2)}) %collective-permute-start.14) | collective-permute-done | bytes 327712 | tf_op jit(solution)/shard_map/ppermute | solution.py:31
  94.3 6.0 %collective-permute-done.15 = bf16[80,2048]{1,0:T(8,128)(2,1)S(1)} collective-permute-done((bf16[80,2048]{1,0:T(8,128)(2,1)S(1)}, bf16[80,2048]{1,0:T(8,128)(2,1)S(1)}, u32[]{:S(2)}, u32[]{:S(2)}) %collective-permute-start.15) | collective-permute-done | bytes 327712 | tf_op jit(solution)/shard_map/ppermute | solution.py:31
  100.3 2.2 %fusion.43 = (bf16[80,2048]{1,0:T(8,128)(2,1)S(1)}, f32[80,2048]{1,0:T(8,128)}) fusion(bf16[80,2048]{1,0:T(8,128)(2,1)S(1)} %collective-permute-done.15, bf16[80,2048]{1,0:T(8,128)(2,1)S(1)} %collective-permute-done.14, bf16[80,2048]{1,0:T(8,128)(2,1)S(1)} %collective-permute-done.13, bf16[320,2048]{1,0:T(8,128)(2,1)} %collective-permute-done.12, ...), kind=kLoop, calls=%fused_computation.104 | loop fusion | flops 1638400 | bytes 2621440 | tf_op jit(solution)/shard_map/convert_element_type | solution.py:338
  103.2 3.8 %collective-permute-start.17 = (bf16[20,2048]{1,0:T(8,128)(2,1)S(1)}, bf16[20,2048]{1,0:T(8,128)(2,1)S(1)}, u32[]{:S(2)}, u32[]{:S(2)}) collective-permute-start(bf16[20,2048]{1,0:T(8,128)(2,1)S(1)} %get-tuple-element.69), channel_id=1, source_target_pairs={{0,16},{1,17},{2,18},{3,19},{4,20},{5,21},{6,22},{7,23},{8,24},{9,... | collective-permute-start | bytes 245768 | tf_op jit(solution)/shard_map/ppermute | solution.py:39
  107.3 1.6 %shard_map.98 = (bf16[128,2560]{1,0:T(8,128)(2,1)}, bf16[128,2560]{1,0:T(8,128)(2,1)}, bf16[128,2560]{1,0:T(8,128)(2,1)}) custom-call(bf16[8,400,256]{2,1,0:T(8,128)(2,1)S(1)} %all-to-all-done.1.back_ref, bf16[64,128]{1,0:T(8,128)(2,1)S(1)} %fusion.7.selector_ref), custom_call_target="tpu_custom_call" | custom-call | flops 20000000000 | bytes 4000000 | tf_op jit(solution)/shard_map/pallas_call | solution.py:158
  108.9 0.9 slice_add_fusion
  109.8 2.2 %collective-permute-done.17 = bf16[20,2048]{1,0:T(8,128)(2,1)S(1)} collective-permute-done((bf16[20,2048]{1,0:T(8,128)(2,1)S(1)}, bf16[20,2048]{1,0:T(8,128)(2,1)S(1)}, u32[]{:S(2)}, u32[]{:S(2)}) %collective-permute-start.17) | collective-permute-done | bytes 81952 | tf_op jit(solution)/shard_map/ppermute | solution.py:39
  112.0 1.8 %collective-permute-done.18 = bf16[20,2048]{1,0:T(8,128)(2,1)S(1)} collective-permute-done((bf16[20,2048]{1,0:T(8,128)(2,1)S(1)}, bf16[20,2048]{1,0:T(8,128)(2,1)S(1)}, u32[]{:S(2)}, u32[]{:S(2)}) %collective-permute-start.18) | collective-permute-done | bytes 81952 | tf_op jit(solution)/shard_map/ppermute | solution.py:39
  (60 shorter events, 11.5 us)
Async XLA Ops:
  0.6 1.1 copy-start
  0.6 1.4 %copy-start.2 = (bf16[1,128,2560]{2,1,0:T(8,128)(2,1)S(1)}, bf16[1,128,2560]{2,1,0:T(8,128)(2,1)}, u32[]{:S(2)}) copy-start(bf16[1,128,2560]{2,1,0:T(8,128)(2,1)} %param.7) | copy-start | bytes 1966084
  2.0 1.1 copy-start.3
  3.3 1.3 %copy-start.1 = (bf16[8,320,384]{2,1,0:T(8,128)(2,1)}, bf16[8,320,384]{2,1,0:T(8,128)(2,1)S(1)}, u32[]{:S(2)}) copy-start(bf16[8,320,384]{2,1,0:T(8,128)(2,1)S(1)} %shard_map.93) | copy-start | bytes 5898244
  4.6 8.1 %copy-start.8 = (bf16[1,64,4096]{2,1,0:T(8,128)(2,1)S(1)}, bf16[1,64,4096]{2,1,0:T(8,128)(2,1)}, u32[]{:S(2)}) copy-start(bf16[1,64,4096]{2,1,0:T(8,128)(2,1)} %param.10) | copy-start | bytes 1572868
  4.6 50.5 %all-to-all-start = ((bf16[8,320,384]{2,1,0:T(8,128)(2,1)}), bf16[8,320,384]{2,1,0:T(8,128)(2,1)S(1)}, u32[]{:S(2)}, u32[]{:S(2)}) async-start(bf16[8,320,384]{2,1,0:T(8,128)(2,1)} %copy-done.1), calls=%async_computation | async-start | bytes 3932160 | tf_op jit(solution)/shard_map/all_to_all | solution.py:27
  23.9 15.4 %collective-permute-start.3 = (bf16[64,640]{1,0:T(8,128)(2,1)S(1)}, bf16[64,640]{1,0:T(8,128)(2,1)S(1)}, u32[]{:S(2)}, u32[]{:S(2)}) collective-permute-start(bf16[64,640]{1,0:T(8,128)(2,1)S(1)} %get-tuple-element.34), channel_id=1, source_target_pairs={{0,96},{16,112},{32,0},{48,16},{64,32},{80,48},{96,64},{112,80},{1... | collective-permute-start | bytes 245768 | tf_op jit(solution)/shard_map/ppermute | solution.py:43
  27.2 14.8 %collective-permute-start.4 = (bf16[64,640]{1,0:T(8,128)(2,1)S(1)}, bf16[64,640]{1,0:T(8,128)(2,1)S(1)}, u32[]{:S(2)}, u32[]{:S(2)}) collective-permute-start(bf16[64,640]{1,0:T(8,128)(2,1)S(1)} %get-tuple-element.35), channel_id=1, source_target_pairs={{0,64},{16,80},{32,96},{48,112},{64,0},{80,16},{96,32},{112,48},{1... | collective-permute-start | bytes 245768 | tf_op jit(solution)/shard_map/ppermute | solution.py:43
  28.1 15.1 %collective-permute-start.5 = (bf16[64,640]{1,0:T(8,128)(2,1)S(1)}, bf16[64,640]{1,0:T(8,128)(2,1)S(1)}, u32[]{:S(2)}, u32[]{:S(2)}) collective-permute-start(bf16[64,640]{1,0:T(8,128)(2,1)S(1)} %get-tuple-element.36), channel_id=1, source_target_pairs={{0,32},{16,48},{32,64},{48,80},{64,96},{80,112},{96,0},{112,16},{1... | collective-permute-start | bytes 245768 | tf_op jit(solution)/shard_map/ppermute | solution.py:43
  30.7 13.3 %collective-permute-start.6 = (bf16[64,2048]{1,0:T(8,128)(2,1)}, bf16[64,2048]{1,0:T(8,128)(2,1)}, u32[]{:S(2)}, u32[]{:S(2)}) collective-permute-start(bf16[64,2048]{1,0:T(8,128)(2,1)} %get-tuple-element.65), channel_id=1, source_target_pairs={{0,16},{16,0},{32,48},{48,32},{64,80},{80,64},{96,112},{112,96},{1... | collective-permute-start | bytes 786440 | tf_op jit(solution)/shard_map/ppermute | solution.py:47
  33.7 13.6 %collective-permute-start = (bf16[64,2048]{1,0:T(8,128)(2,1)S(1)}, bf16[64,2048]{1,0:T(8,128)(2,1)}, u32[]{:S(2)}, u32[]{:S(2)}) collective-permute-start(bf16[64,2048]{1,0:T(8,128)(2,1)S(1)} %get-tuple-element.46.refs_0_), channel_id=1, source_target_pairs={{0,96},{16,112},{32,0},{48,16},{64,32},{80,48},{96,64},{112,80},{1... | collective-permute-start | bytes 786440 | tf_op jit(solution)/shard_map/ppermute | solution.py:43
  39.4 10.5 %collective-permute-start.1 = (bf16[64,2048]{1,0:T(8,128)(2,1)S(1)}, bf16[64,2048]{1,0:T(8,128)(2,1)S(1)}, u32[]{:S(2)}, u32[]{:S(2)}) collective-permute-start(bf16[64,2048]{1,0:T(8,128)(2,1)S(1)} %get-tuple-element.46.refs_0_), channel_id=1, source_target_pairs={{0,64},{16,80},{32,96},{48,112},{64,0},{80,16},{96,32},{112,48},{1... | collective-permute-start | bytes 786440 | tf_op jit(solution)/shard_map/ppermute | solution.py:43
  42.0 12.4 %collective-permute-start.2 = (bf16[64,2048]{1,0:T(8,128)(2,1)S(1)}, bf16[64,2048]{1,0:T(8,128)(2,1)S(1)}, u32[]{:S(2)}, u32[]{:S(2)}) collective-permute-start(bf16[64,2048]{1,0:T(8,128)(2,1)S(1)} %get-tuple-element.46.refs_0_), channel_id=1, source_target_pairs={{0,32},{16,48},{32,64},{48,80},{64,96},{80,112},{96,0},{112,16},{1... | collective-permute-start | bytes 786440 | tf_op jit(solution)/shard_map/ppermute | solution.py:43
  44.8 16.9 %collective-permute-start.7 = (bf16[256,384]{1,0:T(8,128)(2,1)}, bf16[256,384]{1,0:T(8,128)(2,1)S(1)}, u32[]{:S(2)}, u32[]{:S(2)}) collective-permute-start(bf16[256,384]{1,0:T(8,128)(2,1)} %pad_maximum_fusion.1), channel_id=1, source_target_pairs={{0,16},{16,0},{32,48},{48,32},{64,80},{80,64},{96,112},{112,96},{1... | collective-permute-start | bytes 589832 | tf_op jit(solution)/shard_map/ppermute | solution.py:47
  46.7 21.8 %collective-permute-start.10 = (bf16[64,2048]{1,0:T(8,128)(2,1)}, bf16[64,2048]{1,0:T(8,128)(2,1)}, u32[]{:S(2)}, u32[]{:S(2)}) collective-permute-start(bf16[64,2048]{1,0:T(8,128)(2,1)} %collective-permute-done.6.refs_4_), channel_id=1, source_target_pairs={{0,32},{16,48},{32,64},{48,80},{64,96},{80,112},{96,0},{112,16},{1... | collective-permute-start | bytes 786440 | tf_op jit(solution)/shard_map/ppermute | solution.py:43
  47.2 21.2 %collective-permute-start.8 = (bf16[64,2048]{1,0:T(8,128)(2,1)}, bf16[64,2048]{1,0:T(8,128)(2,1)}, u32[]{:S(2)}, u32[]{:S(2)}) collective-permute-start(bf16[64,2048]{1,0:T(8,128)(2,1)} %collective-permute-done.6.refs_4_), channel_id=1, source_target_pairs={{0,96},{16,112},{32,0},{48,16},{64,32},{80,48},{96,64},{112,80},{1... | collective-permute-start | bytes 786440 | tf_op jit(solution)/shard_map/ppermute | solution.py:43
  49.9 0.7 copy-start.4
  50.6 17.9 %collective-permute-start.9 = (bf16[64,2048]{1,0:T(8,128)(2,1)}, bf16[64,2048]{1,0:T(8,128)(2,1)}, u32[]{:S(2)}, u32[]{:S(2)}) collective-permute-start(bf16[64,2048]{1,0:T(8,128)(2,1)} %collective-permute-done.6.refs_4_), channel_id=1, source_target_pairs={{0,64},{16,80},{32,96},{48,112},{64,0},{80,16},{96,32},{112,48},{1... | collective-permute-start | bytes 786440 | tf_op jit(solution)/shard_map/ppermute | solution.py:43
  54.4 0.7 copy-start.6
  59.4 9.1 %collective-permute-start.11 = (bf16[256,512]{1,0:T(8,128)(2,1)S(1)}, bf16[256,512]{1,0:T(8,128)(2,1)S(1)}, u32[]{:S(2)}, u32[]{:S(2)}) collective-permute-start(bf16[256,512]{1,0:T(8,128)(2,1)S(1)} %slice.51), channel_id=1, source_target_pairs={{0,16},{16,0},{32,48},{48,32},{64,80},{80,64},{96,112},{112,96},{1... | collective-permute-start | bytes 786440 | tf_op jit(solution)/shard_map/ppermute | solution.py:47
  61.7 6.2 %copy-start.9 = (pred[640,640]{1,0:T(32,128)(4,1)S(1)}, pred[640,640]{1,0:T(32,128)(4,1)}, u32[]{:S(2)}) copy-start(pred[640,640]{1,0:T(32,128)(4,1)} %iota_compare_fusion) | copy-start | bytes 1228804
  68.4 1.0 copy-start.5
  68.4 1.0 copy-start.7
  73.8 6.0 %collective-permute-start.12 = (bf16[320,2048]{1,0:T(8,128)(2,1)}, bf16[320,2048]{1,0:T(8,128)(2,1)}, u32[]{:S(2)}, u32[]{:S(2)}) collective-permute-start(bf16[320,2048]{1,0:T(8,128)(2,1)} %get-tuple-element.55), channel_id=1, source_target_pairs={{0,1},{1,0},{2,3},{3,2},{4,5},{5,4},{6,7},{7,6},{8,9},{9,8},{10,11... | collective-permute-start | bytes 3932168 | tf_op jit(solution)/shard_map/ppermute | solution.py:51
  73.8 33.5 %all-to-all-start.1 = ((bf16[8,400,256]{2,1,0:T(8,128)(2,1)}), bf16[8,400,256]{2,1,0:T(8,128)(2,1)S(1)}, u32[]{:S(2)}, u32[]{:S(2)}) async-start(bf16[8,400,256]{2,1,0:T(8,128)(2,1)} %shard_map.96), calls=%async_computation.1 | async-start | bytes 3276800 | tf_op jit(solution)/shard_map/all_to_all | solution.py:27
  81.6 10.6 %collective-permute-start.13 = (bf16[80,2048]{1,0:T(8,128)(2,1)S(1)}, bf16[80,2048]{1,0:T(8,128)(2,1)S(1)}, u32[]{:S(2)}, u32[]{:S(2)}) collective-permute-start(bf16[80,2048]{1,0:T(8,128)(2,1)S(1)} %get-tuple-element.62), channel_id=1, source_target_pairs={{0,4},{1,5},{2,6},{3,7},{4,8},{5,9},{6,10},{7,11},{8,12},{9,13},{1... | collective-permute-start | bytes 983048 | tf_op jit(solution)/shard_map/ppermute | solution.py:31
  82.2 12.1 %collective-permute-start.14 = (bf16[80,2048]{1,0:T(8,128)(2,1)S(1)}, bf16[80,2048]{1,0:T(8,128)(2,1)S(1)}, u32[]{:S(2)}, u32[]{:S(2)}) collective-permute-start(bf16[80,2048]{1,0:T(8,128)(2,1)S(1)} %get-tuple-element.64), channel_id=1, source_target_pairs={{0,8},{1,9},{2,10},{3,11},{4,12},{5,13},{6,14},{7,15},{8,0},{9,1},... | collective-permute-start | bytes 983048 | tf_op jit(solution)/shard_map/ppermute | solution.py:31
  84.6 15.7 %collective-permute-start.15 = (bf16[80,2048]{1,0:T(8,128)(2,1)S(1)}, bf16[80,2048]{1,0:T(8,128)(2,1)S(1)}, u32[]{:S(2)}, u32[]{:S(2)}) collective-permute-start(bf16[80,2048]{1,0:T(8,128)(2,1)S(1)} %get-tuple-element.63), channel_id=1, source_target_pairs={{0,12},{1,13},{2,14},{3,15},{4,0},{5,1},{6,2},{7,3},{8,4},{9,5},{1... | collective-permute-start | bytes 983048 | tf_op jit(solution)/shard_map/ppermute | solution.py:31
  102.5 6.4 %collective-permute-start.16 = (bf16[20,2048]{1,0:T(8,128)(2,1)S(1)}, bf16[20,2048]{1,0:T(8,128)(2,1)S(1)}, u32[]{:S(2)}, u32[]{:S(2)}) collective-permute-start(bf16[20,2048]{1,0:T(8,128)(2,1)S(1)} %get-tuple-element.67), channel_id=1, source_target_pairs={{0,2},{1,3},{2,0},{3,1},{4,6},{5,7},{6,4},{7,5},{8,10},{9,11},{10,... | collective-permute-start | bytes 245768 | tf_op jit(solution)/shard_map/ppermute | solution.py:39
  103.2 8.7 %collective-permute-start.17 = (bf16[20,2048]{1,0:T(8,128)(2,1)S(1)}, bf16[20,2048]{1,0:T(8,128)(2,1)S(1)}, u32[]{:S(2)}, u32[]{:S(2)}) collective-permute-start(bf16[20,2048]{1,0:T(8,128)(2,1)S(1)} %get-tuple-element.69), channel_id=1, source_target_pairs={{0,16},{1,17},{2,18},{3,19},{4,20},{5,21},{6,22},{7,23},{8,24},{9,... | collective-permute-start | bytes 245768 | tf_op jit(solution)/shard_map/ppermute | solution.py:39
  107.1 6.7 %collective-permute-start.18 = (bf16[20,2048]{1,0:T(8,128)(2,1)S(1)}, bf16[20,2048]{1,0:T(8,128)(2,1)S(1)}, u32[]{:S(2)}, u32[]{:S(2)}) collective-permute-start(bf16[20,2048]{1,0:T(8,128)(2,1)S(1)} %get-tuple-element.68), channel_id=1, source_target_pairs={{0,18},{1,19},{2,16},{3,17},{4,22},{5,23},{6,20},{7,21},{8,26},{9,... | collective-permute-start | bytes 245768 | tf_op jit(solution)/shard_map/ppermute | solution.py:39

commit v5 on v4

--- a/solution.py
+++ b/solution.py
@@ -291,24 +291,6 @@
     grads_out = pack_grads(ring * 640, masked_grad)
     own_grad = [grads_out[0]] + [move_z(grads_out[4 - dz], 4 - dz) for dz in (1, 2, 3)]
     own_all = jnp.concatenate(own_grad, axis=0)
-    own_all, cot_got = lax.optimization_barrier((own_all, cot_got))
-    got_grad = swap_y(
-        jnp.concatenate(
-            [lax.dynamic_slice_in_dim(own_all, (1 - y) * 384, 256, 1), own_all[:, 256:384]], axis=1
-        )
-    )
-    place = jnp.concatenate([jnp.stack([y, 3 * y, 3 * y + 1, 0 * y + 2]), columns]).astype(jnp.int32)
-    own_parts = [cot_kept] + [move_z(cot_kept, dz) for dz in (3, 2, 1)]
-    other_parts = [cot_got] + [move_z(cot_got, dz) for dz in (3, 2, 1)]
-    probs, att = forward(heads_in)
-    att_got = swap_y(att[:256])
-    place_back, own_parts = lax.optimization_barrier((place, own_parts))
-    outs = backward(place_back, heads_in, own_grad, got_grad, probs, att)
-
-    back = exchange(outs)
-    own_parts, other_parts, att_got, _ = lax.optimization_barrier(
-        (own_parts, other_parts, att_got, outs)
-    )
     r = jnp.arange(640, dtype=jnp.int32)
     rc, rx, rl, rh, rr = r // 320, (r // 80) % 4, (r // 40) % 2, (r // 20) % 2, r % 20
     wanted = (
@@ -322,6 +304,24 @@
     high_place = jnp.where(y == 0, wanted, wanted - 384)
     index = jnp.where(wanted < 256, low_place, jnp.where(wanted < 384, wanted, high_place))
     pick = (index[:, None] == r[None, :]).astype(BF)
+    own_all, cot_got, pick = lax.optimization_barrier((own_all, cot_got, pick))
+    got_grad = swap_y(
+        jnp.concatenate(
+            [lax.dynamic_slice_in_dim(own_all, (1 - y) * 384, 256, 1), own_all[:, 256:384]], axis=1
+        )
+    )
+    place = jnp.concatenate([jnp.stack([y, 3 * y, 3 * y + 1, 0 * y + 2]), columns]).astype(jnp.int32)
+    own_parts = [cot_kept] + [move_z(cot_kept, dz) for dz in (3, 2, 1)]
+    other_parts = [cot_got] + [move_z(cot_got, dz) for dz in (3, 2, 1)]
+    probs, att = forward(heads_in)
+    att_got = swap_y(att[:256])
+    place_back, own_parts = lax.optimization_barrier((place, own_parts))
+    outs = backward(place_back, heads_in, own_grad, got_grad, probs, att)
+
+    back = exchange(outs)
+    own_parts, other_parts, att_got, _ = lax.optimization_barrier(
+        (own_parts, other_parts, att_got, outs)
+    )
     att_rows = (dot(pick[:, :SLAB], att, 1, 0) + dot(pick[:, SLAB:], att_got, 1, 0)).astype(BF)
     att_rows = lax.dynamic_slice_in_dim(
         jnp.concatenate([att_rows, att_rows], axis=1), z * 2 * MSK, QUERIES, 1

time: 115 us -> 129 us (1.12)
  waiting for transfers between devices: 24.5 us -> 40.8 us
  starting transfers between devices: 45.3 us -> 41.4 us
    ppermute x3, waiting for transfers between devices: 0.84 us -> 12.3 us  [swap_y(): return lax.ppermute(a, 'blk', [(i, i ^ 1) for i in range(8)])]
    ppermute x9, waiting for transfers between devices: 4.11 us -> 9.6 us  [move_z(): return lax.ppermute(a, 'blk', [(i, (i + 2 * dz) % 8) for i in range(8)])]
    all_to_all x2, starting transfers between devices: 14.1 us -> 11.6 us  [exchange(): return lax.all_to_all(a, 'blk', 0, 0, tiled=True)]
    ppermute x9, starting transfers between devices: 17.3 us -> 15.3 us  [move_z(): return lax.ppermute(a, 'blk', [(i, (i + 2 * dz) % 8) for i in range(8)])]
    unnamed x20 -> x16, local copies, waits for them, and re-layouts: 4.5 us -> 4.91 us
  transfers between devices with their start and end apart: 21 -> 21, of which waited for: 8 -> 8; matrix products, arithmetic and copies ran while one was open for 17% -> 14% of each run, Pallas kernels for 11% -> 10%
where the time goes in v5:
time: 129 us; the launch traced here: 128 us
  starting transfers between devices  41.4 us (32%)
  waiting for transfers between devices  40.8 us (32%)
  Pallas kernels  17.3 us (13%)
  matrix products  12.7 us (10%)
  other arithmetic  7.78 us (6%)
  local copies, waits for them, and re-layouts  7.66 us (6%)
    ppermute x3, waiting for transfers between devices, move_x(): return lax.ppermute(a, 'dp', [(i, (i + 4 * dx) % 16) for i in range(16)])  15.6 us
    ppermute x9, starting transfers between devices, move_z(): return lax.ppermute(a, 'blk', [(i, (i + 2 * dz) % 8) for i in range(8)])  15.3 us
    dot_general x4, matrix products, dot(): lax.dot_general(a, b, (((ca,), (cb,)), ((), ())), preferred_element_type=...  12.7 us
    ppermute x3, waiting for transfers between devices, swap_y(): return lax.ppermute(a, 'blk', [(i, i ^ 1) for i in range(8)])  12.3 us
    all_to_all x2, starting transfers between devices, exchange(): return lax.all_to_all(a, 'blk', 0, 0, tiled=True)  11.6 us
    ppermute x9, waiting for transfers between devices, move_z(): return lax.ppermute(a, 'blk', [(i, (i + 2 * dz) % 8) for i in range(8)])  9.6 us
    ppermute x3, starting transfers between devices, swap_y(): return lax.ppermute(a, 'blk', [(i, i ^ 1) for i in range(8)])  6.73 us
    pallas_call x1, Pallas kernels, backward(): pl.pallas_call(backward_kernel, grid_spec=pltpu.PrefetchScalarGridSpec(nu...  6.2 us
  transfers between devices with their start and end apart: 21, of which 8 were waited for; matrix products, arithmetic and copies ran while one was open for 14% of the time, Pallas kernels for 10%

profile of v5, /device:TPU:6, one launch (start us, length us, event | category | flops | bytes accessed | tf_op | source)
XLA Modules:
  0.0 128.4 jit_solution(13742200213511407445)
XLA Ops:
  0.7 1.9 %dynamic-slice_bitcast_fusion = (bf16[64,2048]{1,0:T(8,128)(2,1)S(1)}, bf16[64,2048]{1,0:T(8,128)(2,1)}) fusion(bf16[1,64,4096]{2,1,0:T(8,128)(2,1)} %param.10, s32[]{:T(128)S(6)} %select_n.185, s32[]{:T(128)S(6)} %select_n.184), kind=kLoop, calls=%fused_computation.20 | loop fusion | bytes 1048584 | tf_op jit(solution)/shard_map/dynamic_slice | solution.py:283
  2.6 4.0 %collective-permute-start = (bf16[64,2048]{1,0:T(8,128)(2,1)}, bf16[64,2048]{1,0:T(8,128)(2,1)}, u32[]{:S(2)}, u32[]{:S(2)}) collective-permute-start(bf16[64,2048]{1,0:T(8,128)(2,1)} %get-tuple-element.48.refs_0_), channel_id=1, source_target_pairs={{0,96},{16,112},{32,0},{48,16},{64,32},{80,48},{96,64},{112,80},{1... | collective-permute-start | bytes 786440 | tf_op jit(solution)/shard_map/ppermute | solution.py:43
  7.9 1.3 %copy-done.1 = bf16[8,320,384]{2,1,0:T(8,128)(2,1)} copy-done((bf16[8,320,384]{2,1,0:T(8,128)(2,1)}, bf16[8,320,384]{2,1,0:T(8,128)(2,1)S(1)}, u32[]{:S(2)}) %copy-start.1) | copy-done | bytes 1966104
  9.2 7.6 %all-to-all-start = ((bf16[8,320,384]{2,1,0:T(8,128)(2,1)}), bf16[8,320,384]{2,1,0:T(8,128)(2,1)S(1)}, u32[]{:S(2)}, u32[]{:S(2)}) async-start(bf16[8,320,384]{2,1,0:T(8,128)(2,1)} %copy-done.1), calls=%async_computation | async-start | bytes 3932160 | tf_op jit(solution)/shard_map/all_to_all | solution.py:27
  16.8 10.6 %convolution_convert_fusion.grad_ref = bf16[64,2560]{1,0:T(8,128)(2,1)S(1)} fusion(bf16[2560,4096]{1,0:T(8,128)(2,1)} %param.11, bf16[1,64,4096]{2,1,0:T(8,128)(2,1)S(1)} %copy-done.6), kind=kOutput, calls=%fused_computation | convolution fusion | flops 1342341120 | bytes 21823488 | tf_op jit(solution)/shard_map/dot_general | solution.py:55
  28.0 3.3 %collective-permute-start.3 = (bf16[64,640]{1,0:T(8,128)(2,1)S(1)}, bf16[64,640]{1,0:T(8,128)(2,1)S(1)}, u32[]{:S(2)}, u32[]{:S(2)}) collective-permute-start(bf16[64,640]{1,0:T(8,128)(2,1)S(1)} %get-tuple-element.35), channel_id=1, source_target_pairs={{0,96},{16,112},{32,0},{48,16},{64,32},{80,48},{96,64},{112,80},{1... | collective-permute-start | bytes 245768 | tf_op jit(solution)/shard_map/ppermute | solution.py:43
  33.0 9.6 %collective-permute-done.3.refs_1_ = bf16[64,640]{1,0:T(8,128)(2,1)S(1)} collective-permute-done((bf16[64,640]{1,0:T(8,128)(2,1)S(1)}, bf16[64,640]{1,0:T(8,128)(2,1)S(1)}, u32[]{:S(2)}, u32[]{:S(2)}) %collective-permute-start.3) | collective-permute-done | bytes 81952 | tf_op jit(solution)/shard_map/ppermute | solution.py:43
  42.6 3.2 %collective-permute-start.6 = (bf16[64,2048]{1,0:T(8,128)(2,1)S(1)}, bf16[64,2048]{1,0:T(8,128)(2,1)}, u32[]{:S(2)}, u32[]{:S(2)}) collective-permute-start(bf16[64,2048]{1,0:T(8,128)(2,1)S(1)} %get-tuple-element.67), channel_id=1, source_target_pairs={{0,16},{16,0},{32,48},{48,32},{64,80},{80,64},{96,112},{112,96},{1... | collective-permute-start | bytes 786440 | tf_op jit(solution)/shard_map/ppermute | solution.py:47
  46.9 4.2 %collective-permute-done.6.refs_4_ = bf16[64,2048]{1,0:T(8,128)(2,1)} collective-permute-done((bf16[64,2048]{1,0:T(8,128)(2,1)S(1)}, bf16[64,2048]{1,0:T(8,128)(2,1)}, u32[]{:S(2)}, u32[]{:S(2)}) %collective-permute-start.6) | collective-permute-done | bytes 262176 | tf_op jit(solution)/shard_map/ppermute | solution.py:47
  51.1 3.1 %collective-permute-start.10 = (bf16[64,2048]{1,0:T(8,128)(2,1)}, bf16[64,2048]{1,0:T(8,128)(2,1)}, u32[]{:S(2)}, u32[]{:S(2)}) collective-permute-start(bf16[64,2048]{1,0:T(8,128)(2,1)} %collective-permute-done.6.refs_4_), channel_id=1, source_target_pairs={{0,32},{16,48},{32,64},{48,80},{64,96},{80,112},{96,0},{112,16},{1... | collective-permute-start | bytes 786440 | tf_op jit(solution)/shard_map/ppermute | solution.py:43
  54.3 1.6 %collective-permute-start.8 = (bf16[64,2048]{1,0:T(8,128)(2,1)}, bf16[64,2048]{1,0:T(8,128)(2,1)}, u32[]{:S(2)}, u32[]{:S(2)}) collective-permute-start(bf16[64,2048]{1,0:T(8,128)(2,1)} %collective-permute-done.6.refs_4_), channel_id=1, source_target_pairs={{0,96},{16,112},{32,0},{48,16},{64,32},{80,48},{96,64},{112,80},{1... | collective-permute-start | bytes 786440 | tf_op jit(solution)/shard_map/ppermute | solution.py:43
  55.9 4.3 %shard_map.95 = (bf16[3,1024,512]{2,1,0:T(8,128)(2,1)S(1)}, bf16[384,512]{1,0:T(8,128)(2,1)S(1)}) custom-call(bf16[8,320,384]{2,1,0:T(8,128)(2,1)S(1)} %all-to-all-done.in_ref), custom_call_target="tpu_custom_call" | custom-call | flops 1000000 | bytes 100000 | tf_op jit(solution)/shard_map/pallas_call | solution.py:238
  60.2 1.6 %copy-done.2 = bf16[3,1024,512]{2,1,0:T(8,128)(2,1)} copy-done((bf16[3,1024,512]{2,1,0:T(8,128)(2,1)}, bf16[3,1024,512]{2,1,0:T(8,128)(2,1)S(1)}, u32[]{:S(2)}) %copy-start.2) | copy-done | bytes 3145752
  62.5 1.5 %collective-permute-start.9 = (bf16[64,2048]{1,0:T(8,128)(2,1)}, bf16[64,2048]{1,0:T(8,128)(2,1)}, u32[]{:S(2)}, u32[]{:S(2)}) collective-permute-start(bf16[64,2048]{1,0:T(8,128)(2,1)} %collective-permute-done.6.refs_4_), channel_id=1, source_target_pairs={{0,64},{16,80},{32,96},{48,112},{64,0},{80,16},{96,32},{112,48},{1... | collective-permute-start | bytes 786440 | tf_op jit(solution)/shard_map/ppermute | solution.py:43
  64.0 1.6 %collective-permute-start.11 = (bf16[256,512]{1,0:T(8,128)(2,1)}, bf16[256,512]{1,0:T(8,128)(2,1)}, u32[]{:S(2)}, u32[]{:S(2)}) collective-permute-start(bf16[256,512]{1,0:T(8,128)(2,1)} %slice.51), channel_id=1, source_target_pairs={{0,16},{16,0},{32,48},{48,32},{64,80},{80,64},{96,112},{112,96},{1... | collective-permute-start | bytes 786440 | tf_op jit(solution)/shard_map/ppermute | solution.py:47
  66.3 2.0 %collective-permute-start.7 = (bf16[256,384]{1,0:T(8,128)(2,1)}, bf16[256,384]{1,0:T(8,128)(2,1)S(1)}, u32[]{:S(2)}, u32[]{:S(2)}) collective-permute-start(bf16[256,384]{1,0:T(8,128)(2,1)} %pad_maximum_fusion.1), channel_id=1, source_target_pairs={{0,16},{16,0},{32,48},{48,32},{64,80},{80,64},{96,112},{112,96},{1... | collective-permute-start | bytes 589832 | tf_op jit(solution)/shard_map/ppermute | solution.py:47
  68.3 8.1 %collective-permute-done.7.refs_4_ = bf16[256,384]{1,0:T(8,128)(2,1)S(1)} collective-permute-done((bf16[256,384]{1,0:T(8,128)(2,1)}, bf16[256,384]{1,0:T(8,128)(2,1)S(1)}, u32[]{:S(2)}, u32[]{:S(2)}) %collective-permute-start.7) | collective-permute-done | bytes 196640 | tf_op jit(solution)/shard_map/ppermute | solution.py:47
  76.5 1.9 %copy-done.3 = bf16[3,1024,512]{2,1,0:T(8,128)(2,1)S(1)} copy-done((bf16[3,1024,512]{2,1,0:T(8,128)(2,1)S(1)}, bf16[3,1024,512]{2,1,0:T(8,128)(2,1)}, u32[]{:S(2)}) %copy-start.3) | copy-done | bytes 3145752
  78.3 6.2 %shard_map.96 = bf16[8,400,256]{2,1,0:T(8,128)(2,1)} custom-call(s32[8]{0:T(128)S(1)} %concatenate.18.place_ref, bf16[8,320,384]{2,1,0:T(8,128)(2,1)S(1)} %all-to-all-done.in_ref, bf16[64,640]{1,0:T(8,128)(2,1)S(1)} %get-tuple-element.34.refs_0_, bf16[64,640]{1,0:T(8,128)(2,1)S(1)} %collective-permute-done.3.refs_1_, ...), custom_call_target="tpu_custom_call" | custom-call | flops 1000000 | bytes 100000 | tf_op jit(solution)/shard_map/pallas_call | solution.py:253
  84.6 1.3 fusion.6
  86.6 4.5 %shard_map.97 = (bf16[320,2048]{1,0:T(8,128)(2,1)}, bf16[320,2048]{1,0:T(8,128)(2,1)}) custom-call(s32[8]{0:T(128)S(1)} %concatenate.18.place_ref, bf16[640,512]{1,0:T(8,128)(2,1)S(1)} %fusion.2.att_ref, bf16[64,2048]{1,0:T(8,128)(2,1)} %get-tuple-element.48.refs_0_, bf16[64,2048]{1,0:T(8,128)(2,1)} %collective-permute-done.refs_1_, ...), custom_call_target="tpu_custom_call" | custom-call | flops 1400000000 | bytes 8000000 | tf_op jit(solution)/shard_map/pallas_call | solution.py:114
  91.1 4.1 %all-to-all-start.1 = ((bf16[8,400,256]{2,1,0:T(8,128)(2,1)}), bf16[8,400,256]{2,1,0:T(8,128)(2,1)S(1)}, u32[]{:S(2)}, u32[]{:S(2)}) async-start(bf16[8,400,256]{2,1,0:T(8,128)(2,1)} %shard_map.96), calls=%async_computation.1 | async-start | bytes 3276800 | tf_op jit(solution)/shard_map/all_to_all | solution.py:27
  95.2 1.8 %add_convert_fusion.2 = (bf16[80,2048]{1,0:T(8,128)(2,1)S(1)}, bf16[80,2048]{1,0:T(8,128)(2,1)S(1)}, bf16[80,2048]{1,0:T(8,128)(2,1)S(1)}) fusion(bf16[320,2048]{1,0:T(8,128)(2,1)} %collective-permute-done.12, bf16[320,2048]{1,0:T(8,128)(2,1)} %get-tuple-element.56), kind=kLoop, calls=%fused_computation.13 | loop fusion | flops 1966080 | bytes 2949120 | tf_op jit(solution)/shard_map/convert_element_type | solution.py:336
  97.6 2.4 %collective-permute-start.14 = (bf16[80,2048]{1,0:T(8,128)(2,1)S(1)}, bf16[80,2048]{1,0:T(8,128)(2,1)S(1)}, u32[]{:S(2)}, u32[]{:S(2)}) collective-permute-start(bf16[80,2048]{1,0:T(8,128)(2,1)S(1)} %get-tuple-element.66), channel_id=1, source_target_pairs={{0,8},{1,9},{2,10},{3,11},{4,12},{5,13},{6,14},{7,15},{8,0},{9,1},... | collective-permute-start | bytes 983048 | tf_op jit(solution)/shard_map/ppermute | solution.py:31
  100.1 7.6 %collective-permute-done.13 = bf16[80,2048]{1,0:T(8,128)(2,1)S(1)} collective-permute-done((bf16[80,2048]{1,0:T(8,128)(2,1)S(1)}, bf16[80,2048]{1,0:T(8,128)(2,1)S(1)}, u32[]{:S(2)}, u32[]{:S(2)}) %collective-permute-start.13) | collective-permute-done | bytes 327712 | tf_op jit(solution)/shard_map/ppermute | solution.py:31
  107.7 2.1 %collective-permute-done.14 = bf16[80,2048]{1,0:T(8,128)(2,1)S(1)} collective-permute-done((bf16[80,2048]{1,0:T(8,128)(2,1)S(1)}, bf16[80,2048]{1,0:T(8,128)(2,1)S(1)}, u32[]{:S(2)}, u32[]{:S(2)}) %collective-permute-start.14) | collective-permute-done | bytes 327712 | tf_op jit(solution)/shard_map/ppermute | solution.py:31
  109.7 5.9 %collective-permute-done.15 = bf16[80,2048]{1,0:T(8,128)(2,1)S(1)} collective-permute-done((bf16[80,2048]{1,0:T(8,128)(2,1)S(1)}, bf16[80,2048]{1,0:T(8,128)(2,1)S(1)}, u32[]{:S(2)}, u32[]{:S(2)}) %collective-permute-start.15) | collective-permute-done | bytes 327712 | tf_op jit(solution)/shard_map/ppermute | solution.py:31
  115.7 1.3 %fusion.44 = (bf16[80,2048]{1,0:T(8,128)(2,1)S(1)}, f32[80,2048]{1,0:T(8,128)S(1)}) fusion(bf16[80,2048]{1,0:T(8,128)(2,1)S(1)} %collective-permute-done.15, bf16[80,2048]{1,0:T(8,128)(2,1)S(1)} %collective-permute-done.14, bf16[80,2048]{1,0:T(8,128)(2,1)S(1)} %collective-permute-done.13, bf16[320,2048]{1,0:T(8,128)(2,1)} %collective-permute-done.12, ...), kind=kLoop, calls=%fused_computation.105 | loop fusion | flops 1638400 | bytes 2621440 | tf_op jit(solution)/shard_map/convert_element_type | solution.py:338
  117.2 3.7 %collective-permute-start.17 = (bf16[20,2048]{1,0:T(8,128)(2,1)S(1)}, bf16[20,2048]{1,0:T(8,128)(2,1)S(1)}, u32[]{:S(2)}, u32[]{:S(2)}) collective-permute-start(bf16[20,2048]{1,0:T(8,128)(2,1)S(1)} %get-tuple-element.71), channel_id=1, source_target_pairs={{0,16},{1,17},{2,18},{3,19},{4,20},{5,21},{6,22},{7,23},{8,24},{9,... | collective-permute-start | bytes 245768 | tf_op jit(solution)/shard_map/ppermute | solution.py:39
  121.8 1.6 %shard_map.98 = (bf16[128,2560]{1,0:T(8,128)(2,1)}, bf16[128,2560]{1,0:T(8,128)(2,1)}, bf16[128,2560]{1,0:T(8,128)(2,1)}) custom-call(bf16[8,400,256]{2,1,0:T(8,128)(2,1)S(1)} %all-to-all-done.1.back_ref, bf16[64,128]{1,0:T(8,128)(2,1)S(1)} %fusion.8.selector_ref), custom_call_target="tpu_custom_call" | custom-call | flops 20000000000 | bytes 4000000 | tf_op jit(solution)/shard_map/pallas_call | solution.py:158
  124.4 1.5 %collective-permute-done.17 = bf16[20,2048]{1,0:T(8,128)(2,1)S(1)} collective-permute-done((bf16[20,2048]{1,0:T(8,128)(2,1)S(1)}, bf16[20,2048]{1,0:T(8,128)(2,1)S(1)}, u32[]{:S(2)}, u32[]{:S(2)}) %collective-permute-start.17) | collective-permute-done | bytes 81952 | tf_op jit(solution)/shard_map/ppermute | solution.py:39
  125.8 1.8 %collective-permute-done.18 = bf16[20,2048]{1,0:T(8,128)(2,1)S(1)} collective-permute-done((bf16[20,2048]{1,0:T(8,128)(2,1)S(1)}, bf16[20,2048]{1,0:T(8,128)(2,1)S(1)}, u32[]{:S(2)}, u32[]{:S(2)}) %collective-permute-start.18) | collective-permute-done | bytes 81952 | tf_op jit(solution)/shard_map/ppermute | solution.py:39
  (56 shorter events, 10.5 us)
Async XLA Ops:
  0.6 6.7 %copy-start = (bf16[1,128,2560]{2,1,0:T(8,128)(2,1)S(1)}, bf16[1,128,2560]{2,1,0:T(8,128)(2,1)}, u32[]{:S(2)}) copy-start(bf16[1,128,2560]{2,1,0:T(8,128)(2,1)} %param.6) | copy-start | bytes 1966084
  0.6 7.0 %copy-start.4 = (bf16[1,128,2560]{2,1,0:T(8,128)(2,1)S(1)}, bf16[1,128,2560]{2,1,0:T(8,128)(2,1)}, u32[]{:S(2)}) copy-start(bf16[1,128,2560]{2,1,0:T(8,128)(2,1)} %param.7) | copy-start | bytes 1966084
  2.6 59.9 %collective-permute-start = (bf16[64,2048]{1,0:T(8,128)(2,1)}, bf16[64,2048]{1,0:T(8,128)(2,1)}, u32[]{:S(2)}, u32[]{:S(2)}) collective-permute-start(bf16[64,2048]{1,0:T(8,128)(2,1)} %get-tuple-element.48.refs_0_), channel_id=1, source_target_pairs={{0,96},{16,112},{32,0},{48,16},{64,32},{80,48},{96,64},{112,80},{1... | collective-permute-start | bytes 786440 | tf_op jit(solution)/shard_map/ppermute | solution.py:43
  6.6 57.4 %collective-permute-start.1 = (bf16[64,2048]{1,0:T(8,128)(2,1)}, bf16[64,2048]{1,0:T(8,128)(2,1)}, u32[]{:S(2)}, u32[]{:S(2)}) collective-permute-start(bf16[64,2048]{1,0:T(8,128)(2,1)} %get-tuple-element.48.refs_0_), channel_id=1, source_target_pairs={{0,64},{16,80},{32,96},{48,112},{64,0},{80,16},{96,32},{112,48},{1... | collective-permute-start | bytes 786440 | tf_op jit(solution)/shard_map/ppermute | solution.py:43
  6.6 1.1 copy-start.5
  7.9 1.3 %copy-start.1 = (bf16[8,320,384]{2,1,0:T(8,128)(2,1)}, bf16[8,320,384]{2,1,0:T(8,128)(2,1)S(1)}, u32[]{:S(2)}) copy-start(bf16[8,320,384]{2,1,0:T(8,128)(2,1)S(1)} %shard_map.93) | copy-start | bytes 5898244
  9.2 7.6 %copy-start.6 = (bf16[1,64,4096]{2,1,0:T(8,128)(2,1)S(1)}, bf16[1,64,4096]{2,1,0:T(8,128)(2,1)}, u32[]{:S(2)}) copy-start(bf16[1,64,4096]{2,1,0:T(8,128)(2,1)} %param.10) | copy-start | bytes 1572868
  9.2 46.7 %all-to-all-start = ((bf16[8,320,384]{2,1,0:T(8,128)(2,1)}), bf16[8,320,384]{2,1,0:T(8,128)(2,1)S(1)}, u32[]{:S(2)}, u32[]{:S(2)}) async-start(bf16[8,320,384]{2,1,0:T(8,128)(2,1)} %copy-done.1), calls=%async_computation | async-start | bytes 3932160 | tf_op jit(solution)/shard_map/all_to_all | solution.py:27
  28.0 14.6 %collective-permute-start.3 = (bf16[64,640]{1,0:T(8,128)(2,1)S(1)}, bf16[64,640]{1,0:T(8,128)(2,1)S(1)}, u32[]{:S(2)}, u32[]{:S(2)}) collective-permute-start(bf16[64,640]{1,0:T(8,128)(2,1)S(1)} %get-tuple-element.35), channel_id=1, source_target_pairs={{0,96},{16,112},{32,0},{48,16},{64,32},{80,48},{96,64},{112,80},{1... | collective-permute-start | bytes 245768 | tf_op jit(solution)/shard_map/ppermute | solution.py:43
  31.3 15.6 %collective-permute-start.4 = (bf16[64,640]{1,0:T(8,128)(2,1)S(1)}, bf16[64,640]{1,0:T(8,128)(2,1)S(1)}, u32[]{:S(2)}, u32[]{:S(2)}) collective-permute-start(bf16[64,640]{1,0:T(8,128)(2,1)S(1)} %get-tuple-element.36), channel_id=1, source_target_pairs={{0,64},{16,80},{32,96},{48,112},{64,0},{80,16},{96,32},{112,48},{1... | collective-permute-start | bytes 245768 | tf_op jit(solution)/shard_map/ppermute | solution.py:43
  32.1 14.8 %collective-permute-start.5 = (bf16[64,640]{1,0:T(8,128)(2,1)S(1)}, bf16[64,640]{1,0:T(8,128)(2,1)S(1)}, u32[]{:S(2)}, u32[]{:S(2)}) collective-permute-start(bf16[64,640]{1,0:T(8,128)(2,1)S(1)} %get-tuple-element.37), channel_id=1, source_target_pairs={{0,32},{16,48},{32,64},{48,80},{64,96},{80,112},{96,0},{112,16},{1... | collective-permute-start | bytes 245768 | tf_op jit(solution)/shard_map/ppermute | solution.py:43
  42.6 8.5 %collective-permute-start.6 = (bf16[64,2048]{1,0:T(8,128)(2,1)S(1)}, bf16[64,2048]{1,0:T(8,128)(2,1)}, u32[]{:S(2)}, u32[]{:S(2)}) collective-permute-start(bf16[64,2048]{1,0:T(8,128)(2,1)S(1)} %get-tuple-element.67), channel_id=1, source_target_pairs={{0,16},{16,0},{32,48},{48,32},{64,80},{80,64},{96,112},{112,96},{1... | collective-permute-start | bytes 786440 | tf_op jit(solution)/shard_map/ppermute | solution.py:47
  46.9 19.4 %collective-permute-start.2 = (bf16[64,2048]{1,0:T(8,128)(2,1)}, bf16[64,2048]{1,0:T(8,128)(2,1)}, u32[]{:S(2)}, u32[]{:S(2)}) collective-permute-start(bf16[64,2048]{1,0:T(8,128)(2,1)} %get-tuple-element.48.refs_0_), channel_id=1, source_target_pairs={{0,32},{16,48},{32,64},{48,80},{64,96},{80,112},{96,0},{112,16},{1... | collective-permute-start | bytes 786440 | tf_op jit(solution)/shard_map/ppermute | solution.py:43
  51.1 33.4 %collective-permute-start.10 = (bf16[64,2048]{1,0:T(8,128)(2,1)}, bf16[64,2048]{1,0:T(8,128)(2,1)}, u32[]{:S(2)}, u32[]{:S(2)}) collective-permute-start(bf16[64,2048]{1,0:T(8,128)(2,1)} %collective-permute-done.6.refs_4_), channel_id=1, source_target_pairs={{0,32},{16,48},{32,64},{48,80},{64,96},{80,112},{96,0},{112,16},{1... | collective-permute-start | bytes 786440 | tf_op jit(solution)/shard_map/ppermute | solution.py:43
  54.3 30.3 %collective-permute-start.8 = (bf16[64,2048]{1,0:T(8,128)(2,1)}, bf16[64,2048]{1,0:T(8,128)(2,1)}, u32[]{:S(2)}, u32[]{:S(2)}) collective-permute-start(bf16[64,2048]{1,0:T(8,128)(2,1)} %collective-permute-done.6.refs_4_), channel_id=1, source_target_pairs={{0,96},{16,112},{32,0},{48,16},{64,32},{80,48},{96,64},{112,80},{1... | collective-permute-start | bytes 786440 | tf_op jit(solution)/shard_map/ppermute | solution.py:43
  60.1 1.6 %copy-start.2 = (bf16[3,1024,512]{2,1,0:T(8,128)(2,1)}, bf16[3,1024,512]{2,1,0:T(8,128)(2,1)S(1)}, u32[]{:S(2)}) copy-start(bf16[3,1024,512]{2,1,0:T(8,128)(2,1)S(1)} %get-tuple-element.39.refs_5_) | copy-start | bytes 9437188
  62.5 22.1 %collective-permute-start.9 = (bf16[64,2048]{1,0:T(8,128)(2,1)}, bf16[64,2048]{1,0:T(8,128)(2,1)}, u32[]{:S(2)}, u32[]{:S(2)}) collective-permute-start(bf16[64,2048]{1,0:T(8,128)(2,1)} %collective-permute-done.6.refs_4_), channel_id=1, source_target_pairs={{0,64},{16,80},{32,96},{48,112},{64,0},{80,16},{96,32},{112,48},{1... | collective-permute-start | bytes 786440 | tf_op jit(solution)/shard_map/ppermute | solution.py:43
  64.0 20.6 %collective-permute-start.11 = (bf16[256,512]{1,0:T(8,128)(2,1)}, bf16[256,512]{1,0:T(8,128)(2,1)}, u32[]{:S(2)}, u32[]{:S(2)}) collective-permute-start(bf16[256,512]{1,0:T(8,128)(2,1)} %slice.51), channel_id=1, source_target_pairs={{0,16},{16,0},{32,48},{48,32},{64,80},{80,64},{96,112},{112,96},{1... | collective-permute-start | bytes 786440 | tf_op jit(solution)/shard_map/ppermute | solution.py:47
  66.3 10.2 %collective-permute-start.7 = (bf16[256,384]{1,0:T(8,128)(2,1)}, bf16[256,384]{1,0:T(8,128)(2,1)S(1)}, u32[]{:S(2)}, u32[]{:S(2)}) collective-permute-start(bf16[256,384]{1,0:T(8,128)(2,1)} %pad_maximum_fusion.1), channel_id=1, source_target_pairs={{0,16},{16,0},{32,48},{48,32},{64,80},{80,64},{96,112},{112,96},{1... | collective-permute-start | bytes 589832 | tf_op jit(solution)/shard_map/ppermute | solution.py:47
  76.5 1.9 %copy-start.3 = (bf16[3,1024,512]{2,1,0:T(8,128)(2,1)S(1)}, bf16[3,1024,512]{2,1,0:T(8,128)(2,1)}, u32[]{:S(2)}) copy-start(bf16[3,1024,512]{2,1,0:T(8,128)(2,1)} %copy-done.2) | copy-start | bytes 9437188
  78.3 6.2 %copy-start.7 = (bf16[640,640]{1,0:T(8,128)(2,1)S(1)}, bf16[640,640]{1,0:T(8,128)(2,1)}, u32[]{:S(2)}) copy-start(bf16[640,640]{1,0:T(8,128)(2,1)} %fusion) | copy-start | bytes 2457604
  91.1 4.1 %collective-permute-start.12 = (bf16[320,2048]{1,0:T(8,128)(2,1)}, bf16[320,2048]{1,0:T(8,128)(2,1)}, u32[]{:S(2)}, u32[]{:S(2)}) collective-permute-start(bf16[320,2048]{1,0:T(8,128)(2,1)} %get-tuple-element.57), channel_id=1, source_target_pairs={{0,1},{1,0},{2,3},{3,2},{4,5},{5,4},{6,7},{7,6},{8,9},{9,8},{10,11... | collective-permute-start | bytes 3932168 | tf_op jit(solution)/shard_map/ppermute | solution.py:51
  91.1 30.7 %all-to-all-start.1 = ((bf16[8,400,256]{2,1,0:T(8,128)(2,1)}), bf16[8,400,256]{2,1,0:T(8,128)(2,1)S(1)}, u32[]{:S(2)}, u32[]{:S(2)}) async-start(bf16[8,400,256]{2,1,0:T(8,128)(2,1)} %shard_map.96), calls=%async_computation.1 | async-start | bytes 3276800 | tf_op jit(solution)/shard_map/all_to_all | solution.py:27
  97.1 10.6 %collective-permute-start.13 = (bf16[80,2048]{1,0:T(8,128)(2,1)S(1)}, bf16[80,2048]{1,0:T(8,128)(2,1)S(1)}, u32[]{:S(2)}, u32[]{:S(2)}) collective-permute-start(bf16[80,2048]{1,0:T(8,128)(2,1)S(1)} %get-tuple-element.64), channel_id=1, source_target_pairs={{0,4},{1,5},{2,6},{3,7},{4,8},{5,9},{6,10},{7,11},{8,12},{9,13},{1... | collective-permute-start | bytes 983048 | tf_op jit(solution)/shard_map/ppermute | solution.py:31
  97.6 12.1 %collective-permute-start.14 = (bf16[80,2048]{1,0:T(8,128)(2,1)S(1)}, bf16[80,2048]{1,0:T(8,128)(2,1)S(1)}, u32[]{:S(2)}, u32[]{:S(2)}) collective-permute-start(bf16[80,2048]{1,0:T(8,128)(2,1)S(1)} %get-tuple-element.66), channel_id=1, source_target_pairs={{0,8},{1,9},{2,10},{3,11},{4,12},{5,13},{6,14},{7,15},{8,0},{9,1},... | collective-permute-start | bytes 983048 | tf_op jit(solution)/shard_map/ppermute | solution.py:31
  100.0 15.7 %collective-permute-start.15 = (bf16[80,2048]{1,0:T(8,128)(2,1)S(1)}, bf16[80,2048]{1,0:T(8,128)(2,1)S(1)}, u32[]{:S(2)}, u32[]{:S(2)}) collective-permute-start(bf16[80,2048]{1,0:T(8,128)(2,1)S(1)} %get-tuple-element.65), channel_id=1, source_target_pairs={{0,12},{1,13},{2,14},{3,15},{4,0},{5,1},{6,2},{7,3},{8,4},{9,5},{1... | collective-permute-start | bytes 983048 | tf_op jit(solution)/shard_map/ppermute | solution.py:31
  117.1 6.4 %collective-permute-start.16 = (bf16[20,2048]{1,0:T(8,128)(2,1)S(1)}, bf16[20,2048]{1,0:T(8,128)(2,1)}, u32[]{:S(2)}, u32[]{:S(2)}) collective-permute-start(bf16[20,2048]{1,0:T(8,128)(2,1)S(1)} %get-tuple-element.69), channel_id=1, source_target_pairs={{0,2},{1,3},{2,0},{3,1},{4,6},{5,7},{6,4},{7,5},{8,10},{9,11},{10,... | collective-permute-start | bytes 245768 | tf_op jit(solution)/shard_map/ppermute | solution.py:39
  117.2 8.6 %collective-permute-start.17 = (bf16[20,2048]{1,0:T(8,128)(2,1)S(1)}, bf16[20,2048]{1,0:T(8,128)(2,1)S(1)}, u32[]{:S(2)}, u32[]{:S(2)}) collective-permute-start(bf16[20,2048]{1,0:T(8,128)(2,1)S(1)} %get-tuple-element.71), channel_id=1, source_target_pairs={{0,16},{1,17},{2,18},{3,19},{4,20},{5,21},{6,22},{7,23},{8,24},{9,... | collective-permute-start | bytes 245768 | tf_op jit(solution)/shard_map/ppermute | solution.py:39
  120.9 6.7 %collective-permute-start.18 = (bf16[20,2048]{1,0:T(8,128)(2,1)S(1)}, bf16[20,2048]{1,0:T(8,128)(2,1)S(1)}, u32[]{:S(2)}, u32[]{:S(2)}) collective-permute-start(bf16[20,2048]{1,0:T(8,128)(2,1)S(1)} %get-tuple-element.70), channel_id=1, source_target_pairs={{0,18},{1,19},{2,16},{3,17},{4,22},{5,23},{6,20},{7,21},{8,26},{9,... | collective-permute-start | bytes 245768 | tf_op jit(solution)/shard_map/ppermute | solution.py:39
